TPU v7x, 512 devices: a whole 4x4x16 slice. The times are simulated.
512 devices in a mesh: lat: 8 (over z_lo), lon: 64 (over y, x, z_hi, core).
Axes of the slice: x: 4, y: 4, z: 16 (z_hi: 2, z_lo: 8; z = z_hi * 8 + z_lo), core: 2. Of those that a mesh axis runs over, the one named last changes fastest.
Arguments:
- tokens: bfloat16 [96, 768, 512], P('lat', 'lon'), may hold values from -50 to 50
- query_key_value_weight: bfloat16 [512, 1536], replicated, may hold values from -0.25 to 0.25
- output_weight: bfloat16 [512, 512], replicated, may hold values from -0.25 to 0.25
- adapter_down_map: bfloat16 [2, 8, 512], replicated, may hold values from -0.25 to 0.25
- adapter_up_map: bfloat16 [2, 8, 512], replicated, may hold values from -2 to 2
- relative_position_bias: float32 [16, 72, 72], replicated, may hold values from -4 to 320
- readout: bfloat16 [512], replicated, may hold values from -0.25 to 0.25
- observation_index: int32 [8, 64, 64, 4, 128], P('lat', 'lon'), may hold values from 0 to 143
- observation_weight: float32 [8, 64, 64, 4, 128], P('lat', 'lon'), may hold values from 0.05 to 1
- observation_value: float32 [8, 64, 64, 128], P('lat', 'lon'), may hold values from -6 to 6
- observation_count: int32 [8, 64, 64], P('lat', 'lon'), may hold values from 0 to 128, as said below
Outputs:
- block_out: bfloat16 [96, 768, 512], P('lat', 'lon')
- innovation: float32 [8, 64, 64, 128], P('lat', 'lon')
- rolled_adjoint: float32 [96, 768], P('lat', 'lon')
- down_map_gradient: float32 [2, 8, 512], replicated
- up_map_gradient: float32 [2, 8, 512], replicated
Inputs may be any that keep to these rules, and one draw needn't show every extreme that they name: `observation_index`: positions, row by row, inside the destination tile of 12 x 12 patches. `observation_count`: in every band one strip receives 128 live slots from every shard of the band, and every shard fills some strip.
All inputs are finite; a program needn't handle non-finite values.
Results may differ from a plain program's by a relative error of at most 0.008.
Values may be sent and summed in bfloat16 or wider, within the bound.
No kernel may reach another device: no remote copies, remote signals or barrier semaphores. Data moves between devices by JAX's collectives and lax.ppermute only.
A program may use at most 64 MiB of HBM per device.

v0:
```python
import math

import jax
import jax.numpy as jnp
from jax import lax
from jax.sharding import PartitionSpec as P

HEADS = 16
HEAD_DIM = 32
WIN_LAT = 6
WIN_LON = 12
SHIFT_LAT = 3
SHIFT_LON = 6


adapter_scale = 0.5
norm_eps = 1e-05
mask_fill = -1000000000.0


def shifted(value, axis, steps):
    count = lax.axis_size(axis)
    pairs = [(source, (source + steps) % count) for source in range(count)]
    return lax.ppermute(value, axis, pairs)


def split_into_windows(tile):
    n_rows, n_cols = (tile.shape[0], tile.shape[1])
    tail_shape = tile.shape[2:]
    blocks = tile.reshape((n_rows // WIN_LAT, WIN_LAT, n_cols // WIN_LON, WIN_LON) + tail_shape)
    blocks = jnp.swapaxes(blocks, 1, 2)
    return blocks.reshape((n_rows // WIN_LAT * (n_cols // WIN_LON), WIN_LAT * WIN_LON) + tail_shape)


def from_windows(window_tokens, n_rows, n_cols):
    tail_shape = window_tokens.shape[2:]
    blocks = window_tokens.reshape(
        (n_rows // WIN_LAT, n_cols // WIN_LON, WIN_LAT, WIN_LON) + tail_shape
    )
    blocks = jnp.swapaxes(blocks, 1, 2)
    return blocks.reshape((n_rows, n_cols) + tail_shape)


def split_heads(array):
    return array.reshape(array.shape[:2] + (HEADS, HEAD_DIM))


def layer_norm(features):
    center = features - jnp.mean(features, axis=-1, keepdims=True)
    spread = jnp.mean(center * center, axis=-1, keepdims=True)
    return center * lax.rsqrt(spread + norm_eps)


def window_front_pass(
    window_tokens,
    window_region,
    query_key_value_weight,
    output_weight,
    adapter_down_map,
    adapter_up_map,
    relative_position_bias,
):
    width_of_model = window_tokens.shape[2]
    normalized_input = layer_norm(window_tokens.astype(jnp.float32)).astype(jnp.bfloat16)
    frozen_query_key_value = jnp.einsum(
        "ntd,de->nte", normalized_input, query_key_value_weight, preferred_element_type=jnp.float32
    )
    reduced_rank_input = jnp.einsum(
        "qip,jyp->jqiy", normalized_input, adapter_down_map, preferred_element_type=jnp.float32
    ).astype(jnp.bfloat16)
    adapter_update = adapter_scale * jnp.einsum(
        "vwus,vso->vwuo", reduced_rank_input, adapter_up_map, preferred_element_type=jnp.float32
    )
    query_rows = (frozen_query_key_value[..., :width_of_model] + adapter_update[0]).astype(
        jnp.bfloat16
    )
    key_rows = frozen_query_key_value[..., width_of_model : 2 * width_of_model].astype(jnp.bfloat16)
    value_block_rows = (
        frozen_query_key_value[..., 2 * width_of_model :] + adapter_update[1]
    ).astype(jnp.bfloat16)
    scale_factor = 1.0 / math.sqrt(HEAD_DIM)
    scores = (
        jnp.einsum(
            "nthe,nuhe->nhtu",
            split_heads(query_rows),
            split_heads(key_rows),
            preferred_element_type=jnp.float32,
        )
        * scale_factor
        + relative_position_bias[None]
    )
    same_region = (window_region[:, :, None] == window_region[:, None, :])[:, None]
    scores = jnp.where(same_region, scores, mask_fill)
    row_max = jnp.max(scores, axis=-1, keepdims=True)
    raised = jnp.exp(scores - row_max)
    probs = raised / jnp.sum(raised, axis=-1, keepdims=True)
    probs_bf = probs.astype(jnp.bfloat16)
    attended = jnp.einsum(
        "nhtu,nuhe->nthe",
        probs_bf,
        split_heads(value_block_rows),
        preferred_element_type=jnp.float32,
    )
    attended = attended.reshape(window_tokens.shape).astype(jnp.bfloat16)
    projected = jnp.einsum(
        "ntd,de->nte", attended, output_weight, preferred_element_type=jnp.float32
    )
    output_rows = (window_tokens.astype(jnp.float32) + projected).astype(jnp.bfloat16)
    return (
        output_rows,
        (normalized_input, reduced_rank_input, key_rows, value_block_rows, probs, probs_bf),
    )


def window_reverse_pass(input_gradient, stored_state, output_weight, adapter_up_map):
    normalized_input, reduced_rank_input, key_rows, value_block_rows, probs, probs_bf = stored_state
    grad_attn = jnp.einsum(
        "nte,de->ntd", input_gradient, output_weight, preferred_element_type=jnp.float32
    ).astype(jnp.bfloat16)
    heads_grad = split_heads(grad_attn)
    grad_probs = jnp.einsum(
        "nthe,nuhe->nhtu",
        heads_grad,
        split_heads(value_block_rows),
        preferred_element_type=jnp.float32,
    )
    grad_value = jnp.einsum(
        "nhtu,nthe->nuhe", probs_bf, heads_grad, preferred_element_type=jnp.float32
    ).reshape(input_gradient.shape)
    weighted_sum = jnp.sum(grad_probs * probs, axis=-1, keepdims=True)
    grad_scores = (probs * (grad_probs - weighted_sum) / math.sqrt(HEAD_DIM)).astype(jnp.bfloat16)
    grad_query = jnp.einsum(
        "nhtu,nuhe->nthe", grad_scores, split_heads(key_rows), preferred_element_type=jnp.float32
    ).reshape(input_gradient.shape)
    paired_gradient = jnp.stack([grad_query, grad_value]).astype(jnp.bfloat16)
    up_map_gradient = adapter_scale * jnp.einsum(
        "msqa,msqu->mau", reduced_rank_input, paired_gradient, preferred_element_type=jnp.float32
    )
    low_rank_gradient = (
        adapter_scale
        * jnp.einsum(
            "busf,baf->busa", paired_gradient, adapter_up_map, preferred_element_type=jnp.float32
        )
    ).astype(jnp.bfloat16)
    down_map_gradient = jnp.einsum(
        "cntr,ntd->crd", low_rank_gradient, normalized_input, preferred_element_type=jnp.float32
    )
    return (down_map_gradient, up_map_gradient)


def slot_block(field_rows, index_block, weight_block, value_block, count_block, loss_scale):
    cells = field_rows.shape[-1]
    slot_total = value_block.shape[-1]
    selector = (index_block[..., None] == jnp.arange(cells, dtype=jnp.int32)).astype(jnp.float32)
    picked = jnp.einsum("gksc,gc->gks", selector, field_rows, precision=lax.Precision.HIGHEST)
    predicted = jnp.sum(weight_block * picked, axis=1)
    live_slots = jnp.arange(slot_total, dtype=jnp.int32)[None, :] < count_block[:, None]
    innov_block = jnp.where(live_slots, predicted - value_block, 0.0)
    terms = loss_scale * weight_block * innov_block[:, None, :]
    cell_terms = jnp.einsum("gksc,gks->gc", selector, terms, precision=lax.Precision.HIGHEST)
    return (innov_block, cell_terms)


def blocked_slots(field_rows, index_all, weight_all, value_all, count_all, loss_scale):
    strip_total = index_all.shape[0]
    group = math.gcd(8, strip_total)
    blocks = strip_total // group

    def regroup(array):
        return array.reshape((blocks, group) + array.shape[1:])

    def one_block(carry, packed):
        fields, index_block, weight_block, value_block, count_block = packed
        innov_block, cell_terms = slot_block(
            fields, index_block, weight_block, value_block, count_block, loss_scale
        )
        return (carry, (innov_block, cell_terms))

    unused, (innov_all, cell_all) = lax.scan(
        one_block,
        0,
        (
            regroup(field_rows),
            regroup(index_all),
            regroup(weight_all),
            regroup(value_all),
            regroup(count_all),
        ),
    )
    return (innov_all.reshape(value_all.shape), cell_all.reshape(field_rows.shape))


def shards(
    tokens,
    query_key_value_weight,
    output_weight,
    adapter_down_map,
    adapter_up_map,
    relative_position_bias,
    readout,
    observation_index,
    observation_weight,
    observation_value,
    observation_count,
):
    n_rows, n_cols = (tokens.shape[0], tokens.shape[1])
    lat_count = lax.axis_size("lat")
    lon_count = lax.axis_size("lon")
    from_below = shifted(tokens[:SHIFT_LAT], "lat", -1)
    moved_rows = jnp.concatenate([tokens[SHIFT_LAT:], from_below], axis=0)
    beside = shifted(moved_rows[:, :SHIFT_LON], "lon", -1)
    cyclic_shifted = jnp.concatenate([moved_rows[:, SHIFT_LON:], beside], axis=1)
    global_row = lax.axis_index("lat") * n_rows + jnp.arange(n_rows, dtype=jnp.int32)
    region_rows = (global_row >= n_rows * lat_count - SHIFT_LAT).astype(jnp.int32)
    window_region = split_into_windows(jnp.broadcast_to(region_rows[:, None], (n_rows, n_cols)))
    output_rows, stored_state = window_front_pass(
        split_into_windows(cyclic_shifted),
        window_region,
        query_key_value_weight,
        output_weight,
        adapter_down_map,
        adapter_up_map,
        relative_position_bias,
    )
    rolled_out = from_windows(output_rows, n_rows, n_cols)
    upper_rows = shifted(rolled_out[n_rows - SHIFT_LAT :], "lat", 1)
    back_rows = jnp.concatenate([upper_rows, rolled_out[: n_rows - SHIFT_LAT]], axis=0)
    leftward = shifted(back_rows[:, n_cols - SHIFT_LON :], "lon", 1)
    block_out = jnp.concatenate([leftward, back_rows[:, : n_cols - SHIFT_LON]], axis=1)
    obs_field = jnp.dot(
        block_out.reshape(n_rows * n_cols, -1), readout, preferred_element_type=jnp.float32
    )
    loss_scale = 1.0 / math.sqrt(lat_count * lon_count)
    strip_total = observation_value.shape[2]
    cells = n_rows * n_cols
    got_index, got_count = (
        lax.all_to_all(observation_index, "lon", split_axis=2, concat_axis=2, tiled=True),
        lax.all_to_all(observation_count, "lon", split_axis=2, concat_axis=2, tiled=True),
    )
    got_weight, got_value = (
        lax.all_to_all(observation_weight, "lon", split_axis=2, concat_axis=2, tiled=True),
        lax.all_to_all(observation_value, "lon", split_axis=2, concat_axis=2, tiled=True),
    )
    field_rows = jnp.broadcast_to(obs_field[None, :], (strip_total, cells))
    owner_innov, cell_all = blocked_slots(
        field_rows, got_index[0, 0], got_weight[0, 0], got_value[0, 0], got_count[0, 0], loss_scale
    )
    adjoint = jnp.sum(cell_all, axis=0)
    innovation = lax.all_to_all(
        owner_innov.reshape(observation_value.shape), "lon", split_axis=2, concat_axis=2, tiled=True
    )
    adjoint = adjoint.reshape(n_rows, n_cols)
    adjoint_below = shifted(adjoint[:SHIFT_LAT], "lat", -1)
    adjoint_rows = jnp.concatenate([adjoint[SHIFT_LAT:], adjoint_below], axis=0)
    adjoint_beside = shifted(adjoint_rows[:, :SHIFT_LON], "lon", -1)
    adjoint_rolled = jnp.concatenate([adjoint_rows[:, SHIFT_LON:], adjoint_beside], axis=1)
    rolled_adjoint = adjoint_rolled * math.sqrt(lat_count * lon_count)
    input_gradient = (adjoint_rolled[:, :, None] * readout.astype(jnp.float32)).astype(jnp.bfloat16)
    down_map_gradient, up_map_gradient = window_reverse_pass(
        split_into_windows(input_gradient), stored_state, output_weight, adapter_up_map
    )
    down_map_gradient, up_map_gradient = lax.psum(
        (down_map_gradient, up_map_gradient), ("lat", "lon")
    )
    return (block_out, innovation, rolled_adjoint, down_map_gradient, up_map_gradient)


def solution(mesh):
    return jax.shard_map(
        shards,
        mesh=mesh,
        in_specs=(
            P("lat", "lon", None),
            P(),
            P(),
            P(),
            P(),
            P(),
            P(),
            P("lat", "lon", None, None, None),
            P("lat", "lon", None, None, None),
            P("lat", "lon", None, None),
            P("lat", "lon", None),
        ),
        out_specs=(P("lat", "lon", None), P("lat", "lon", None, None), P("lat", "lon"), P(), P()),
        check_vma=False,
    )
```

profile of v0, /device:TPU:1, one launch (start us, length us, event | category | flops | bytes accessed | tf_op | source)
XLA Modules:
  0.0 654.5 jit_solution(4967325546152505416)
XLA Ops:
  7.2 1.0 slice.75
  8.1 13.7 %collective-permute-start = (bf16[3,12,512]{2,1,0:T(8,128)(2,1)S(1)}, bf16[3,12,512]{2,1,0:T(8,128)(2,1)S(1)}, u32[]{:S(2)}, u32[]{:S(2)}) collective-permute-start(bf16[3,12,512]{2,1,0:T(8,128)(2,1)S(1)} %slice.75), channel_id=1, source_target_pairs={{0,448},{64,0},{128,64},{192,128},{256,192},{320,256},{384,320},{4... | collective-permute-start | bytes 110600 | tf_op jit(solution)/shard_map/ppermute | solution.py:24
  21.8 1.4 copy.88
  23.2 14.2 %all-to-all-start = ((s32[1,1,64]{1,0,2:T(1,128)}), s32[1,1,64]{1,0,2:T(1,128)S(1)}, u32[]{:S(2)}, u32[]{:S(2)}) async-start(s32[1,1,64]{1,0,2:T(1,128)} %copy.88), calls=%async_computation | async-start | bytes 65536 | tf_op jit(solution)/shard_map/all_to_all | solution.py:238
  37.4 0.9 slice.74
  38.6 2.4 collective-permute-start.1
  41.8 11.7 %collective-permute-done.1 = bf16[12,6,512]{2,1,0:T(8,128)(2,1)S(1)} collective-permute-done((bf16[12,6,512]{2,1,0:T(8,128)(2,1)S(1)}, bf16[12,6,512]{2,1,0:T(8,128)(2,1)S(1)}, u32[]{:S(2)}, u32[]{:S(2)}) %collective-permute-start.1) | collective-permute-done | bytes 73760 | tf_op jit(solution)/shard_map/ppermute | solution.py:24
  57.3 20.8 %all-to-all-start.3 = ((f32[1,1,64,128]{3,1,0,2:T(1,128)}), f32[1,1,64,128]{3,1,0,2:T(1,128)S(1)}, u32[]{:S(2)}, u32[]{:S(2)}) async-start(f32[1,1,64,128]{3,1,0,2:T(1,128)} %bitcast.33), calls=%async_computation.3 | async-start | bytes 65536 | tf_op jit(solution)/shard_map/all_to_all | solution.py:242
  78.1 2.4 fusion.61
  80.6 13.8 %all-to-all-done.3 = f32[1,1,64,128]{3,1,0,2:T(1,128)S(1)} async-done(((f32[1,1,64,128]{3,1,0,2:T(1,128)}), f32[1,1,64,128]{3,1,0,2:T(1,128)S(1)}, u32[]{:S(2)}, u32[]{:S(2)}) %all-to-all-start.3) | async-done | bytes 32800 | tf_op jit(solution)/shard_map/all_to_all | solution.py:242
  94.4 4.8 all-to-all-start.1
  99.3 1.6 convolution_convert_fusion.1
  101.2 3.5 collective-permute-start.2
  104.7 11.9 %all-to-all-done.1 = f32[1,1,64,4,128]{4,3,1,0,2:T(4,128)S(1)} async-done(((f32[1,1,64,4,128]{4,3,1,0,2:T(4,128)}), f32[1,1,64,4,128]{4,3,1,0,2:T(4,128)S(1)}, u32[]{:S(2)}, u32[]{:S(2)}) %all-to-all-start.1) | async-done | bytes 131104 | tf_op jit(solution)/shard_map/all_to_all | solution.py:241
  116.6 6.1 all-to-all-start.2
  122.7 12.3 %collective-permute-start.3 = (bf16[12,6,512]{2,1,0:T(8,128)(2,1)S(1)}, bf16[12,6,512]{2,1,0:T(8,128)(2,1)S(1)}, u32[]{:S(2)}, u32[]{:S(2)}) collective-permute-start(bf16[12,6,512]{2,1,0:T(8,128)(2,1)S(1)} %fusion.46), channel_id=1, source_target_pairs={{0,1},{1,2},{2,3},{3,4},{4,5},{5,6},{6,7},{7,8},{8,9},{9,10},{10,1... | collective-permute-start | bytes 221192 | tf_op jit(solution)/shard_map/ppermute | solution.py:24
  135.1 1.2 reduce.3
  136.4 1.2 collective-permute-done.3
  137.8 2.1 all-to-all-done.2
  139.9 22.5 %while.12 = (s32[]{:T(128)}, f32[8,8,128]{2,1,0:T(8,128)}, f32[8,8,144]{2,1,0:T(8,128)S(1)}, s32[8,8]{1,0:T(8,128)S(1)}, f32[8,8,4,128]{3,2,1,0:T(4,128)S(1)}, /...) while((s32[]{:T(128)}, f32[8,8,128]{2,1,0:T(8,128)}, ...), condition=%wide.region_6.7_spmd, body=%wide.region_4.6_spmd.sunk | while | flops 15353858 | bytes 232185 | solution.py:179
  140.0 0.8 fusion.87
  140.9 1.1 fusion.92
  142.8 0.8 fusion.87
  143.7 1.1 fusion.92
  145.6 0.8 fusion.87
  146.5 1.1 fusion.92
  148.4 0.8 fusion.87
  149.3 1.1 fusion.92
  151.2 0.8 fusion.87
  152.2 1.1 fusion.92
  154.0 0.8 fusion.87
  155.0 1.1 fusion.92
  156.8 0.8 fusion.87
  157.8 1.1 fusion.92
  159.6 0.8 fusion.87
  160.6 1.1 fusion.92
  162.5 8.5 %collective-permute-start.4 = (f32[3,12]{1,0:T(4,128)S(1)}, f32[3,12]{1,0:T(4,128)S(1)}, u32[]{:S(2)}, u32[]{:S(2)}) collective-permute-start(f32[3,12]{1,0:T(4,128)S(1)} %slice.90), channel_id=1, source_target_pairs={{0,448},{64,0},{128,64},{192,128},{256,192},{320,256},{384,320},{4... | collective-permute-start | bytes 440 | tf_op jit(solution)/shard_map/ppermute | solution.py:24
  171.8 7.4 %collective-permute-start.5 = (f32[12,6]{1,0:T(8,128)S(1)}, f32[12,6]{1,0:T(8,128)S(1)}, u32[]{:S(2)}, u32[]{:S(2)}) collective-permute-start(f32[12,6]{1,0:T(8,128)S(1)} %get-tuple-element.90), channel_id=1, source_target_pairs={{0,63},{1,0},{2,1},{3,2},{4,3},{5,4},{6,5},{7,6},{8,7},{9,8},{10,9... | collective-permute-start | bytes 872 | tf_op jit(solution)/shard_map/ppermute | solution.py:24
  179.2 12.0 %all-to-all-start.4 = ((f32[1,1,64,128]{3,1,0,2:T(1,128)}), f32[1,1,64,128]{3,1,0,2:T(1,128)S(1)}, u32[]{:S(2)}, u32[]{:S(2)}) async-start(f32[1,1,64,128]{3,1,0,2:T(1,128)} %bitcast.35), calls=%async_computation.4 | async-start | bytes 65536 | tf_op jit(solution)/shard_map/all_to_all | solution.py:249
  193.8 1.1 convolution_convert_fusion
  194.9 2.9 fusion.24
  197.8 1.1 copy.95
  199.1 0.8 fusion.26
  199.9 1.0 convolution_bitcast_fusion.1
  200.9 6.6 %all-to-all-done.4 = f32[1,1,64,128]{3,1,0,2:T(1,128)S(1)} async-done(((f32[1,1,64,128]{3,1,0,2:T(1,128)}), f32[1,1,64,128]{3,1,0,2:T(1,128)S(1)}, u32[]{:S(2)}, u32[]{:S(2)}) %all-to-all-start.4) | async-done | bytes 32800 | tf_op jit(solution)/shard_map/all_to_all | solution.py:249
  207.5 436.7 %all-reduce.3.cloned.1.call-done = (f32[2,8,512]{2,1,0:T(8,128)}, f32[2,8,512]{2,1,0:T(8,128)}) async-done(((f32[2,8,512]{2,1,0:T(8,128)}, f32[2,8,512]{2,1,0:T(8,128)}), (f32[2,8,512]{2,1,0:T(8,128)}, f32[2,8,512]{2,1,0:T(8,128)})) %all-reduce.3.cloned.1.call-update) | async-done | bytes 65552 | tf_op jit(solution)/shard_map/psum | solution.py:262
  644.9 1.4 copy.138
  646.2 1.4 copy.139
  (157 shorter events, 16.3 us)
Async XLA Ops:
  7.2 47.1 %copy-start = (bf16[512,1536]{1,0:T(8,128)(2,1)S(1)}, bf16[512,1536]{1,0:T(8,128)(2,1)}, u32[]{:S(2)}) copy-start(bf16[512,1536]{1,0:T(8,128)(2,1)} %param.14) | copy-start | bytes 4718596
  7.2 34.4 %copy-start.3 = (f32[16,72,72]{2,1,0:T(8,128)S(1)}, f32[16,72,72]{2,1,0:T(8,128)}, u32[]{:S(2)}) copy-start(f32[16,72,72]{2,1,0:T(8,128)} %param.18) | copy-start | bytes 995332
  8.1 30.4 %collective-permute-start = (bf16[3,12,512]{2,1,0:T(8,128)(2,1)S(1)}, bf16[3,12,512]{2,1,0:T(8,128)(2,1)S(1)}, u32[]{:S(2)}, u32[]{:S(2)}) collective-permute-start(bf16[3,12,512]{2,1,0:T(8,128)(2,1)S(1)} %slice.75), channel_id=1, source_target_pairs={{0,448},{64,0},{128,64},{192,128},{256,192},{320,256},{384,320},{4... | collective-permute-start | bytes 110600 | tf_op jit(solution)/shard_map/ppermute | solution.py:24
  23.2 33.4 %all-to-all-start = ((s32[1,1,64]{1,0,2:T(1,128)}), s32[1,1,64]{1,0,2:T(1,128)S(1)}, u32[]{:S(2)}, u32[]{:S(2)}) async-start(s32[1,1,64]{1,0,2:T(1,128)} %copy.88), calls=%async_computation | async-start | bytes 65536 | tf_op jit(solution)/shard_map/all_to_all | solution.py:238
  38.6 14.9 %collective-permute-start.1 = (bf16[12,6,512]{2,1,0:T(8,128)(2,1)S(1)}, bf16[12,6,512]{2,1,0:T(8,128)(2,1)S(1)}, u32[]{:S(2)}, u32[]{:S(2)}) collective-permute-start(bf16[12,6,512]{2,1,0:T(8,128)(2,1)S(1)} %get-tuple-element.88), channel_id=1, source_target_pairs={{0,63},{1,0},{2,1},{3,2},{4,3},{5,4},{6,5},{7,6},{8,7},{9,8},{10,9... | collective-permute-start | bytes 221192 | tf_op jit(solution)/shard_map/ppermute | solution.py:24
  54.3 0.7 copy-start.14
  54.3 1.5 copy-start.12
  55.1 0.6 copy-start.9
  56.1 22.0 %copy-start.11 = (pred[2,72,72]{1,2,0:T(8,128)(4,1)S(1)}, pred[2,72,72]{1,2,0:T(8,128)(4,1)}, u32[]{:S(2)}) copy-start(pred[2,72,72]{1,2,0:T(8,128)(4,1)} %broadcast_compare_fusion) | copy-start | bytes 31108
  56.6 23.9 %copy-start.4 = (bf16[2,72,512]{1,2,0:T(8,128)(2,1)}, bf16[2,72,512]{1,2,0:T(8,128)(2,1)S(1)}, u32[]{:S(2)}) copy-start(bf16[2,72,512]{1,2,0:T(8,128)(2,1)S(1)} %copy.84) | copy-start | bytes 442372
  56.6 0.7 copy-start.7
  57.3 37.2 %all-to-all-start.3 = ((f32[1,1,64,128]{3,1,0,2:T(1,128)}), f32[1,1,64,128]{3,1,0,2:T(1,128)S(1)}, u32[]{:S(2)}, u32[]{:S(2)}) async-start(f32[1,1,64,128]{3,1,0,2:T(1,128)} %bitcast.33), calls=%async_computation.3 | async-start | bytes 65536 | tf_op jit(solution)/shard_map/all_to_all | solution.py:242
  94.4 22.2 %all-to-all-start.1 = ((f32[1,1,64,4,128]{4,3,1,0,2:T(4,128)}), f32[1,1,64,4,128]{4,3,1,0,2:T(4,128)S(1)}, u32[]{:S(2)}, u32[]{:S(2)}) async-start(f32[1,1,64,4,128]{4,3,1,0,2:T(4,128)} %bitcast.28), calls=%async_computation.1 | async-start | bytes 262144 | tf_op jit(solution)/shard_map/all_to_all | solution.py:241
  99.3 1.6 copy-start.1
  100.9 34.1 %copy-start.15 = (bf16[512]{0:T(512)(128)(2,1)S(1)}, bf16[512]{0:T(512)(128)(2,1)}, u32[]{:S(2)}) copy-start(bf16[512]{0:T(512)(128)(2,1)} %param.19) | copy-start | bytes 3076
  100.9 34.1 %copy-start.8 = (s32[1,1,64]{1,0,2:T(1,128)S(1)}, s32[1,1,64]{1,0,2:T(1,128)}, u32[]{:S(2)}) copy-start(s32[1,1,64]{1,0,2:T(1,128)} %copy-done.7) | copy-start | bytes 772
  101.2 21.4 %collective-permute-start.2 = (bf16[3,12,512]{2,1,0:T(8,128)(2,1)S(1)}, bf16[3,12,512]{2,1,0:T(8,128)(2,1)S(1)}, u32[]{:S(2)}, u32[]{:S(2)}) collective-permute-start(bf16[3,12,512]{2,1,0:T(8,128)(2,1)S(1)} %slice.100), channel_id=1, source_target_pairs={{0,64},{64,128},{128,192},{192,256},{256,320},{320,384},{384,448},... | collective-permute-start | bytes 110600 | tf_op jit(solution)/shard_map/ppermute | solution.py:24
  116.6 23.3 %all-to-all-start.2 = ((s32[1,1,64,4,128]{4,3,1,0,2:T(4,128)}), s32[1,1,64,4,128]{4,3,1,0,2:T(4,128)S(1)}, u32[]{:S(2)}, u32[]{:S(2)}) async-start(s32[1,1,64,4,128]{4,3,1,0,2:T(4,128)} %bitcast.30), calls=%async_computation.2 | async-start | bytes 262144 | tf_op jit(solution)/shard_map/all_to_all | solution.py:237
  122.7 14.8 %collective-permute-start.3 = (bf16[12,6,512]{2,1,0:T(8,128)(2,1)S(1)}, bf16[12,6,512]{2,1,0:T(8,128)(2,1)S(1)}, u32[]{:S(2)}, u32[]{:S(2)}) collective-permute-start(bf16[12,6,512]{2,1,0:T(8,128)(2,1)S(1)} %fusion.46), channel_id=1, source_target_pairs={{0,1},{1,2},{2,3},{3,4},{4,5},{5,6},{6,7},{7,8},{8,9},{9,10},{10,1... | collective-permute-start | bytes 221192 | tf_op jit(solution)/shard_map/ppermute | solution.py:24
  137.6 2.3 copy-start.2
  162.5 9.2 %collective-permute-start.4 = (f32[3,12]{1,0:T(4,128)S(1)}, f32[3,12]{1,0:T(4,128)S(1)}, u32[]{:S(2)}, u32[]{:S(2)}) collective-permute-start(f32[3,12]{1,0:T(4,128)S(1)} %slice.90), channel_id=1, source_target_pairs={{0,448},{64,0},{128,64},{192,128},{256,192},{320,256},{384,320},{4... | collective-permute-start | bytes 440 | tf_op jit(solution)/shard_map/ppermute | solution.py:24
  171.8 19.4 %collective-permute-start.5 = (f32[12,6]{1,0:T(8,128)S(1)}, f32[12,6]{1,0:T(8,128)S(1)}, u32[]{:S(2)}, u32[]{:S(2)}) collective-permute-start(f32[12,6]{1,0:T(8,128)S(1)} %get-tuple-element.90), channel_id=1, source_target_pairs={{0,63},{1,0},{2,1},{3,2},{4,3},{5,4},{6,5},{7,6},{8,7},{9,8},{10,9... | collective-permute-start | bytes 872 | tf_op jit(solution)/shard_map/ppermute | solution.py:24
  179.2 28.4 %all-to-all-start.4 = ((f32[1,1,64,128]{3,1,0,2:T(1,128)}), f32[1,1,64,128]{3,1,0,2:T(1,128)S(1)}, u32[]{:S(2)}, u32[]{:S(2)}) async-start(f32[1,1,64,128]{3,1,0,2:T(1,128)} %bitcast.35), calls=%async_computation.4 | async-start | bytes 65536 | tf_op jit(solution)/shard_map/all_to_all | solution.py:249
  191.2 453.1 %all-reduce.3.cloned.1.call-start = ((), (), s32[]{:S(2)}) async-start(), calls=%async_computation.5 | async-start | bytes 131072 | tf_op jit(solution)/shard_map/psum | solution.py:262
  192.3 0.7 copy-start.17
  192.5 1.3 copy-start.16
  193.8 1.1 copy-start.5
  194.9 4.0 copy-start.6
  194.9 4.1 copy-start.10
  197.8 2.1 copy-start.13
Sparse Core Ops, SparseCore 0:
  201.1 443.1 all-reduce.2
where the time goes:
time: 655 us; the launch traced here: 654 us
  waiting for transfers between devices  485 us (74%)
  starting transfers between devices  105 us (16%)
  matrix products  27.7 us (4%)
  between operations  14.6 us (2%)
  local copies, waits for them, and re-layouts  12.2 us (2%)
  other arithmetic  9.78 us (1%)
    psum x1, waiting for transfers between devices, shards(): lax.psum((down_map_gradient, up_map_gradient), ('lat', 'lon'))  437 us
    ppermute x6, starting transfers between devices, shifted(): return lax.ppermute(value, axis, pairs)  47.6 us
    all_to_all x1, starting transfers between devices, shards(): lax.all_to_all(observation_value, 'lon', split_axis=2, concat_axis=2, til...  20.8 us
    all_to_all x1, starting transfers between devices, shards(): lax.all_to_all(observation_count, 'lon', split_axis=2, concat_axis=2, til...  14.2 us
    all_to_all x1, waiting for transfers between devices, shards(): lax.all_to_all(observation_value, 'lon', split_axis=2, concat_axis=2, til...  13.8 us
    ppermute x6, waiting for transfers between devices, shifted(): return lax.ppermute(value, axis, pairs)  13.4 us
  transfers between devices with their start and end apart: 12, of which 8 were waited for; matrix products, arithmetic and copies ran while one was open for 3% of the time, Pallas kernels for 0%

commit v1 on v0

v1 whole, which is shorter than its diff:
```python
import functools
import math

import jax
import jax.numpy as jnp
from jax import lax
from jax.experimental import pallas as pl
from jax.experimental.pallas import tpu as pltpu
from jax.sharding import PartitionSpec as P

F32 = jnp.float32
BF16 = jnp.bfloat16
HEADS = 16
HEAD_DIM = 32
MODEL = 512
GROUP = 24
SLOT = 32
LIVE = 18
OWN = 8 * GROUP
NORM_EPS = 1e-05
NEG = -1e30
NT = (((1,), (1,)), ((), ()))
TN = (((0,), (0,)), ((), ()))
NN = (((1,), (0,)), ((), ()))


def mm(a, b, dims=NN, precision=None):
    return lax.dot_general(a, b, dims, precision=precision, preferred_element_type=F32)


def exact(a, b, dims=NN):
    return mm(a, b, dims, precision=lax.Precision.HIGHEST)


def own_slot(n):
    half, row = n // 4, n % 4
    window_row, part = (row + 1) // 2, (row + 1) % 2
    return ((half * 3 + window_row) * 2 + (1 - half)) * 2 + part


def bias_kernel(bias_ref, out_ref, wide_ref):
    shape = (72, 128)
    lane = lax.broadcasted_iota(jnp.int32, shape, 1)
    row = lane % SLOT
    column = 12 * (3 * ((lane // SLOT) % 2) + row // 6) + 6 * (lane // 64) + row % 6
    hit = (column == lax.broadcasted_iota(jnp.int32, shape, 0)) & (row < LIVE)
    wide = exact(bias_ref[...], hit.astype(F32))
    lanes = lax.broadcasted_iota(jnp.int32, (1, 128), 1)
    wide = wide + jnp.where(lanes % SLOT < LIVE, 0.0, NEG)
    wide_ref[...] = wide.reshape(HEADS, 72, 128)
    out_ref[...] = jnp.zeros_like(out_ref)
    for parity in range(2):
        for half in range(2):
            for m in range(3):
                start = 12 * (3 * (1 - parity) + m) + 6 * (1 - half)
                out_ref[parity * 2 + half, :, 6 * m : 6 * m + 6, :] = wide_ref[:, start : start + 6, :]


def ordered_bias(bias):
    return pl.pallas_call(
        bias_kernel,
        out_shape=jax.ShapeDtypeStruct((4, HEADS, GROUP, 128), F32),
        scratch_shapes=[pltpu.VMEM((HEADS, 72, 128), F32)],
        cost_estimate=pl.CostEstimate(flops=2 * 10**8, bytes_accessed=2 * 10**6, transcendentals=0),
        name="ordered_bias",
    )(bias.reshape(HEADS * 72, 72))


def forward_kernel(
    flags_ref,
    own_ref,
    near_lon_ref,
    far_lon_ref,
    near_lat_ref,
    far_lat_ref,
    qkv_ref,
    wo_ref,
    down_ref,
    up_ref,
    readout_ref,
    bias_ref,
    block_ref,
    field_ref,
    probs_ref,
    gq_ref,
    low_ref,
    norm_ref,
    w_ref,
    k_ref,
    v_ref,
    q_ref,
    att_ref,
):
    even_lon = flags_ref[0] == 0
    even_lat = flags_ref[1] == 0
    first = flags_ref[2].astype(F32)
    last = flags_ref[3].astype(F32)

    def pick(cond, a, b):
        return jnp.where(cond, a.astype(F32), b.astype(F32))

    for strip in range(4):
        for group in range(6):
            if group == 0:
                x = pick(even_lat, far_lat_ref[strip], near_lat_ref[strip])
            elif group == 5:
                x = pick(even_lat, near_lat_ref[strip], far_lat_ref[strip])
            elif strip == 0:
                x = pick(even_lon, far_lon_ref[group - 1], near_lon_ref[group - 1])
            elif strip == 3:
                x = pick(even_lon, near_lon_ref[group - 1], far_lon_ref[group - 1])
            else:
                x = own_ref[strip - 1, group - 1].astype(F32)
            center = x - jnp.mean(x, axis=1, keepdims=True)
            spread = jnp.mean(center * center, axis=1, keepdims=True)
            y = center * lax.rsqrt(spread + NORM_EPS)
            y = jnp.concatenate([y, jnp.zeros((SLOT - GROUP, MODEL), F32)], axis=0).astype(BF16)
            slot = (((strip // 2) * 3 + group // 2) * 2 + strip % 2) * 2 + group % 2
            norm_ref[slot * SLOT : (slot + 1) * SLOT, :] = y

    normed = norm_ref[...]
    rank_row = lax.broadcasted_iota(jnp.int32, (16, MODEL), 0)
    up_half = 0.5 * up_ref[...].astype(F32)
    up_query = jnp.where(rank_row < 8, up_half, 0.0).astype(BF16)
    up_value = jnp.where(rank_row >= 8, up_half, 0.0).astype(BF16)
    low = mm(normed, down_ref[...], NT).astype(BF16)
    low_ref[...] = low
    k_ref[...] = mm(normed, qkv_ref[:, MODEL : 2 * MODEL]).astype(BF16)
    v_ref[...] = (mm(normed, qkv_ref[:, 2 * MODEL :]) + mm(low, up_value)).astype(BF16)
    own_rows = [slice(own_slot(n) * SLOT, (own_slot(n) + 1) * SLOT) for n in range(8)]
    normed_own = jnp.concatenate([norm_ref[rows, :] for rows in own_rows], axis=0)
    low_own = jnp.concatenate([low_ref[rows, :] for rows in own_rows], axis=0)
    query = mm(normed_own, qkv_ref[:, :MODEL]) + mm(low_own, up_query)
    q_ref[...] = query.astype(BF16).astype(F32)

    readout = jnp.broadcast_to(readout_ref[...].astype(F32), (8, MODEL)).astype(BF16)
    w_row = mm(readout, wo_ref[...], NT)
    w_ref[...] = w_row

    scale = 1.0 / math.sqrt(HEAD_DIM)
    head_of = lax.broadcasted_iota(jnp.int32, (8, 1, 256), 2) // HEAD_DIM
    head_mask = head_of == lax.broadcasted_iota(jnp.int32, (8, 1, 256), 0)
    lane_part = (lax.broadcasted_iota(jnp.int32, (1, 128), 1) // SLOT) % 2
    masked_first = jnp.where(lane_part == 0, NEG * first, 0.0)
    masked_last = jnp.where(lane_part == 1, NEG * last, 0.0)

    def fold(rows):
        return jnp.sum(jnp.where(head_mask, rows.reshape(8, GROUP, 256), 0.0), axis=0)

    for n in range(8):
        half, row = n // 4, n % 4
        window = half * 3 + (row + 1) // 2
        keys = slice(window * 128, (window + 1) * 128)
        for part in range(2):
            cols = slice(256 * part, 256 * (part + 1))
            k_win, v_win = k_ref[keys, cols], v_ref[keys, cols]
            q_own = q_ref[n * SLOT : n * SLOT + GROUP, cols]
            lhs = jnp.where(head_mask, q_own[None], 0.0).reshape(8 * GROUP, 256).astype(BF16)
            bias = bias_ref[(row % 2) * 2 + half, 8 * part : 8 * part + 8].reshape(8 * GROUP, 128)
            scores = mm(lhs, k_win, NT) * scale + bias
            if row == 0:
                scores = scores + masked_first
            if row == 3:
                scores = scores + masked_last
            raised = jnp.exp(scores - jnp.max(scores, axis=1, keepdims=True))
            probs = raised * (1.0 / jnp.sum(raised, axis=1, keepdims=True))
            probs_bf = probs.astype(BF16)
            probs_ref[n, 8 * GROUP * part : 8 * GROUP * (part + 1), :] = probs_bf
            att_ref[n * GROUP : (n + 1) * GROUP, cols] = fold(mm(probs_bf, v_win))
            w_masked = jnp.where(head_mask[:, 0, :], w_row[:, cols], 0.0)
            w_high = w_masked.astype(BF16).astype(F32)
            w_pair = jnp.concatenate([w_high, w_masked - w_high], axis=0).astype(BF16)
            v_pair = mm(w_pair, v_win, NT)
            v_w = (v_pair[:8] + v_pair[8:]).reshape(8, 1, 128)
            probs3 = probs.reshape(8, GROUP, 128)
            mean = jnp.sum(probs3 * v_w, axis=2, keepdims=True)
            slope = (probs3 * (v_w - mean) * scale).reshape(8 * GROUP, 128).astype(BF16)
            gq_ref[n * GROUP : (n + 1) * GROUP, cols] = fold(mm(slope, k_win))

    x_own = own_ref[...].astype(F32).reshape(OWN, MODEL)
    out = (x_own + mm(att_ref[...].astype(BF16), wo_ref[...])).astype(BF16)
    block_ref[...] = out
    field_ref[...] = jnp.zeros_like(field_ref)
    field_ref[:, :OWN] = mm(readout, out, NT)


def forward(flags, own, near_lon, far_lon, near_lat, far_lat, qkv, wo, down, up, readout, bias):
    shape = jax.ShapeDtypeStruct
    vmem = pl.BlockSpec(memory_space=pltpu.VMEM)
    return pl.pallas_call(
        forward_kernel,
        in_specs=[pl.BlockSpec(memory_space=pltpu.SMEM)] + [vmem] * 11,
        out_specs=[vmem] * 7,
        out_shape=[
            shape((OWN, MODEL), BF16),
            shape((8, 256), F32),
            shape((8, HEADS * GROUP, 128), BF16),
            shape((OWN, MODEL), F32),
            shape((24 * SLOT, 16), BF16),
            shape((24 * SLOT, MODEL), BF16),
            shape((8, MODEL), F32),
        ],
        scratch_shapes=[
            pltpu.VMEM((24 * SLOT, MODEL), BF16),
            pltpu.VMEM((24 * SLOT, MODEL), BF16),
            pltpu.VMEM((8 * SLOT, MODEL), F32),
            pltpu.VMEM((OWN, MODEL), F32),
        ],
        compiler_params=pltpu.CompilerParams(vmem_limit_bytes=40 * 1024 * 1024),
        cost_estimate=pl.CostEstimate(
            flops=3 * 10**9, bytes_accessed=8 * 10**6, transcendentals=4 * 10**5
        ),
        name="window_forward",
    )(flags, own, near_lon, far_lon, near_lat, far_lat, qkv, wo, down, up, readout, bias)


def observe_kernel(
    slots_ref,
    field_ref,
    probs_ref,
    gq_ref,
    low_ref,
    norm_ref,
    w_ref,
    up_ref,
    innov_ref,
    adjoint_ref,
    grads_ref,
    term_ref,
    place_ref,
    loss_scale,
):
    sources = innov_ref.shape[0]
    field_low = jnp.broadcast_to(field_ref[0:1, 0:128], (sources, 128))
    field_high = jnp.broadcast_to(field_ref[0:1, 128:256], (sources, 128))
    places, weights = [], []
    for pair in range(2):
        packed = slots_ref[pl.ds(pair, sources, stride=8), :].astype(jnp.int32)
        places += [packed & 1023, packed >> 10]
    predicted = jnp.zeros((sources, 128), F32)
    for k in range(4):
        lane = places[k] & 127
        picked = jnp.where(
            places[k] < 128,
            jnp.take_along_axis(field_low, lane, axis=1),
            jnp.take_along_axis(field_high, lane, axis=1),
        )
        weights.append(slots_ref[pl.ds(2 + k, sources, stride=8), :])
        predicted = predicted + weights[k] * picked
    innov = predicted - slots_ref[pl.ds(6, sources, stride=8), :]
    innov_ref[...] = innov
    for k in range(4):
        term_ref[k * sources : (k + 1) * sources, :] = weights[k] * innov
        place_ref[k * sources : (k + 1) * sources, :] = places[k]

    cell = lax.broadcasted_iota(jnp.int32, (OWN, 128), 0)

    def add_rows(step, total):
        for inner in range(8):
            at = step * 8 + inner
            hit = cell == place_ref[pl.ds(at, 1), :]
            total = total + jnp.where(hit, term_ref[pl.ds(at, 1), :], 0.0)
        return total

    total = lax.fori_loop(0, 4 * sources // 8, add_rows, jnp.zeros((OWN, 128), F32))
    adjoint = jnp.sum(total, axis=1, keepdims=True)
    adjoint_ref[...] = jnp.zeros_like(adjoint_ref)
    adjoint_ref[:, :OWN] = exact(jnp.ones((8, 128), F32), total, NT)

    def own_of(ref):
        blocks = [ref[own_slot(n) * SLOT : (own_slot(n) + 1) * SLOT, :].astype(F32)[:GROUP] for n in range(8)]
        return jnp.concatenate(blocks, axis=0)

    factor = 0.5 * loss_scale
    g_query = gq_ref[...].astype(BF16)
    up = up_ref[...]
    grad_low = mm(g_query, up, NT)
    up_query = mm((own_of(low_ref) * adjoint).astype(BF16), g_query, TN)
    down_query = mm((grad_low * adjoint).astype(BF16), own_of(norm_ref).astype(BF16), TN)

    weighted = [None] * 6
    for n in range(8):
        window = (n // 4) * 3 + (n % 4 + 1) // 2
        probs = probs_ref[n].astype(F32).reshape(HEADS, GROUP, 128)
        part = jnp.sum(probs * adjoint[n * GROUP : (n + 1) * GROUP].reshape(1, GROUP, 1), axis=1)
        weighted[window] = part if weighted[window] is None else weighted[window] + part
    weighted = jnp.concatenate(weighted, axis=1)
    head = lax.broadcasted_iota(jnp.int32, (HEADS, MODEL), 0)
    of_head = head == lax.broadcasted_iota(jnp.int32, (HEADS, MODEL), 1) // HEAD_DIM
    w_masked = jnp.where(of_head, jnp.broadcast_to(w_ref[0:1, :], (HEADS, MODEL)), 0.0)
    rank_head = exact(up.astype(F32), w_masked, NT)
    weighted_bf = weighted.astype(BF16)
    sums = mm(weighted_bf, low_ref[...])
    up_value = exact(sums, w_masked, TN)
    down_value = mm(exact(rank_head, weighted).astype(BF16), norm_ref[...])

    parts = (up_query[:8], up_value[8:], down_query[:8], down_value[8:])
    for m, part in enumerate(parts):
        part = part * factor
        for q in range(4):
            grads_ref[pl.ds(q * 32 + m, 8, stride=4), :] = part[:, 128 * q : 128 * (q + 1)]


def observe(slots, field, probs, gq, low, normed, w, up, loss_scale):
    sources = slots.shape[0] // 8
    shape = jax.ShapeDtypeStruct
    vmem = pl.BlockSpec(memory_space=pltpu.VMEM)
    return pl.pallas_call(
        functools.partial(observe_kernel, loss_scale=loss_scale),
        in_specs=[vmem] * 8,
        out_specs=[vmem] * 3,
        out_shape=[shape((sources, 128), F32), shape((8, 256), F32), shape((128, 128), F32)],
        scratch_shapes=[
            pltpu.VMEM((4 * sources, 128), F32),
            pltpu.VMEM((4 * sources, 128), jnp.int32),
        ],
        compiler_params=pltpu.CompilerParams(vmem_limit_bytes=32 * 1024 * 1024),
        cost_estimate=pl.CostEstimate(flops=10**8, bytes_accessed=4 * 10**6, transcendentals=0),
        name="observe",
    )(slots, field, probs, gq, low, normed, w, up)


def paired(value, axis, odd_first):
    count = lax.axis_size(axis)
    if odd_first:
        pairs = [(i, (i + 1) % count if i % 2 else (i - 1) % count) for i in range(count)]
    else:
        pairs = [(i, i ^ 1) for i in range(count)]
    return lax.ppermute(value, axis, pairs)


def shards(
    tokens,
    query_key_value_weight,
    output_weight,
    adapter_down_map,
    adapter_up_map,
    relative_position_bias,
    readout,
    observation_index,
    observation_weight,
    observation_value,
    observation_count,
):
    lat_count, lon_count = lax.axis_size("lat"), lax.axis_size("lon")
    lat, lon = lax.axis_index("lat"), lax.axis_index("lon")
    even_lat, even_lon = lat % 2 == 0, lon % 2 == 0

    own = tokens.reshape(4, 3, 2, 6, MODEL).transpose(2, 0, 1, 3, 4).reshape(2, 4, LIVE, MODEL)
    own = jnp.pad(own, ((0, 0), (0, 0), (0, GROUP - LIVE), (0, 0)))
    near_lon = paired(jnp.where(even_lon, own[1], own[0]), "lon", False)
    far_lon = paired(jnp.where(even_lon, own[0], own[1]), "lon", True)

    patch_row, patch_col = observation_index[0, 0] // 12, observation_index[0, 0] % 12
    place = ((patch_col // 6) * 4 + patch_row // 3) * GROUP + (patch_row % 3) * 6 + patch_col % 6
    live = jnp.arange(128, dtype=jnp.int32)[None, :] < observation_count[0, 0][:, None]
    slots = jnp.concatenate(
        [
            (place[:, 0::2] + 1024 * place[:, 1::2]).astype(F32),
            jnp.where(live[:, None, :], observation_weight[0, 0], 0.0),
            jnp.where(live[:, None, :], observation_value[0, 0][:, None, :], 0.0),
            jnp.zeros((lon_count, 1, 128), F32),
        ],
        axis=1,
    )
    slots = lax.all_to_all(slots, "lon", 0, 0, tiled=True).reshape(lon_count * 8, 128)

    left = jnp.where(even_lon, far_lon, near_lon)
    right = jnp.where(even_lon, near_lon, far_lon)
    top = jnp.stack([left[0], own[0, 0], own[1, 0], right[0]])
    bottom = jnp.stack([left[3], own[0, 3], own[1, 3], right[3]])
    near_lat = paired(jnp.where(even_lat, bottom, top), "lat", False)
    far_lat = paired(jnp.where(even_lat, top, bottom), "lat", True)

    flags = jnp.stack([lon % 2, lat % 2, (lat == 0).astype(jnp.int32), (lat == lat_count - 1).astype(jnp.int32)])
    down_rows = adapter_down_map.reshape(16, MODEL)
    up_rows = adapter_up_map.reshape(16, MODEL)
    block, field, probs, gq, low, normed, w = forward(
        flags.astype(jnp.int32),
        own,
        near_lon,
        far_lon,
        near_lat,
        far_lat,
        query_key_value_weight,
        output_weight,
        down_rows,
        up_rows,
        readout.reshape(1, MODEL),
        ordered_bias(relative_position_bias),
    )
    block = block.reshape(2, 4, GROUP, MODEL)[:, :, :LIVE].reshape(2, 4, 3, 6, MODEL)
    block_out = block.transpose(1, 2, 0, 3, 4).reshape(12, 12, MODEL)

    loss_scale = 1.0 / math.sqrt(lat_count * lon_count)
    innov, adjoint, grads = observe(slots, field, probs, gq, low, normed, w, up_rows, loss_scale)

    planes = [[i for i in range(lon_count) if (i // 2) % 2 == h] for h in range(2)]
    columns = [
        [a * lon_count + plane * 4 + h * 2 + c for h in range(2) for a in range(lat_count)]
        for plane in range(lon_count // 4)
        for c in range(2)
    ]
    chunks = lax.all_to_all(
        grads.reshape(32, 4, 128), "lon", 0, 0, axis_index_groups=planes, tiled=True
    )
    chunk = jnp.sum(chunks, axis=0).reshape(2, 1, 2, 128)
    adjoint_row = adjoint[0].reshape(1, 1, 2, 128)
    chunk = jnp.concatenate(
        [
            jnp.broadcast_to(chunk, (2, lat_count, 2, 128)),
            jnp.broadcast_to(adjoint_row, (2, lat_count, 2, 128)),
        ],
        axis=2,
    ).reshape(2 * lat_count, 4, 128)
    along = lax.all_to_all(chunk, ("lat", "lon"), 0, 0, axis_index_groups=columns, tiled=True)
    half = jnp.sum(along[:, :2], axis=0)
    below = lax.dynamic_index_in_dim(
        along, ((lon // 2) % 2) * lat_count + (lat + 1) % lat_count, 0, keepdims=False
    )[2:]
    below = below.reshape(256)[:OWN].reshape(2, 4, GROUP)
    here = adjoint[0, :OWN].reshape(2, 4, GROUP)
    moved = jnp.concatenate([here[:, 1:], below[:, :1]], axis=1)
    edge = jnp.pad(moved[0].reshape(1, 1, 4 * GROUP), ((0, 0), (0, 0), (0, 128 - 4 * GROUP)))
    last = jnp.concatenate(
        [
            jnp.broadcast_to(half[None], (lon_count, 2, 128)),
            innov[:, None, :],
            jnp.broadcast_to(edge, (lon_count, 1, 128)),
        ],
        axis=1,
    )
    final = lax.all_to_all(last, "lon", 0, 0, tiled=True)
    innovation = final[:, 2][None, None]
    beside = lax.dynamic_index_in_dim(final[:, 3], (lon + 1) % lon_count, 0, keepdims=False)
    beside = beside[: 4 * GROUP].reshape(4, GROUP)
    rolled = jnp.stack([moved[1], beside])[:, :, :LIVE].reshape(2, 4, 3, 6)
    rolled_adjoint = rolled.transpose(1, 2, 0, 3).reshape(12, 12)
    parts = final[:, :2].reshape(lon_count // 4, 2, 2, 2, 128)

    def whole(part):
        part = part.reshape(4, 8, 2, 128)
        return part.transpose(2, 1, 0, 3).reshape(2, 8, MODEL)

    return block_out, innovation, rolled_adjoint, whole(parts[:, 1]), whole(parts[:, 0])


def solution(mesh):
    return jax.shard_map(
        shards,
        mesh=mesh,
        in_specs=(
            P("lat", "lon", None),
            P(),
            P(),
            P(),
            P(),
            P(),
            P(),
            P("lat", "lon", None, None, None),
            P("lat", "lon", None, None, None),
            P("lat", "lon", None, None),
            P("lat", "lon", None),
        ),
        out_specs=(P("lat", "lon", None), P("lat", "lon", None, None), P("lat", "lon"), P(), P()),
        check_vma=False,
    )
```

time: 655 us -> 138 us (0.21)
  waiting for transfers between devices: 485 us -> 46.3 us
  starting transfers between devices: 105 us -> 58.3 us
  matrix products: 27.7 us -> 0 us
  Pallas kernels: 0 us -> 17.7 us
  between operations: 14.6 us -> 1.08 us
    psum x1 -> x0, waiting for transfers between devices: 437 us -> none  [shards(): lax.psum((down_map_gradient, up_map_gradient), ('lat', 'lon'))]
    all_to_all x5 -> x4, starting transfers between devices: 57.8 us -> 29.3 us  [the longest x1 9.18 us: shards(): lax.all_to_all(slots, 'lon', 0, 0, tiled=True).reshape(lon_count * 8, 128)]
    dot_general x28 -> x0, matrix products: 25.4 us -> none  [the longest x8 9.14 us: slot_block(): jnp.einsum('gksc,gks->gc', selector, terms, precision=lax.Precision.HIGHEST)]
    ppermute x6 -> x4, starting transfers between devices: 47.6 us -> 29 us  [paired(): return lax.ppermute(value, axis, pairs)]
    pallas_call x0 -> x3, Pallas kernels: none -> 17.7 us  [the longest x1 8.98 us: forward(): pl.pallas_call(forward_kernel, in_specs=[pl.BlockSpec(memory_space=pltpu....]
    ppermute x6 -> x4, waiting for transfers between devices: 13.4 us -> 11 us  [paired(): return lax.ppermute(value, axis, pairs)]
    all_to_all x5 -> x4, waiting for transfers between devices: 34.5 us -> 35.3 us  [the longest x1 16.7 us: shards(): final = lax.all_to_all(last, 'lon', 0, 0, tiled=True)]
  transfers between devices with their start and end apart: 12 -> 8, of which waited for: 8 -> 5; matrix products, arithmetic and copies ran while one was open for 3% -> 3% of each run, Pallas kernels for 0% -> 9%
where the time goes in v1:
time: 138 us; the launch traced here: 137 us
  starting transfers between devices  58.3 us (42%)
  waiting for transfers between devices  46.3 us (34%)
  Pallas kernels  17.7 us (13%)
  local copies, waits for them, and re-layouts  9.8 us (7%)
  other arithmetic  3.5 us (3%)
    ppermute x4, starting transfers between devices, paired(): return lax.ppermute(value, axis, pairs)  29 us
    all_to_all x1, waiting for transfers between devices, shards(): final = lax.all_to_all(last, 'lon', 0, 0, tiled=True)  16.7 us
    all_to_all x1, waiting for transfers between devices, shards(): lax.all_to_all(chunk, ('lat', 'lon'), 0, 0, axis_index_groups=columns, ti...  11.3 us
    ppermute x4, waiting for transfers between devices, paired(): return lax.ppermute(value, axis, pairs)  11 us
    all_to_all x1, starting transfers between devices, shards(): lax.all_to_all(slots, 'lon', 0, 0, tiled=True).reshape(lon_count * 8, 128)  9.18 us
    pallas_call x1, Pallas kernels, forward(): pl.pallas_call(forward_kernel, in_specs=[pl.BlockSpec(memory_space=pltpu....  8.98 us
    all_to_all x1, starting transfers between devices, shards(): lax.all_to_all(grads.reshape(32, 4, 128), 'lon', 0, 0, axis_index_groups=...  7.64 us
    all_to_all x1, waiting for transfers between devices, shards(): lax.all_to_all(grads.reshape(32, 4, 128), 'lon', 0, 0, axis_index_groups=...  7.31 us
  transfers between devices with their start and end apart: 8, of which 5 were waited for; matrix products, arithmetic and copies ran while one was open for 3% of the time, Pallas kernels for 9%

profile of v1, /device:TPU:1, one launch (start us, length us, event | category | flops | bytes accessed | tf_op | source)
XLA Modules:
  0.0 136.7 jit_solution(12545333454899022496)
XLA Ops:
  0.7 1.1 reshape.157
  1.8 0.1 copy.65
  1.9 0.0 copy-start.9
  2.0 8.8 %collective-permute-start = (bf16[4,24,512]{2,1,0:T(8,128)(2,1)S(1)}, bf16[4,24,512]{2,1,0:T(8,128)(2,1)S(1)}, u32[]{:S(2)}, u32[]{:S(2)}) collective-permute-start(bf16[4,24,512]{2,1,0:T(8,128)(2,1)S(1)} %get-tuple-element.34), channel_id=1, source_target_pairs={{0,1},{1,0},{2,3},{3,2},{4,5},{5,4},{6,7},{7,6},{8,9},{9,8},{10,11... | collective-permute-start | bytes 294920 | tf_op jit(solution)/shard_map/ppermute | solution.py:329
  10.8 10.0 %collective-permute-start.1 = (bf16[4,24,512]{2,1,0:T(8,128)(2,1)S(1)}, bf16[4,24,512]{2,1,0:T(8,128)(2,1)S(1)}, u32[]{:S(2)}, u32[]{:S(2)}) collective-permute-start(bf16[4,24,512]{2,1,0:T(8,128)(2,1)S(1)} %get-tuple-element.33), channel_id=1, source_target_pairs={{0,63},{1,2},{2,1},{3,4},{4,3},{5,6},{6,5},{7,8},{8,7},{9,10},{10,... | collective-permute-start | bytes 294920 | tf_op jit(solution)/shard_map/ppermute | solution.py:329
  20.8 0.0 copy-done.5
  20.8 0.8 fusion.3
  21.6 0.4 slice.102
  22.0 0.4 slice.103
  22.5 0.1 iota_compare_fusion.1
  22.6 0.1 bitcast_select_fusion.1
  22.8 0.8 pad_maximum_fusion
  23.6 9.2 %all-to-all-start = ((f32[64,8,128]{2,1,0:T(8,128)}), f32[64,8,128]{2,1,0:T(8,128)S(1)}, u32[]{:S(2)}, u32[]{:S(2)}) async-start(f32[64,8,128]{2,1,0:T(8,128)} %pad_maximum_fusion), calls=%async_computation | async-start | bytes 524288 | tf_op jit(solution)/shard_map/all_to_all | solution.py:366
  32.8 0.0 copy-start.1
  32.8 0.0 copy-start.4
  32.9 2.7 %ordered_bias.1.bias_ref = f32[4,16,24,128]{3,2,1,0:T(8,128)} custom-call(f32[1152,72]{1,0:T(8,128)} %bitcast.92), custom_call_target="tpu_custom_call" | custom-call | flops 200000000 | bytes 2000000 | tf_op jit(solution)/shard_map/ordered_bias/pallas_call | solution.py:60
  35.6 0.0 collective-permute-done.near_lon_ref
  35.6 0.0 collective-permute-done.1.far_lon_ref
  35.6 2.7 %collective-permute-start.2 = (bf16[4,24,512]{2,1,0:T(8,128)(2,1)S(1)}, bf16[4,24,512]{2,1,0:T(8,128)(2,1)S(1)}, u32[]{:S(2)}, u32[]{:S(2)}) collective-permute-start(bf16[4,24,512]{2,1,0:T(8,128)(2,1)S(1)} %get-tuple-element.26), channel_id=1, source_target_pairs={{0,64},{64,0},{128,192},{192,128},{256,320},{320,256},{384,448},{4... | collective-permute-start | bytes 294920 | tf_op jit(solution)/shard_map/ppermute | solution.py:329
  38.3 7.6 %collective-permute-start.3 = (bf16[4,24,512]{2,1,0:T(8,128)(2,1)S(1)}, bf16[4,24,512]{2,1,0:T(8,128)(2,1)S(1)}, u32[]{:S(2)}, u32[]{:S(2)}) collective-permute-start(bf16[4,24,512]{2,1,0:T(8,128)(2,1)S(1)} %get-tuple-element.25), channel_id=1, source_target_pairs={{0,448},{64,128},{128,64},{192,256},{256,192},{320,384},{384,320},... | collective-permute-start | bytes 294920 | tf_op jit(solution)/shard_map/ppermute | solution.py:329
  45.9 0.1 pad_add_fusion.flags_ref
  46.0 1.4 %collective-permute-done.2.near_lat_ref = bf16[4,24,512]{2,1,0:T(8,128)(2,1)S(1)} collective-permute-done((bf16[4,24,512]{2,1,0:T(8,128)(2,1)S(1)}, bf16[4,24,512]{2,1,0:T(8,128)(2,1)S(1)}, u32[]{:S(2)}, u32[]{:S(2)}) %collective-permute-start.2) | collective-permute-done | bytes 98336 | tf_op jit(solution)/shard_map/ppermute | solution.py:329
  47.4 9.6 %collective-permute-done.3.far_lat_ref = bf16[4,24,512]{2,1,0:T(8,128)(2,1)S(1)} collective-permute-done((bf16[4,24,512]{2,1,0:T(8,128)(2,1)S(1)}, bf16[4,24,512]{2,1,0:T(8,128)(2,1)S(1)}, u32[]{:S(2)}, u32[]{:S(2)}) %collective-permute-start.3) | collective-permute-done | bytes 98336 | tf_op jit(solution)/shard_map/ppermute | solution.py:329
  57.0 1.1 copy-done
  58.1 1.4 %copy-done.2 = bf16[512,1536]{1,0:T(8,128)(2,1)S(1)} copy-done((bf16[512,1536]{1,0:T(8,128)(2,1)S(1)}, bf16[512,1536]{1,0:T(8,128)(2,1)}, u32[]{:S(2)}) %copy-start.2) | copy-done | bytes 1572888
  59.5 1.0 copy-done.3
  60.6 9.0 %window_forward.1 = (bf16[192,512]{1,0:T(8,128)(2,1)S(1)}, f32[8,256]{1,0:T(8,128)S(1)}, bf16[8,384,128]{2,1,0:T(8,128)(2,1)S(1)}, f32[192,512]{1,0:T(8,128)S(1)...) custom-call(s32[4]{0:T(128)S(1)} %pad_add_fusion.flags_ref, ...), custom_call_target="tpu_custom_call" | custom-call | flops 3000000000 | bytes 8000000 | tf_op jit(solution)/shard_map/window_forward/pallas_call | solution.py:190
  69.6 0.0 all-to-all-done
  69.6 6.0 %observe.1 = (f32[64,128]{1,0:T(8,128)S(1)}, f32[8,256]{1,0:T(8,128)S(1)}, f32[128,128]{1,0:T(8,128)}) custom-call(f32[512,128]{1,0:T(8,128)S(1)} %bitcast.85, f32[8,256]{1,0:T(8,128)S(1)} %get-tuple-element.16.field_ref, bf16[8,384,128]{2,1,0:T(8,128)(2,1)S(1)} %get-tuple-element.17.probs_ref, f32[192,512]{1,0:T(8,128)S(1)} %get-tuple-element.18.gq_ref, ...), custom_call_target="tpu_custom_call" | custom-call | flops 100000000 | bytes 4000000 | tf_op jit(solution)/shard_map/observe/pallas_call | solution.py:308
  75.6 7.6 %all-to-all-start.1 = ((f32[32,4,128]{2,1,0:T(4,128)}), f32[32,4,128]{2,1,0:T(4,128)S(1)}, u32[]{:S(2)}, u32[]{:S(2)}) async-start(f32[32,4,128]{2,1,0:T(4,128)} %bitcast.27), calls=%async_computation.1 | async-start | bytes 131072 | tf_op jit(solution)/shard_map/all_to_all | solution.py:404
  83.3 7.3 %all-to-all-done.1 = f32[32,4,128]{2,1,0:T(4,128)S(1)} async-done(((f32[32,4,128]{2,1,0:T(4,128)}), f32[32,4,128]{2,1,0:T(4,128)S(1)}, u32[]{:S(2)}, u32[]{:S(2)}) %all-to-all-start.1) | async-done | bytes 65568 | tf_op jit(solution)/shard_map/all_to_all | solution.py:404
  90.6 0.6 pad_maximum_fusion.4
  91.3 6.5 %all-to-all-start.2 = ((f32[16,4,128]{2,1,0:T(4,128)}), f32[16,4,128]{2,1,0:T(4,128)S(1)}, u32[]{:S(2)}, u32[]{:S(2)}) async-start(f32[16,4,128]{2,1,0:T(4,128)} %bitcast.30), calls=%async_computation.2 | async-start | bytes 65536 | tf_op jit(solution)/shard_map/all_to_all | solution.py:416
  97.8 0.1 reshape_squeeze.13
  97.9 11.3 %all-to-all-done.2 = f32[16,4,128]{2,1,0:T(4,128)S(1)} async-done(((f32[16,4,128]{2,1,0:T(4,128)}), f32[16,4,128]{2,1,0:T(4,128)S(1)}, u32[]{:S(2)}, u32[]{:S(2)}) %all-to-all-start.2) | async-done | bytes 32800 | tf_op jit(solution)/shard_map/all_to_all | solution.py:416
  109.2 0.1 reshape.170
  109.3 0.1 reshape_squeeze.14
  109.5 0.7 pad_maximum_fusion.1
  110.3 6.0 %all-to-all-start.3 = ((f32[64,4,128]{2,1,0:T(4,128)}), f32[64,4,128]{2,1,0:T(4,128)S(1)}, u32[]{:S(2)}, u32[]{:S(2)}) async-start(f32[64,4,128]{2,1,0:T(4,128)} %pad_maximum_fusion.1), calls=%async_computation.3 | async-start | bytes 262144 | tf_op jit(solution)/shard_map/all_to_all | solution.py:433
  116.3 0.1 copy.77
  116.5 0.7 reshape.165
  117.2 16.7 %all-to-all-done.3 = f32[64,4,128]{2,1,0:T(4,128)S(1)} async-done(((f32[64,4,128]{2,1,0:T(4,128)}), f32[64,4,128]{2,1,0:T(4,128)S(1)}, u32[]{:S(2)}, u32[]{:S(2)}) %all-to-all-start.3) | async-done | bytes 131104 | tf_op jit(solution)/shard_map/all_to_all | solution.py:433
  133.9 0.6 copy.80
  134.5 0.6 copy.81
  135.1 0.7 fusion.10
  135.8 0.1 stack_reshape.3
  135.9 0.1 reshape.171
  136.0 0.7 reshape.172
  (45 shorter events, 0.6 us)
Async XLA Ops:
  0.6 20.1 %copy-start.5 = (s32[1,1,64,4,128]{4,3,2,1,0:T(4,128)S(1)}, s32[1,1,64,4,128]{4,3,2,1,0:T(4,128)}, u32[]{:S(2)}) copy-start(s32[1,1,64,4,128]{4,3,2,1,0:T(4,128)} %param.18) | copy-start | bytes 393220
  0.6 21.8 %copy-start.8 = (s32[1,1,64]{2,1,0:T(1,128)S(1)}, s32[1,1,64]{2,1,0:T(1,128)}, u32[]{:S(2)}) copy-start(s32[1,1,64]{2,1,0:T(1,128)} %param.21) | copy-start | bytes 772
  0.7 21.9 %copy-start.7 = (f32[1,1,64,128]{3,2,1,0:T(8,128)S(1)}, f32[1,1,64,128]{3,2,1,0:T(8,128)}, u32[]{:S(2)}) copy-start(f32[1,1,64,128]{3,2,1,0:T(8,128)} %param.20) | copy-start | bytes 98308
  0.7 22.0 %copy-start.6 = (f32[1,1,64,4,128]{4,3,2,1,0:T(4,128)S(1)}, f32[1,1,64,4,128]{4,3,2,1,0:T(4,128)}, u32[]{:S(2)}) copy-start(f32[1,1,64,4,128]{4,3,2,1,0:T(4,128)} %param.19) | copy-start | bytes 393220
  1.9 30.9 %copy-start.9 = (bf16[512]{0:T(512)(128)(2,1)S(1)}, bf16[512]{0:T(512)(128)(2,1)}, u32[]{:S(2)}) copy-start(bf16[512]{0:T(512)(128)(2,1)} %param.17) | copy-start | bytes 3076
  2.0 33.6 %collective-permute-start = (bf16[4,24,512]{2,1,0:T(8,128)(2,1)S(1)}, bf16[4,24,512]{2,1,0:T(8,128)(2,1)S(1)}, u32[]{:S(2)}, u32[]{:S(2)}) collective-permute-start(bf16[4,24,512]{2,1,0:T(8,128)(2,1)S(1)} %get-tuple-element.34), channel_id=1, source_target_pairs={{0,1},{1,0},{2,3},{3,2},{4,5},{5,4},{6,7},{7,6},{8,9},{9,8},{10,11... | collective-permute-start | bytes 294920 | tf_op jit(solution)/shard_map/ppermute | solution.py:329
  10.8 24.8 %collective-permute-start.1 = (bf16[4,24,512]{2,1,0:T(8,128)(2,1)S(1)}, bf16[4,24,512]{2,1,0:T(8,128)(2,1)S(1)}, u32[]{:S(2)}, u32[]{:S(2)}) collective-permute-start(bf16[4,24,512]{2,1,0:T(8,128)(2,1)S(1)} %get-tuple-element.33), channel_id=1, source_target_pairs={{0,63},{1,2},{2,1},{3,4},{4,3},{5,6},{6,5},{7,8},{8,7},{9,10},{10,... | collective-permute-start | bytes 294920 | tf_op jit(solution)/shard_map/ppermute | solution.py:329
  23.6 46.0 %all-to-all-start = ((f32[64,8,128]{2,1,0:T(8,128)}), f32[64,8,128]{2,1,0:T(8,128)S(1)}, u32[]{:S(2)}, u32[]{:S(2)}) async-start(f32[64,8,128]{2,1,0:T(8,128)} %pad_maximum_fusion), calls=%async_computation | async-start | bytes 524288 | tf_op jit(solution)/shard_map/all_to_all | solution.py:366
  32.8 24.2 %copy-start.1 = (bf16[2,8,512]{2,1,0:T(8,128)(2,1)S(1)}, bf16[2,8,512]{2,1,0:T(8,128)(2,1)}, u32[]{:S(2)}) copy-start(bf16[2,8,512]{2,1,0:T(8,128)(2,1)} %param.15) | copy-start | bytes 49156
  32.8 24.2 %copy-start.4 = (bf16[2,8,512]{2,1,0:T(8,128)(2,1)S(1)}, bf16[2,8,512]{2,1,0:T(8,128)(2,1)}, u32[]{:S(2)}) copy-start(bf16[2,8,512]{2,1,0:T(8,128)(2,1)} %param.14) | copy-start | bytes 49156
  35.6 11.7 %collective-permute-start.2 = (bf16[4,24,512]{2,1,0:T(8,128)(2,1)S(1)}, bf16[4,24,512]{2,1,0:T(8,128)(2,1)S(1)}, u32[]{:S(2)}, u32[]{:S(2)}) collective-permute-start(bf16[4,24,512]{2,1,0:T(8,128)(2,1)S(1)} %get-tuple-element.26), channel_id=1, source_target_pairs={{0,64},{64,0},{128,192},{192,128},{256,320},{320,256},{384,448},{4... | collective-permute-start | bytes 294920 | tf_op jit(solution)/shard_map/ppermute | solution.py:329
  38.3 18.7 %collective-permute-start.3 = (bf16[4,24,512]{2,1,0:T(8,128)(2,1)S(1)}, bf16[4,24,512]{2,1,0:T(8,128)(2,1)S(1)}, u32[]{:S(2)}, u32[]{:S(2)}) collective-permute-start(bf16[4,24,512]{2,1,0:T(8,128)(2,1)S(1)} %get-tuple-element.25), channel_id=1, source_target_pairs={{0,448},{64,128},{128,64},{192,256},{256,192},{320,384},{384,320},... | collective-permute-start | bytes 294920 | tf_op jit(solution)/shard_map/ppermute | solution.py:329
  57.0 1.1 copy-start
  58.1 1.4 %copy-start.2 = (bf16[512,1536]{1,0:T(8,128)(2,1)S(1)}, bf16[512,1536]{1,0:T(8,128)(2,1)}, u32[]{:S(2)}) copy-start(bf16[512,1536]{1,0:T(8,128)(2,1)} %qkv_ref.1) | copy-start | bytes 4718596
  59.5 1.0 copy-start.3
  75.6 15.0 %all-to-all-start.1 = ((f32[32,4,128]{2,1,0:T(4,128)}), f32[32,4,128]{2,1,0:T(4,128)S(1)}, u32[]{:S(2)}, u32[]{:S(2)}) async-start(f32[32,4,128]{2,1,0:T(4,128)} %bitcast.27), calls=%async_computation.1 | async-start | bytes 131072 | tf_op jit(solution)/shard_map/all_to_all | solution.py:404
  91.3 18.0 %all-to-all-start.2 = ((f32[16,4,128]{2,1,0:T(4,128)}), f32[16,4,128]{2,1,0:T(4,128)S(1)}, u32[]{:S(2)}, u32[]{:S(2)}) async-start(f32[16,4,128]{2,1,0:T(4,128)} %bitcast.30), calls=%async_computation.2 | async-start | bytes 65536 | tf_op jit(solution)/shard_map/all_to_all | solution.py:416
  110.3 23.6 %all-to-all-start.3 = ((f32[64,4,128]{2,1,0:T(4,128)}), f32[64,4,128]{2,1,0:T(4,128)S(1)}, u32[]{:S(2)}, u32[]{:S(2)}) async-start(f32[64,4,128]{2,1,0:T(4,128)} %pad_maximum_fusion.1), calls=%async_computation.3 | async-start | bytes 262144 | tf_op jit(solution)/shard_map/all_to_all | solution.py:433

commit v2 on v1

--- a/solution.py
+++ b/solution.py
@@ -66,19 +66,19 @@
     )(bias.reshape(HEADS * 72, 72))
 
 
-def forward_kernel(
+def forward_part(
     flags_ref,
     own_ref,
     near_lon_ref,
     far_lon_ref,
     near_lat_ref,
     far_lat_ref,
-    qkv_ref,
-    wo_ref,
+    qkv_hbm,
+    wo_hbm,
     down_ref,
     up_ref,
     readout_ref,
-    bias_ref,
+    bias_hbm,
     block_ref,
     field_ref,
     probs_ref,
@@ -90,7 +90,19 @@
     v_ref,
     q_ref,
     att_ref,
+    qkv_ref,
+    wo_ref,
+    bias_ref,
+    copy_sems,
 ):
+    loads = [
+        pltpu.make_async_copy(source, target, copy_sems.at[i])
+        for i, (source, target) in enumerate(
+            ((qkv_hbm, qkv_ref), (bias_hbm, bias_ref), (wo_hbm, wo_ref))
+        )
+    ]
+    for load in loads:
+        load.start()
     even_lon = flags_ref[0] == 0
     even_lat = flags_ref[1] == 0
     first = flags_ref[2].astype(F32)
@@ -119,6 +131,8 @@
             norm_ref[slot * SLOT : (slot + 1) * SLOT, :] = y
 
     normed = norm_ref[...]
+    for load in loads:
+        load.wait()
     rank_row = lax.broadcasted_iota(jnp.int32, (16, MODEL), 0)
     up_half = 0.5 * up_ref[...].astype(F32)
     up_query = jnp.where(rank_row < 8, up_half, 0.0).astype(BF16)
@@ -184,37 +198,8 @@
     field_ref[:, :OWN] = mm(readout, out, NT)
 
 
-def forward(flags, own, near_lon, far_lon, near_lat, far_lat, qkv, wo, down, up, readout, bias):
-    shape = jax.ShapeDtypeStruct
-    vmem = pl.BlockSpec(memory_space=pltpu.VMEM)
-    return pl.pallas_call(
-        forward_kernel,
-        in_specs=[pl.BlockSpec(memory_space=pltpu.SMEM)] + [vmem] * 11,
-        out_specs=[vmem] * 7,
-        out_shape=[
-            shape((OWN, MODEL), BF16),
-            shape((8, 256), F32),
-            shape((8, HEADS * GROUP, 128), BF16),
-            shape((OWN, MODEL), F32),
-            shape((24 * SLOT, 16), BF16),
-            shape((24 * SLOT, MODEL), BF16),
-            shape((8, MODEL), F32),
-        ],
-        scratch_shapes=[
-            pltpu.VMEM((24 * SLOT, MODEL), BF16),
-            pltpu.VMEM((24 * SLOT, MODEL), BF16),
-            pltpu.VMEM((8 * SLOT, MODEL), F32),
-            pltpu.VMEM((OWN, MODEL), F32),
-        ],
-        compiler_params=pltpu.CompilerParams(vmem_limit_bytes=40 * 1024 * 1024),
-        cost_estimate=pl.CostEstimate(
-            flops=3 * 10**9, bytes_accessed=8 * 10**6, transcendentals=4 * 10**5
-        ),
-        name="window_forward",
-    )(flags, own, near_lon, far_lon, near_lat, far_lat, qkv, wo, down, up, readout, bias)
-
-
-def observe_kernel(
+def observe_part(
+    flags_ref,
     slots_ref,
     field_ref,
     probs_ref,
@@ -223,9 +208,9 @@
     norm_ref,
     w_ref,
     up_ref,
+    adjoint_ref,
+    sends_ref,
     innov_ref,
-    adjoint_ref,
-    grads_ref,
     term_ref,
     place_ref,
     loss_scale,
@@ -294,30 +279,276 @@
     up_value = exact(sums, w_masked, TN)
     down_value = mm(exact(rank_head, weighted).astype(BF16), norm_ref[...])
 
+    sends_ref[...] = jnp.zeros_like(sends_ref)
     parts = (up_query[:8], up_value[8:], down_query[:8], down_value[8:])
     for m, part in enumerate(parts):
         part = part * factor
         for q in range(4):
-            grads_ref[pl.ds(q * 32 + m, 8, stride=4), :] = part[:, 128 * q : 128 * (q + 1)]
-
-
-def observe(slots, field, probs, gq, low, normed, w, up, loss_scale):
+            sends_ref[pl.ds(q * 64 + m, 8, stride=8), :] = part[:, 128 * q : 128 * (q + 1)]
+    low_plane = flags_ref[4] == 0
+    for core in range(2):
+        planes = [innov_ref[pl.ds(2 * h + core, sources // 4, stride=4), :] for h in range(2)]
+        mine = jnp.where(low_plane, planes[0], planes[1])
+        other = jnp.where(low_plane, planes[1], planes[0])
+        sends_ref[pl.ds(8 * core + 4, sources // 4, stride=16), :] = mine
+        sends_ref[pl.ds(8 * core + 5, sources // 4, stride=16), :] = other
+
+
+def core_kernel(
+    flags_ref,
+    own_ref,
+    near_lon_ref,
+    far_lon_ref,
+    near_lat_ref,
+    far_lat_ref,
+    qkv_hbm,
+    wo_hbm,
+    down_ref,
+    up_ref,
+    readout_ref,
+    bias_hbm,
+    slots_hbm,
+    block_ref,
+    adjoint_ref,
+    sends_ref,
+    field_ref,
+    probs_ref,
+    gq_ref,
+    low_ref,
+    norm_ref,
+    w_ref,
+    k_ref,
+    v_ref,
+    q_ref,
+    att_ref,
+    qkv_ref,
+    wo_ref,
+    bias_ref,
+    copy_sems,
+    innov_ref,
+    term_ref,
+    place_ref,
+    slots_ref,
+    loss_scale,
+):
+    slot_load = pltpu.make_async_copy(slots_hbm, slots_ref, copy_sems.at[3])
+    slot_load.start()
+    forward_part(
+        flags_ref,
+        own_ref,
+        near_lon_ref,
+        far_lon_ref,
+        near_lat_ref,
+        far_lat_ref,
+        qkv_hbm,
+        wo_hbm,
+        down_ref,
+        up_ref,
+        readout_ref,
+        bias_hbm,
+        block_ref,
+        field_ref,
+        probs_ref,
+        gq_ref,
+        low_ref,
+        norm_ref,
+        w_ref,
+        k_ref,
+        v_ref,
+        q_ref,
+        att_ref,
+        qkv_ref,
+        wo_ref,
+        bias_ref,
+        copy_sems,
+    )
+    slot_load.wait()
+    observe_part(
+        flags_ref,
+        slots_ref,
+        field_ref,
+        probs_ref,
+        gq_ref,
+        low_ref,
+        norm_ref,
+        w_ref,
+        up_ref,
+        adjoint_ref,
+        sends_ref,
+        innov_ref,
+        term_ref,
+        place_ref,
+        loss_scale,
+    )
+
+
+def core(flags, own, halos, qkv, wo, down, up, readout, bias, slots, loss_scale):
     sources = slots.shape[0] // 8
+    shape = jax.ShapeDtypeStruct
+    vmem, far = pl.BlockSpec(memory_space=pltpu.VMEM), pl.BlockSpec(memory_space=pl.ANY)
+    smem = pl.BlockSpec(memory_space=pltpu.SMEM)
+    return pl.pallas_call(
+        functools.partial(core_kernel, loss_scale=loss_scale),
+        in_specs=[smem] + [vmem] * 5 + [far] * 2 + [vmem] * 3 + [far] * 2,
+        out_specs=[vmem] * 3,
+        out_shape=[
+            shape((OWN, MODEL), BF16),
+            shape((8, 256), F32),
+            shape((sources // 2 * 8, 128), F32),
+        ],
+        scratch_shapes=[
+            pltpu.VMEM((8, 256), F32),
+            pltpu.VMEM((8, HEADS * GROUP, 128), BF16),
+            pltpu.VMEM((OWN, MODEL), F32),
+            pltpu.VMEM((24 * SLOT, 16), BF16),
+            pltpu.VMEM((24 * SLOT, MODEL), BF16),
+            pltpu.VMEM((8, MODEL), F32),
+            pltpu.VMEM((24 * SLOT, MODEL), BF16),
+            pltpu.VMEM((24 * SLOT, MODEL), BF16),
+            pltpu.VMEM((8 * SLOT, MODEL), F32),
+            pltpu.VMEM((OWN, MODEL), F32),
+            pltpu.VMEM((MODEL, 3 * MODEL), BF16),
+            pltpu.VMEM((MODEL, MODEL), BF16),
+            pltpu.VMEM((4, HEADS, GROUP, 128), F32),
+            pltpu.SemaphoreType.DMA((4,)),
+            pltpu.VMEM((sources, 128), F32),
+            pltpu.VMEM((4 * sources, 128), F32),
+            pltpu.VMEM((4 * sources, 128), jnp.int32),
+            pltpu.VMEM((sources * 8, 128), F32),
+        ],
+        compiler_params=pltpu.CompilerParams(vmem_limit_bytes=58 * 1024 * 1024),
+        cost_estimate=pl.CostEstimate(
+            flops=3 * 10**9, bytes_accessed=8 * 10**6, transcendentals=4 * 10**5
+        ),
+        name="window_and_observe",
+    )(flags, own, *halos, qkv, wo, down, up, readout, bias, slots)
+
+
+BLOCK = 48
+
+
+def scatter_kernel(chunks_ref, adjoint_ref, out_ref, rows_ref):
+    total = jnp.sum(chunks_ref[...].reshape(-1, 8, 128), axis=0)
+    rows_ref[...] = jnp.zeros_like(rows_ref)
+    for at, values in ((0, total[0:4]), (8, None)):
+        if values is None:
+            values = jnp.concatenate([adjoint_ref[0:1, :128], adjoint_ref[0:1, 128:]], axis=0)
+        high = values.astype(BF16).astype(F32)
+        count = values.shape[0]
+        rows_ref[at : at + count, :] = high
+        rows_ref[at + count : at + 2 * count, :] = values - high
+    head = rows_ref[...].astype(BF16)
+    members = chunks_ref.shape[0] // 8
+    other = chunks_ref[pl.ds(5, members, stride=8), :].astype(BF16)
+    for at in range(out_ref.shape[0] // BLOCK):
+        out_ref[at * BLOCK : at * BLOCK + 16, :] = head
+        out_ref[at * BLOCK + 16 : (at + 1) * BLOCK, :] = other
+
+
+def scatter(chunks, adjoint, members):
+    vmem = pl.BlockSpec(memory_space=pltpu.VMEM)
+    return pl.pallas_call(
+        scatter_kernel,
+        in_specs=[vmem] * 2,
+        out_specs=vmem,
+        out_shape=jax.ShapeDtypeStruct((members * BLOCK, 128), BF16),
+        scratch_shapes=[pltpu.VMEM((16, 128), F32)],
+        name="scatter_rows",
+    )(chunks, adjoint)
+
+
+def gather_kernel(flags_ref, along_ref, chunks_ref, adjoint_ref, out_ref, innov_ref, moved_ref):
+    lat_count = along_ref.shape[0] // BLOCK // 2
+    plane, lat = flags_ref[4], flags_ref[5]
+    next_lat = jnp.where(lat == lat_count - 1, 0, lat + 1)
+
+    def rows_of(h, a):
+        start = pl.multiple_of((h * lat_count + a) * BLOCK, 16)
+        return along_ref[pl.ds(start, 16), :].astype(F32)
+
+    def adjoint_of(rows):
+        values = rows[8:10] + rows[10:12]
+        return jnp.concatenate([values[0:1], values[1:2]], axis=1)
+
+    lane = lax.broadcasted_iota(jnp.int32, (1, 256), 1)
+
+    def shift_rows(here, below):
+        kept = pltpu.roll(here, 256 - GROUP, 1)
+        new = pltpu.roll(below, 3 * GROUP, 1)
+        return jnp.where(lane % (4 * GROUP) < 3 * GROUP, kept, new)
+
+    moved = shift_rows(adjoint_ref[0:1, :], adjoint_of(rows_of(plane, next_lat)))
+    twin = shift_rows(
+        adjoint_of(rows_of(1 - plane, lat)), adjoint_of(rows_of(1 - plane, next_lat))
+    )
+    moved_ref[...] = jnp.broadcast_to(moved, (8, 256))
+
+    total = jnp.zeros((16, 128), F32)
+    for at in range(2 * lat_count):
+        total = total + along_ref[at * BLOCK : at * BLOCK + 16, :].astype(F32)
+    total = total[0:4] + total[4:8]
+    block = jnp.concatenate([total, moved[:, :128], twin[:, :128], jnp.zeros((2, 128), F32)], axis=0)
+    members = out_ref.shape[0] // 8
+    for at in range(members):
+        out_ref[at * 8 : at * 8 + 8, :] = block
+
+    near = chunks_ref[pl.ds(4, members, stride=8), :]
+    start = pl.multiple_of(((1 - plane) * lat_count + lat) * BLOCK + 16, 16)
+    far = along_ref[pl.ds(start, members), :].astype(F32)
+    low_plane = plane == 0
+    planes = (jnp.where(low_plane, near, far), jnp.where(low_plane, far, near))
+    for h in range(2):
+        for m in range(members // 2):
+            innov_ref[4 * m + 2 * h : 4 * m + 2 * h + 2, :] = planes[h][2 * m : 2 * m + 2]
+
+
+def gather(flags, along, chunks, adjoint):
+    members = chunks.shape[0] // 8
     shape = jax.ShapeDtypeStruct
     vmem = pl.BlockSpec(memory_space=pltpu.VMEM)
     return pl.pallas_call(
-        functools.partial(observe_kernel, loss_scale=loss_scale),
-        in_specs=[vmem] * 8,
+        gather_kernel,
+        in_specs=[pl.BlockSpec(memory_space=pltpu.SMEM)] + [vmem] * 3,
         out_specs=[vmem] * 3,
-        out_shape=[shape((sources, 128), F32), shape((8, 256), F32), shape((128, 128), F32)],
-        scratch_shapes=[
-            pltpu.VMEM((4 * sources, 128), F32),
-            pltpu.VMEM((4 * sources, 128), jnp.int32),
-        ],
-        compiler_params=pltpu.CompilerParams(vmem_limit_bytes=32 * 1024 * 1024),
-        cost_estimate=pl.CostEstimate(flops=10**8, bytes_accessed=4 * 10**6, transcendentals=0),
-        name="observe",
-    )(slots, field, probs, gq, low, normed, w, up)
+        out_shape=[shape((members * 8, 128), F32), shape((2 * members, 128), F32), shape((8, 256), F32)],
+        name="gather_rows",
+    )(flags, along, chunks, adjoint)
+
+
+def finish_kernel(flags_ref, final_ref, moved_ref, up_ref, down_ref, rolled_ref):
+    for m, (ref, which) in enumerate(((up_ref, 0), (up_ref, 1), (down_ref, 0), (down_ref, 1))):
+        for q in range(4):
+            ref[which, :, 128 * q : 128 * (q + 1)] = final_ref[pl.ds(q * 64 + m, 8, stride=8), :]
+    members = final_ref.shape[0] // 8
+    plane, member = flags_ref[4], flags_ref[6]
+    across = member - 1 + 2 * plane
+    across = jnp.where(across >= members, 0, across)
+    row = jnp.where(flags_ref[0] == 0, (member + 1) * 8 + 4, across * 8 + 5)
+    beside = final_ref[pl.ds(row, 1), :]
+    moved = pltpu.roll(moved_ref[0:1, :], 256 - 4 * GROUP, 1)[:, :128]
+    lane = lax.broadcasted_iota(jnp.int32, (16, 128), 1)
+    out_row = lax.broadcasted_iota(jnp.int32, (16, 128), 0)
+    in_group = lane % GROUP
+    belongs = (lane // GROUP * 3 + in_group // 6 == out_row) & (in_group < LIVE) & (lane < 4 * GROUP)
+    from_lane = lax.broadcasted_iota(jnp.int32, (128, 128), 0)
+    to_lane = lax.broadcasted_iota(jnp.int32, (128, 128), 1)
+    out = jnp.zeros((16, 128), F32)
+    for half, values in enumerate((moved, beside)):
+        place = (from_lane % GROUP % 6 + 6 * half == to_lane).astype(F32)
+        out = out + exact(jnp.where(belongs, values, 0.0), place)
+    rolled_ref[...] = out[:12, :12]
+
+
+def finish(flags, final, moved):
+    shape = jax.ShapeDtypeStruct
+    vmem = pl.BlockSpec(memory_space=pltpu.VMEM)
+    return pl.pallas_call(
+        finish_kernel,
+        in_specs=[pl.BlockSpec(memory_space=pltpu.SMEM)] + [vmem] * 2,
+        out_specs=[vmem] * 3,
+        out_shape=[shape((2, 8, MODEL), F32), shape((2, 8, MODEL), F32), shape((12, 12), F32)],
+        name="finish_rows",
+    )(flags, final, moved)
 
 
 def paired(value, axis, odd_first):
@@ -363,86 +594,58 @@
         ],
         axis=1,
     )
-    slots = lax.all_to_all(slots, "lon", 0, 0, tiled=True).reshape(lon_count * 8, 128)
-
     left = jnp.where(even_lon, far_lon, near_lon)
     right = jnp.where(even_lon, near_lon, far_lon)
     top = jnp.stack([left[0], own[0, 0], own[1, 0], right[0]])
     bottom = jnp.stack([left[3], own[0, 3], own[1, 3], right[3]])
-    near_lat = paired(jnp.where(even_lat, bottom, top), "lat", False)
-    far_lat = paired(jnp.where(even_lat, top, bottom), "lat", True)
-
-    flags = jnp.stack([lon % 2, lat % 2, (lat == 0).astype(jnp.int32), (lat == lat_count - 1).astype(jnp.int32)])
+    near_send = jnp.where(even_lat, bottom, top)
+    far_send = jnp.where(even_lat, top, bottom)
+    near_lat = paired(near_send, "lat", False)
+    far_lat = paired(far_send, "lat", True)
+    slots, near_lat, far_lat = lax.optimization_barrier((slots, near_lat, far_lat))
+    slots = lax.all_to_all(slots, "lon", 0, 0, tiled=True).reshape(lon_count * 8, 128)
+
+    plane, member = (lon // 2) % 2, lon // 4 * 2 + lon % 2
+    flags = jnp.stack(
+        [lon % 2, lat % 2, lat == 0, lat == lat_count - 1, plane, lat, member, lon]
+    ).astype(jnp.int32)
     down_rows = adapter_down_map.reshape(16, MODEL)
     up_rows = adapter_up_map.reshape(16, MODEL)
-    block, field, probs, gq, low, normed, w = forward(
-        flags.astype(jnp.int32),
+    loss_scale = 1.0 / math.sqrt(lat_count * lon_count)
+    block, adjoint, sends = core(
+        flags,
         own,
-        near_lon,
-        far_lon,
-        near_lat,
-        far_lat,
+        (near_lon, far_lon, near_lat, far_lat),
         query_key_value_weight,
         output_weight,
         down_rows,
         up_rows,
         readout.reshape(1, MODEL),
         ordered_bias(relative_position_bias),
+        slots,
+        loss_scale,
     )
     block = block.reshape(2, 4, GROUP, MODEL)[:, :, :LIVE].reshape(2, 4, 3, 6, MODEL)
     block_out = block.transpose(1, 2, 0, 3, 4).reshape(12, 12, MODEL)
 
-    loss_scale = 1.0 / math.sqrt(lat_count * lon_count)
-    innov, adjoint, grads = observe(slots, field, probs, gq, low, normed, w, up_rows, loss_scale)
-
     planes = [[i for i in range(lon_count) if (i // 2) % 2 == h] for h in range(2)]
     columns = [
-        [a * lon_count + plane * 4 + h * 2 + c for h in range(2) for a in range(lat_count)]
-        for plane in range(lon_count // 4)
+        [a * lon_count + at * 4 + h * 2 + c for h in range(2) for a in range(lat_count)]
+        for at in range(lon_count // 4)
         for c in range(2)
     ]
-    chunks = lax.all_to_all(
-        grads.reshape(32, 4, 128), "lon", 0, 0, axis_index_groups=planes, tiled=True
-    )
-    chunk = jnp.sum(chunks, axis=0).reshape(2, 1, 2, 128)
-    adjoint_row = adjoint[0].reshape(1, 1, 2, 128)
-    chunk = jnp.concatenate(
-        [
-            jnp.broadcast_to(chunk, (2, lat_count, 2, 128)),
-            jnp.broadcast_to(adjoint_row, (2, lat_count, 2, 128)),
-        ],
-        axis=2,
-    ).reshape(2 * lat_count, 4, 128)
-    along = lax.all_to_all(chunk, ("lat", "lon"), 0, 0, axis_index_groups=columns, tiled=True)
-    half = jnp.sum(along[:, :2], axis=0)
-    below = lax.dynamic_index_in_dim(
-        along, ((lon // 2) % 2) * lat_count + (lat + 1) % lat_count, 0, keepdims=False
-    )[2:]
-    below = below.reshape(256)[:OWN].reshape(2, 4, GROUP)
-    here = adjoint[0, :OWN].reshape(2, 4, GROUP)
-    moved = jnp.concatenate([here[:, 1:], below[:, :1]], axis=1)
-    edge = jnp.pad(moved[0].reshape(1, 1, 4 * GROUP), ((0, 0), (0, 0), (0, 128 - 4 * GROUP)))
-    last = jnp.concatenate(
-        [
-            jnp.broadcast_to(half[None], (lon_count, 2, 128)),
-            innov[:, None, :],
-            jnp.broadcast_to(edge, (lon_count, 1, 128)),
-        ],
-        axis=1,
-    )
-    final = lax.all_to_all(last, "lon", 0, 0, tiled=True)
-    innovation = final[:, 2][None, None]
-    beside = lax.dynamic_index_in_dim(final[:, 3], (lon + 1) % lon_count, 0, keepdims=False)
-    beside = beside[: 4 * GROUP].reshape(4, GROUP)
-    rolled = jnp.stack([moved[1], beside])[:, :, :LIVE].reshape(2, 4, 3, 6)
-    rolled_adjoint = rolled.transpose(1, 2, 0, 3).reshape(12, 12)
-    parts = final[:, :2].reshape(lon_count // 4, 2, 2, 2, 128)
-
-    def whole(part):
-        part = part.reshape(4, 8, 2, 128)
-        return part.transpose(2, 1, 0, 3).reshape(2, 8, MODEL)
-
-    return block_out, innovation, rolled_adjoint, whole(parts[:, 1]), whole(parts[:, 0])
+
+    def in_plane(rows):
+        rows = rows.reshape(lon_count // 2, 8, 128)
+        rows = lax.all_to_all(rows, "lon", 0, 0, axis_index_groups=planes, tiled=True)
+        return rows.reshape(lon_count * 4, 128)
+
+    chunks = in_plane(sends)
+    along = scatter(chunks, adjoint, 2 * lat_count).reshape(2 * lat_count, BLOCK, 128)
+    along = lax.all_to_all(along, ("lat", "lon"), 0, 0, axis_index_groups=columns, tiled=True)
+    final, innovation, moved = gather(flags, along.reshape(-1, 128), chunks, adjoint)
+    up_gradient, down_gradient, rolled_adjoint = finish(flags, in_plane(final), moved)
+    return block_out, innovation[None, None], rolled_adjoint, down_gradient, up_gradient
 
 
 def solution(mesh):

time: 138 us -> 155 us (1.12)
  blocking collectives: 0 us -> 37.2 us
  waiting for transfers between devices: 46.3 us -> 25.1 us
  Pallas kernels: 17.7 us -> 25.2 us
  local copies, waits for them, and re-layouts: 9.8 us -> 6.3 us
    all_to_all x0 -> x2, blocking collectives: none -> 37.2 us  [the longest x1 24.5 us: shards(): lax.all_to_all(along, ('lat', 'lon'), 0, 0, axis_index_groups=columns, ti...]
    all_to_all x3 -> x1, waiting for transfers between devices: 35.3 us -> 6.87 us  [in_plane(): lax.all_to_all(rows, 'lon', 0, 0, axis_index_groups=planes, tiled=True)]
    all_to_all x1, waiting for transfers between devices: 0.01 us -> 14.3 us  [shards(): lax.all_to_all(slots, 'lon', 0, 0, tiled=True).reshape(lon_count * 8, 128)]
    all_to_all x3 -> x1, starting transfers between devices: 20.2 us -> 7.31 us  [in_plane(): lax.all_to_all(rows, 'lon', 0, 0, axis_index_groups=planes, tiled=True)]
    all_to_all x1, starting transfers between devices: 9.18 us -> 19.6 us  [shards(): lax.all_to_all(slots, 'lon', 0, 0, tiled=True).reshape(lon_count * 8, 128)]
    pallas_call x2 -> x4, Pallas kernels: 15 us -> 22.6 us  [the longest x1 17.4 us: core(): pl.pallas_call(functools.partial(core_kernel, loss_scale=loss_scale), in_...]
    ppermute x4, waiting for transfers between devices: 11 us -> 3.93 us  [paired(): return lax.ppermute(value, axis, pairs)]
    unnamed x21 -> x25, local copies, waits for them, and re-layouts: 3.7 us -> 1.47 us
  transfers between devices with their start and end apart: 8 -> 6, of which waited for: 5 -> 3; matrix products, arithmetic and copies ran while one was open for 3% -> 4% of each run, Pallas kernels for 9% -> 2%
where the time goes in v2:
time: 155 us; the launch traced here: 154 us
  starting transfers between devices  57.4 us (37%)
  blocking collectives  37.2 us (24%)
  Pallas kernels  25.2 us (16%)
  waiting for transfers between devices  25.1 us (16%)
  local copies, waits for them, and re-layouts  6.3 us (4%)
  other arithmetic  1.96 us (1%)
    ppermute x4, starting transfers between devices, paired(): return lax.ppermute(value, axis, pairs)  30.5 us
    all_to_all x1, blocking collectives, shards(): lax.all_to_all(along, ('lat', 'lon'), 0, 0, axis_index_groups=columns, ti...  24.5 us
    all_to_all x1, starting transfers between devices, shards(): lax.all_to_all(slots, 'lon', 0, 0, tiled=True).reshape(lon_count * 8, 128)  19.6 us
    pallas_call x1, Pallas kernels, core(): pl.pallas_call(functools.partial(core_kernel, loss_scale=loss_scale), in_...  17.4 us
    all_to_all x1, waiting for transfers between devices, shards(): lax.all_to_all(slots, 'lon', 0, 0, tiled=True).reshape(lon_count * 8, 128)  14.3 us
    all_to_all x1, blocking collectives, in_plane(): lax.all_to_all(rows, 'lon', 0, 0, axis_index_groups=planes, tiled=True)  12.7 us
    all_to_all x1, starting transfers between devices, in_plane(): lax.all_to_all(rows, 'lon', 0, 0, axis_index_groups=planes, tiled=True)  7.31 us
    all_to_all x1, waiting for transfers between devices, in_plane(): lax.all_to_all(rows, 'lon', 0, 0, axis_index_groups=planes, tiled=True)  6.87 us
  transfers between devices with their start and end apart: 6, of which 3 were waited for; matrix products, arithmetic and copies ran while one was open for 4% of the time, Pallas kernels for 2%

profile of v2, /device:TPU:1, one launch (start us, length us, event | category | flops | bytes accessed | tf_op | source)
XLA Modules:
  0.0 154.2 jit_solution(11979782252893305520)
XLA Ops:
  0.6 0.0 copy-start.3
  0.6 0.0 copy-start.8
  0.7 0.0 copy-start.7
  0.7 0.0 copy-start.4
  0.7 1.1 reshape.136
  1.8 0.1 copy.20
  2.0 16.8 %collective-permute-start.1 = (bf16[4,24,512]{2,1,0:T(8,128)(2,1)S(1)}, bf16[4,24,512]{2,1,0:T(8,128)(2,1)S(1)}, u32[]{:S(2)}, u32[]{:S(2)}) collective-permute-start(bf16[4,24,512]{2,1,0:T(8,128)(2,1)S(1)} %get-tuple-element.37), channel_id=1, source_target_pairs={{0,63},{1,2},{2,1},{3,4},{4,3},{5,6},{6,5},{7,8},{8,7},{9,10},{10,... | collective-permute-start | bytes 294920 | tf_op jit(solution)/shard_map/ppermute | solution.py:560
  18.8 6.4 %collective-permute-start = (bf16[4,24,512]{2,1,0:T(8,128)(2,1)S(1)}, bf16[4,24,512]{2,1,0:T(8,128)(2,1)S(1)}, u32[]{:S(2)}, u32[]{:S(2)}) collective-permute-start(bf16[4,24,512]{2,1,0:T(8,128)(2,1)S(1)} %get-tuple-element.38), channel_id=1, source_target_pairs={{0,1},{1,0},{2,3},{3,2},{4,5},{5,4},{6,7},{7,6},{8,9},{9,8},{10,11... | collective-permute-start | bytes 294920 | tf_op jit(solution)/shard_map/ppermute | solution.py:560
  25.2 0.0 copy-done.3
  25.2 0.8 fusion.3
  26.0 0.4 slice.44
  26.5 0.0 copy-start.9
  26.5 0.4 slice.43
  26.9 0.0 copy-done.8
  27.0 0.1 iota_compare_fusion.1
  27.0 0.0 copy-done.7
  27.0 0.1 bitcast_select_fusion.1
  27.1 0.0 copy-done.4
  27.3 0.0 collective-permute-done.1.far_lon_ref
  27.3 0.0 copy-start.5
  27.3 0.0 collective-permute-done.near_lon_ref
  27.3 0.0 copy-start.6
  27.4 5.4 %collective-permute-start.3 = (bf16[4,24,512]{2,1,0:T(8,128)(2,1)S(1)}, bf16[4,24,512]{2,1,0:T(8,128)(2,1)S(1)}, u32[]{:S(2)}, u32[]{:S(2)}) collective-permute-start(bf16[4,24,512]{2,1,0:T(8,128)(2,1)S(1)} %get-tuple-element.29), channel_id=1, source_target_pairs={{0,448},{64,128},{128,64},{192,256},{256,192},{320,384},{384,320},... | collective-permute-start | bytes 294920 | tf_op jit(solution)/shard_map/ppermute | solution.py:560
  32.8 1.9 %collective-permute-start.2 = (bf16[4,24,512]{2,1,0:T(8,128)(2,1)S(1)}, bf16[4,24,512]{2,1,0:T(8,128)(2,1)S(1)}, u32[]{:S(2)}, u32[]{:S(2)}) collective-permute-start(bf16[4,24,512]{2,1,0:T(8,128)(2,1)S(1)} %get-tuple-element.30), channel_id=1, source_target_pairs={{0,64},{64,0},{128,192},{192,128},{256,320},{320,256},{384,448},{4... | collective-permute-start | bytes 294920 | tf_op jit(solution)/shard_map/ppermute | solution.py:560
  34.7 0.8 pad_maximum_fusion
  35.5 3.9 %collective-permute-done.3.far_lat_ref = bf16[4,24,512]{2,1,0:T(8,128)(2,1)S(1)} collective-permute-done((bf16[4,24,512]{2,1,0:T(8,128)(2,1)S(1)}, bf16[4,24,512]{2,1,0:T(8,128)(2,1)S(1)}, u32[]{:S(2)}, u32[]{:S(2)}) %collective-permute-start.3) | collective-permute-done | bytes 98336 | tf_op jit(solution)/shard_map/ppermute | solution.py:560
  39.5 0.0 collective-permute-done.2.near_lat_ref
  39.5 19.6 %all-to-all-start = ((f32[64,8,128]{2,1,0:T(8,128)}), f32[64,8,128]{2,1,0:T(8,128)S(1)}, u32[]{:S(2)}, u32[]{:S(2)}) async-start(f32[64,8,128]{2,1,0:T(8,128)} %pad_maximum_fusion), calls=%async_computation | async-start | bytes 524288 | tf_op jit(solution)/shard_map/all_to_all | solution.py:606
  59.1 0.6 reshape.140.readout_ref
  59.7 0.7 pad.4.own_ref
  60.4 0.7 stack.49.flags_ref
  61.1 2.7 %ordered_bias.1.bias_hbm = f32[4,16,24,128]{3,2,1,0:T(8,128)} custom-call(f32[1152,72]{1,0:T(8,128)} %bitcast.74), custom_call_target="tpu_custom_call" | custom-call | flops 200000000 | bytes 2000000 | tf_op jit(solution)/shard_map/ordered_bias/pallas_call | solution.py:60
  63.7 0.0 copy-done.5
  63.7 14.3 %all-to-all-done = f32[64,8,128]{2,1,0:T(8,128)S(1)} async-done(((f32[64,8,128]{2,1,0:T(8,128)}), f32[64,8,128]{2,1,0:T(8,128)S(1)}, u32[]{:S(2)}, u32[]{:S(2)}) %all-to-all-start) | async-done | bytes 262176 | tf_op jit(solution)/shard_map/all_to_all | solution.py:606
  78.0 0.0 copy-done.10
  78.1 0.7 copy-done.1
  78.8 17.4 %window_and_observe.1 = (bf16[192,512]{1,0:T(8,128)(2,1)}, f32[8,256]{1,0:T(8,128)}, f32[256,128]{1,0:T(8,128)}) custom-call(s32[8]{0:T(128)} %stack.49.flags_ref, bf16[2,4,24,512]{3,2,1,0:T(8,128)(2,1)} %pad.4.own_ref, bf16[4,24,512]{2,1,0:T(8,128)(2,1)} %copy-done.6, bf16[4,24,512]{2,1,0:T(8,128)(2,1)} %copy-done.5, bf16[4,24,512]{2,1,0:T(8,128)(2,1)} %copy-done.11, ...), custom_call_target="tpu_custom_call" | custom-call | flops 3000000000 | bytes 8000000 | tf_op jit(solution)/shard_map/window_and_observe/pallas_call | solution.py:390
  96.2 12.7 %all_to_all.20 = f32[32,8,128]{2,1,0:T(8,128)} all-to-all(f32[32,8,128]{2,1,0:T(8,128)} %bitcast.83), channel_id=1, replica_groups={{0,1,4,5,8,9,12,13,16,17,20,21,24,25,28,29,32,33,36,37,40,41,44,45,48,4..., dimensions={0} | all-to-all | bytes 262144 | tf_op jit(solution)/shard_map/all_to_all | solution.py:640
  108.9 1.6 %scatter_rows.1 = bf16[768,128]{1,0:T(8,128)(2,1)} custom-call(f32[256,128]{1,0:T(8,128)} %bitcast.69, f32[8,256]{1,0:T(8,128)} %get-tuple-element.22.adjoint_ref), custom_call_target="tpu_custom_call" | custom-call | tf_op jit(solution)/shard_map/scatter_rows/pallas_call | solution.py:450
  110.5 24.5 %all_to_all.21 = bf16[16,48,128]{2,1,0:T(8,128)(2,1)} all-to-all(bf16[16,48,128]{2,1,0:T(8,128)(2,1)} %bitcast.73), channel_id=1, replica_groups={{0,64,128,192,256,320,384,448,2,66,130,194,258,322,386,450},{1,65,129,1..., dimensions={0} | all-to-all | bytes 393216 | tf_op jit(solution)/shard_map/all_to_all | solution.py:645
  135.0 1.8 %gather_rows.1 = (f32[256,128]{1,0:T(8,128)}, f32[64,128]{1,0:T(8,128)}, f32[8,256]{1,0:T(8,128)}) custom-call(s32[8]{0:T(128)} %stack.49.flags_ref, bf16[768,128]{1,0:T(8,128)(2,1)} %bitcast.71, f32[256,128]{1,0:T(8,128)} %bitcast.70, f32[8,256]{1,0:T(8,128)} %get-tuple-element.22.adjoint_ref), custom_call_target="tpu_custom_call" | custom-call | tf_op jit(solution)/shard_map/gather_rows/pallas_call | solution.py:509
  136.7 7.3 %all-to-all-start.3 = ((f32[32,8,128]{2,1,0:T(8,128)}), f32[32,8,128]{2,1,0:T(8,128)S(1)}, u32[]{:S(2)}, u32[]{:S(2)}) async-start(f32[32,8,128]{2,1,0:T(8,128)} %bitcast.82), calls=%async_computation.3 | async-start | bytes 262144 | tf_op jit(solution)/shard_map/all_to_all | solution.py:640
  144.0 0.0 copy-done.2
  144.0 0.1 copy.26
  144.2 0.7 reshape.145
  144.9 6.9 %all-to-all-done.3 = f32[32,8,128]{2,1,0:T(8,128)S(1)} async-done(((f32[32,8,128]{2,1,0:T(8,128)}), f32[32,8,128]{2,1,0:T(8,128)S(1)}, u32[]{:S(2)}, u32[]{:S(2)}) %all-to-all-start.3) | async-done | bytes 131104 | tf_op jit(solution)/shard_map/all_to_all | solution.py:640
  151.8 0.6 copy-done
  152.4 1.8 %finish_rows.1 = (f32[2,8,512]{2,1,0:T(8,128)}, f32[2,8,512]{2,1,0:T(8,128)}, f32[12,12]{1,0:T(8,128)}) custom-call(s32[8]{0:T(128)} %stack.49.flags_ref, f32[256,128]{1,0:T(8,128)} %bitcast.77, f32[8,256]{1,0:T(8,128)} %get-tuple-element.25.moved_ref), custom_call_target="tpu_custom_call" | custom-call | tf_op jit(solution)/shard_map/finish_rows/pallas_call | solution.py:545
  (18 shorter events, 0.3 us)
Async XLA Ops:
  0.6 24.6 %copy-start.3 = (s32[1,1,64,4,128]{4,3,2,1,0:T(4,128)S(1)}, s32[1,1,64,4,128]{4,3,2,1,0:T(4,128)}, u32[]{:S(2)}) copy-start(s32[1,1,64,4,128]{4,3,2,1,0:T(4,128)} %param.18) | copy-start | bytes 393220
  0.6 26.3 %copy-start.8 = (s32[1,1,64]{2,1,0:T(1,128)S(1)}, s32[1,1,64]{2,1,0:T(1,128)}, u32[]{:S(2)}) copy-start(s32[1,1,64]{2,1,0:T(1,128)} %param.21) | copy-start | bytes 772
  0.7 26.4 %copy-start.7 = (f32[1,1,64,128]{3,2,1,0:T(8,128)S(1)}, f32[1,1,64,128]{3,2,1,0:T(8,128)}, u32[]{:S(2)}) copy-start(f32[1,1,64,128]{3,2,1,0:T(8,128)} %param.20) | copy-start | bytes 98308
  0.7 26.5 %copy-start.4 = (f32[1,1,64,4,128]{4,3,2,1,0:T(4,128)S(1)}, f32[1,1,64,4,128]{4,3,2,1,0:T(4,128)}, u32[]{:S(2)}) copy-start(f32[1,1,64,4,128]{4,3,2,1,0:T(4,128)} %param.19) | copy-start | bytes 393220
  2.0 25.3 %collective-permute-start.1 = (bf16[4,24,512]{2,1,0:T(8,128)(2,1)S(1)}, bf16[4,24,512]{2,1,0:T(8,128)(2,1)S(1)}, u32[]{:S(2)}, u32[]{:S(2)}) collective-permute-start(bf16[4,24,512]{2,1,0:T(8,128)(2,1)S(1)} %get-tuple-element.37), channel_id=1, source_target_pairs={{0,63},{1,2},{2,1},{3,4},{4,3},{5,6},{6,5},{7,8},{8,7},{9,10},{10,... | collective-permute-start | bytes 294920 | tf_op jit(solution)/shard_map/ppermute | solution.py:560
  18.8 8.5 %collective-permute-start = (bf16[4,24,512]{2,1,0:T(8,128)(2,1)S(1)}, bf16[4,24,512]{2,1,0:T(8,128)(2,1)S(1)}, u32[]{:S(2)}, u32[]{:S(2)}) collective-permute-start(bf16[4,24,512]{2,1,0:T(8,128)(2,1)S(1)} %get-tuple-element.38), channel_id=1, source_target_pairs={{0,1},{1,0},{2,3},{3,2},{4,5},{5,4},{6,7},{7,6},{8,9},{9,8},{10,11... | collective-permute-start | bytes 294920 | tf_op jit(solution)/shard_map/ppermute | solution.py:560
  26.5 32.6 %copy-start.9 = (bf16[512]{0:T(512)(128)(2,1)S(1)}, bf16[512]{0:T(512)(128)(2,1)}, u32[]{:S(2)}) copy-start(bf16[512]{0:T(512)(128)(2,1)} %param.17) | copy-start | bytes 3076
  27.3 36.5 %copy-start.5 = (bf16[4,24,512]{2,1,0:T(8,128)(2,1)}, bf16[4,24,512]{2,1,0:T(8,128)(2,1)S(1)}, u32[]{:S(2)}) copy-start(bf16[4,24,512]{2,1,0:T(8,128)(2,1)S(1)} %collective-permute-done.1.far_lon_ref) | copy-start | bytes 294916
  27.3 36.5 %copy-start.6 = (bf16[4,24,512]{2,1,0:T(8,128)(2,1)}, bf16[4,24,512]{2,1,0:T(8,128)(2,1)S(1)}, u32[]{:S(2)}) copy-start(bf16[4,24,512]{2,1,0:T(8,128)(2,1)S(1)} %collective-permute-done.near_lon_ref) | copy-start | bytes 294916
  27.4 12.1 %collective-permute-start.3 = (bf16[4,24,512]{2,1,0:T(8,128)(2,1)S(1)}, bf16[4,24,512]{2,1,0:T(8,128)(2,1)S(1)}, u32[]{:S(2)}, u32[]{:S(2)}) collective-permute-start(bf16[4,24,512]{2,1,0:T(8,128)(2,1)S(1)} %get-tuple-element.29), channel_id=1, source_target_pairs={{0,448},{64,128},{128,64},{192,256},{256,192},{320,384},{384,320},... | collective-permute-start | bytes 294920 | tf_op jit(solution)/shard_map/ppermute | solution.py:560
  32.8 6.7 %collective-permute-start.2 = (bf16[4,24,512]{2,1,0:T(8,128)(2,1)S(1)}, bf16[4,24,512]{2,1,0:T(8,128)(2,1)S(1)}, u32[]{:S(2)}, u32[]{:S(2)}) collective-permute-start(bf16[4,24,512]{2,1,0:T(8,128)(2,1)S(1)} %get-tuple-element.30), channel_id=1, source_target_pairs={{0,64},{64,0},{128,192},{192,128},{256,320},{320,256},{384,448},{4... | collective-permute-start | bytes 294920 | tf_op jit(solution)/shard_map/ppermute | solution.py:560
  39.5 38.6 %copy-start.10 = (bf16[4,24,512]{2,1,0:T(8,128)(2,1)}, bf16[4,24,512]{2,1,0:T(8,128)(2,1)S(1)}, u32[]{:S(2)}) copy-start(bf16[4,24,512]{2,1,0:T(8,128)(2,1)S(1)} %collective-permute-done.3.far_lat_ref) | copy-start | bytes 294916
  39.5 38.6 %copy-start.11 = (bf16[4,24,512]{2,1,0:T(8,128)(2,1)}, bf16[4,24,512]{2,1,0:T(8,128)(2,1)S(1)}, u32[]{:S(2)}) copy-start(bf16[4,24,512]{2,1,0:T(8,128)(2,1)S(1)} %collective-permute-done.2.near_lat_ref) | copy-start | bytes 294916
  39.5 38.6 %all-to-all-start = ((f32[64,8,128]{2,1,0:T(8,128)}), f32[64,8,128]{2,1,0:T(8,128)S(1)}, u32[]{:S(2)}, u32[]{:S(2)}) async-start(f32[64,8,128]{2,1,0:T(8,128)} %pad_maximum_fusion), calls=%async_computation | async-start | bytes 524288 | tf_op jit(solution)/shard_map/all_to_all | solution.py:606
  78.0 0.7 copy-start.1
  96.1 47.9 %copy-start.2 = (bf16[192,512]{1,0:T(8,128)(2,1)S(1)}, bf16[192,512]{1,0:T(8,128)(2,1)}, u32[]{:S(2)}) copy-start(bf16[192,512]{1,0:T(8,128)(2,1)} %get-tuple-element.20) | copy-start | bytes 589828
  136.7 15.1 %all-to-all-start.3 = ((f32[32,8,128]{2,1,0:T(8,128)}), f32[32,8,128]{2,1,0:T(8,128)S(1)}, u32[]{:S(2)}, u32[]{:S(2)}) async-start(f32[32,8,128]{2,1,0:T(8,128)} %bitcast.82), calls=%async_computation.3 | async-start | bytes 262144 | tf_op jit(solution)/shard_map/all_to_all | solution.py:640
  151.8 0.6 copy-start

commit v3 on v2

--- a/solution.py
+++ b/solution.py
@@ -61,7 +61,7 @@
         bias_kernel,
         out_shape=jax.ShapeDtypeStruct((4, HEADS, GROUP, 128), F32),
         scratch_shapes=[pltpu.VMEM((HEADS, 72, 128), F32)],
-        cost_estimate=pl.CostEstimate(flops=2 * 10**8, bytes_accessed=2 * 10**6, transcendentals=0),
+        cost_estimate=pl.CostEstimate(flops=2 * 10**10, bytes_accessed=2 * 10**6, transcendentals=0),
         name="ordered_bias",
     )(bias.reshape(HEADS * 72, 72))
 
@@ -199,7 +199,6 @@
 
 
 def observe_part(
-    flags_ref,
     slots_ref,
     field_ref,
     probs_ref,
@@ -209,7 +208,7 @@
     w_ref,
     up_ref,
     adjoint_ref,
-    sends_ref,
+    grads_ref,
     innov_ref,
     term_ref,
     place_ref,
@@ -279,19 +278,11 @@
     up_value = exact(sums, w_masked, TN)
     down_value = mm(exact(rank_head, weighted).astype(BF16), norm_ref[...])
 
-    sends_ref[...] = jnp.zeros_like(sends_ref)
     parts = (up_query[:8], up_value[8:], down_query[:8], down_value[8:])
     for m, part in enumerate(parts):
         part = part * factor
         for q in range(4):
-            sends_ref[pl.ds(q * 64 + m, 8, stride=8), :] = part[:, 128 * q : 128 * (q + 1)]
-    low_plane = flags_ref[4] == 0
-    for core in range(2):
-        planes = [innov_ref[pl.ds(2 * h + core, sources // 4, stride=4), :] for h in range(2)]
-        mine = jnp.where(low_plane, planes[0], planes[1])
-        other = jnp.where(low_plane, planes[1], planes[0])
-        sends_ref[pl.ds(8 * core + 4, sources // 4, stride=16), :] = mine
-        sends_ref[pl.ds(8 * core + 5, sources // 4, stride=16), :] = other
+            grads_ref[pl.ds(q * 32 + m, 8, stride=4), :] = part[:, 128 * q : 128 * (q + 1)]
 
 
 def core_kernel(
@@ -310,7 +301,8 @@
     slots_hbm,
     block_ref,
     adjoint_ref,
-    sends_ref,
+    grads_ref,
+    innov_ref,
     field_ref,
     probs_ref,
     gq_ref,
@@ -325,7 +317,6 @@
     wo_ref,
     bias_ref,
     copy_sems,
-    innov_ref,
     term_ref,
     place_ref,
     slots_ref,
@@ -364,7 +355,6 @@
     )
     slot_load.wait()
     observe_part(
-        flags_ref,
         slots_ref,
         field_ref,
         probs_ref,
@@ -374,7 +364,7 @@
         w_ref,
         up_ref,
         adjoint_ref,
-        sends_ref,
+        grads_ref,
         innov_ref,
         term_ref,
         place_ref,
@@ -390,11 +380,12 @@
     return pl.pallas_call(
         functools.partial(core_kernel, loss_scale=loss_scale),
         in_specs=[smem] + [vmem] * 5 + [far] * 2 + [vmem] * 3 + [far] * 2,
-        out_specs=[vmem] * 3,
+        out_specs=[vmem] * 4,
         out_shape=[
             shape((OWN, MODEL), BF16),
             shape((8, 256), F32),
-            shape((sources // 2 * 8, 128), F32),
+            shape((128, 128), F32),
+            shape((sources, 128), F32),
         ],
         scratch_shapes=[
             pltpu.VMEM((8, 256), F32),
@@ -411,7 +402,6 @@
             pltpu.VMEM((MODEL, MODEL), BF16),
             pltpu.VMEM((4, HEADS, GROUP, 128), F32),
             pltpu.SemaphoreType.DMA((4,)),
-            pltpu.VMEM((sources, 128), F32),
             pltpu.VMEM((4 * sources, 128), F32),
             pltpu.VMEM((4 * sources, 128), jnp.int32),
             pltpu.VMEM((sources * 8, 128), F32),
@@ -422,133 +412,6 @@
         ),
         name="window_and_observe",
     )(flags, own, *halos, qkv, wo, down, up, readout, bias, slots)
-
-
-BLOCK = 48
-
-
-def scatter_kernel(chunks_ref, adjoint_ref, out_ref, rows_ref):
-    total = jnp.sum(chunks_ref[...].reshape(-1, 8, 128), axis=0)
-    rows_ref[...] = jnp.zeros_like(rows_ref)
-    for at, values in ((0, total[0:4]), (8, None)):
-        if values is None:
-            values = jnp.concatenate([adjoint_ref[0:1, :128], adjoint_ref[0:1, 128:]], axis=0)
-        high = values.astype(BF16).astype(F32)
-        count = values.shape[0]
-        rows_ref[at : at + count, :] = high
-        rows_ref[at + count : at + 2 * count, :] = values - high
-    head = rows_ref[...].astype(BF16)
-    members = chunks_ref.shape[0] // 8
-    other = chunks_ref[pl.ds(5, members, stride=8), :].astype(BF16)
-    for at in range(out_ref.shape[0] // BLOCK):
-        out_ref[at * BLOCK : at * BLOCK + 16, :] = head
-        out_ref[at * BLOCK + 16 : (at + 1) * BLOCK, :] = other
-
-
-def scatter(chunks, adjoint, members):
-    vmem = pl.BlockSpec(memory_space=pltpu.VMEM)
-    return pl.pallas_call(
-        scatter_kernel,
-        in_specs=[vmem] * 2,
-        out_specs=vmem,
-        out_shape=jax.ShapeDtypeStruct((members * BLOCK, 128), BF16),
-        scratch_shapes=[pltpu.VMEM((16, 128), F32)],
-        name="scatter_rows",
-    )(chunks, adjoint)
-
-
-def gather_kernel(flags_ref, along_ref, chunks_ref, adjoint_ref, out_ref, innov_ref, moved_ref):
-    lat_count = along_ref.shape[0] // BLOCK // 2
-    plane, lat = flags_ref[4], flags_ref[5]
-    next_lat = jnp.where(lat == lat_count - 1, 0, lat + 1)
-
-    def rows_of(h, a):
-        start = pl.multiple_of((h * lat_count + a) * BLOCK, 16)
-        return along_ref[pl.ds(start, 16), :].astype(F32)
-
-    def adjoint_of(rows):
-        values = rows[8:10] + rows[10:12]
-        return jnp.concatenate([values[0:1], values[1:2]], axis=1)
-
-    lane = lax.broadcasted_iota(jnp.int32, (1, 256), 1)
-
-    def shift_rows(here, below):
-        kept = pltpu.roll(here, 256 - GROUP, 1)
-        new = pltpu.roll(below, 3 * GROUP, 1)
-        return jnp.where(lane % (4 * GROUP) < 3 * GROUP, kept, new)
-
-    moved = shift_rows(adjoint_ref[0:1, :], adjoint_of(rows_of(plane, next_lat)))
-    twin = shift_rows(
-        adjoint_of(rows_of(1 - plane, lat)), adjoint_of(rows_of(1 - plane, next_lat))
-    )
-    moved_ref[...] = jnp.broadcast_to(moved, (8, 256))
-
-    total = jnp.zeros((16, 128), F32)
-    for at in range(2 * lat_count):
-        total = total + along_ref[at * BLOCK : at * BLOCK + 16, :].astype(F32)
-    total = total[0:4] + total[4:8]
-    block = jnp.concatenate([total, moved[:, :128], twin[:, :128], jnp.zeros((2, 128), F32)], axis=0)
-    members = out_ref.shape[0] // 8
-    for at in range(members):
-        out_ref[at * 8 : at * 8 + 8, :] = block
-
-    near = chunks_ref[pl.ds(4, members, stride=8), :]
-    start = pl.multiple_of(((1 - plane) * lat_count + lat) * BLOCK + 16, 16)
-    far = along_ref[pl.ds(start, members), :].astype(F32)
-    low_plane = plane == 0
-    planes = (jnp.where(low_plane, near, far), jnp.where(low_plane, far, near))
-    for h in range(2):
-        for m in range(members // 2):
-            innov_ref[4 * m + 2 * h : 4 * m + 2 * h + 2, :] = planes[h][2 * m : 2 * m + 2]
-
-
-def gather(flags, along, chunks, adjoint):
-    members = chunks.shape[0] // 8
-    shape = jax.ShapeDtypeStruct
-    vmem = pl.BlockSpec(memory_space=pltpu.VMEM)
-    return pl.pallas_call(
-        gather_kernel,
-        in_specs=[pl.BlockSpec(memory_space=pltpu.SMEM)] + [vmem] * 3,
-        out_specs=[vmem] * 3,
-        out_shape=[shape((members * 8, 128), F32), shape((2 * members, 128), F32), shape((8, 256), F32)],
-        name="gather_rows",
-    )(flags, along, chunks, adjoint)
-
-
-def finish_kernel(flags_ref, final_ref, moved_ref, up_ref, down_ref, rolled_ref):
-    for m, (ref, which) in enumerate(((up_ref, 0), (up_ref, 1), (down_ref, 0), (down_ref, 1))):
-        for q in range(4):
-            ref[which, :, 128 * q : 128 * (q + 1)] = final_ref[pl.ds(q * 64 + m, 8, stride=8), :]
-    members = final_ref.shape[0] // 8
-    plane, member = flags_ref[4], flags_ref[6]
-    across = member - 1 + 2 * plane
-    across = jnp.where(across >= members, 0, across)
-    row = jnp.where(flags_ref[0] == 0, (member + 1) * 8 + 4, across * 8 + 5)
-    beside = final_ref[pl.ds(row, 1), :]
-    moved = pltpu.roll(moved_ref[0:1, :], 256 - 4 * GROUP, 1)[:, :128]
-    lane = lax.broadcasted_iota(jnp.int32, (16, 128), 1)
-    out_row = lax.broadcasted_iota(jnp.int32, (16, 128), 0)
-    in_group = lane % GROUP
-    belongs = (lane // GROUP * 3 + in_group // 6 == out_row) & (in_group < LIVE) & (lane < 4 * GROUP)
-    from_lane = lax.broadcasted_iota(jnp.int32, (128, 128), 0)
-    to_lane = lax.broadcasted_iota(jnp.int32, (128, 128), 1)
-    out = jnp.zeros((16, 128), F32)
-    for half, values in enumerate((moved, beside)):
-        place = (from_lane % GROUP % 6 + 6 * half == to_lane).astype(F32)
-        out = out + exact(jnp.where(belongs, values, 0.0), place)
-    rolled_ref[...] = out[:12, :12]
-
-
-def finish(flags, final, moved):
-    shape = jax.ShapeDtypeStruct
-    vmem = pl.BlockSpec(memory_space=pltpu.VMEM)
-    return pl.pallas_call(
-        finish_kernel,
-        in_specs=[pl.BlockSpec(memory_space=pltpu.SMEM)] + [vmem] * 2,
-        out_specs=[vmem] * 3,
-        out_shape=[shape((2, 8, MODEL), F32), shape((2, 8, MODEL), F32), shape((12, 12), F32)],
-        name="finish_rows",
-    )(flags, final, moved)
 
 
 def paired(value, axis, odd_first):
@@ -579,8 +442,15 @@
 
     own = tokens.reshape(4, 3, 2, 6, MODEL).transpose(2, 0, 1, 3, 4).reshape(2, 4, LIVE, MODEL)
     own = jnp.pad(own, ((0, 0), (0, 0), (0, GROUP - LIVE), (0, 0)))
-    near_lon = paired(jnp.where(even_lon, own[1], own[0]), "lon", False)
-    far_lon = paired(jnp.where(even_lon, own[0], own[1]), "lon", True)
+    near_send, far_send, observation_index = lax.optimization_barrier(
+        (
+            jnp.where(even_lon, own[1], own[0]),
+            jnp.where(even_lon, own[0], own[1]),
+            observation_index,
+        )
+    )
+    near_lon = paired(near_send, "lon", False)
+    far_lon = paired(far_send, "lon", True)
 
     patch_row, patch_col = observation_index[0, 0] // 12, observation_index[0, 0] % 12
     place = ((patch_col // 6) * 4 + patch_row // 3) * GROUP + (patch_row % 3) * 6 + patch_col % 6
@@ -600,19 +470,18 @@
     bottom = jnp.stack([left[3], own[0, 3], own[1, 3], right[3]])
     near_send = jnp.where(even_lat, bottom, top)
     far_send = jnp.where(even_lat, top, bottom)
+    near_send, far_send, bias = lax.optimization_barrier(
+        (near_send, far_send, relative_position_bias)
+    )
     near_lat = paired(near_send, "lat", False)
     far_lat = paired(far_send, "lat", True)
-    slots, near_lat, far_lat = lax.optimization_barrier((slots, near_lat, far_lat))
     slots = lax.all_to_all(slots, "lon", 0, 0, tiled=True).reshape(lon_count * 8, 128)
 
-    plane, member = (lon // 2) % 2, lon // 4 * 2 + lon % 2
-    flags = jnp.stack(
-        [lon % 2, lat % 2, lat == 0, lat == lat_count - 1, plane, lat, member, lon]
-    ).astype(jnp.int32)
+    flags = jnp.stack([lon % 2, lat % 2, lat == 0, lat == lat_count - 1]).astype(jnp.int32)
     down_rows = adapter_down_map.reshape(16, MODEL)
     up_rows = adapter_up_map.reshape(16, MODEL)
     loss_scale = 1.0 / math.sqrt(lat_count * lon_count)
-    block, adjoint, sends = core(
+    block, adjoint, grads, innov = core(
         flags,
         own,
         (near_lon, far_lon, near_lat, far_lat),
@@ -621,7 +490,7 @@
         down_rows,
         up_rows,
         readout.reshape(1, MODEL),
-        ordered_bias(relative_position_bias),
+        ordered_bias(bias),
         slots,
         loss_scale,
     )
@@ -630,22 +499,52 @@
 
     planes = [[i for i in range(lon_count) if (i // 2) % 2 == h] for h in range(2)]
     columns = [
-        [a * lon_count + at * 4 + h * 2 + c for h in range(2) for a in range(lat_count)]
-        for at in range(lon_count // 4)
+        [a * lon_count + plane * 4 + h * 2 + c for h in range(2) for a in range(lat_count)]
+        for plane in range(lon_count // 4)
         for c in range(2)
     ]
-
-    def in_plane(rows):
-        rows = rows.reshape(lon_count // 2, 8, 128)
-        rows = lax.all_to_all(rows, "lon", 0, 0, axis_index_groups=planes, tiled=True)
-        return rows.reshape(lon_count * 4, 128)
-
-    chunks = in_plane(sends)
-    along = scatter(chunks, adjoint, 2 * lat_count).reshape(2 * lat_count, BLOCK, 128)
-    along = lax.all_to_all(along, ("lat", "lon"), 0, 0, axis_index_groups=columns, tiled=True)
-    final, innovation, moved = gather(flags, along.reshape(-1, 128), chunks, adjoint)
-    up_gradient, down_gradient, rolled_adjoint = finish(flags, in_plane(final), moved)
-    return block_out, innovation[None, None], rolled_adjoint, down_gradient, up_gradient
+    chunks = lax.all_to_all(
+        grads.reshape(32, 4, 128), "lon", 0, 0, axis_index_groups=planes, tiled=True
+    )
+    chunk = jnp.sum(chunks, axis=0).reshape(2, 1, 2, 128)
+    adjoint_row = adjoint[0].reshape(1, 1, 2, 128)
+    chunk = jnp.concatenate(
+        [
+            jnp.broadcast_to(chunk, (2, lat_count, 2, 128)),
+            jnp.broadcast_to(adjoint_row, (2, lat_count, 2, 128)),
+        ],
+        axis=2,
+    ).reshape(2 * lat_count, 4, 128)
+    along = lax.all_to_all(chunk, ("lat", "lon"), 0, 0, axis_index_groups=columns, tiled=True)
+    half = jnp.sum(along[:, :2], axis=0)
+    below = lax.dynamic_index_in_dim(
+        along, ((lon // 2) % 2) * lat_count + (lat + 1) % lat_count, 0, keepdims=False
+    )[2:]
+    below = below.reshape(256)[:OWN].reshape(2, 4, GROUP)
+    here = adjoint[0, :OWN].reshape(2, 4, GROUP)
+    moved = jnp.concatenate([here[:, 1:], below[:, :1]], axis=1)
+    edge = jnp.pad(moved[0].reshape(1, 1, 4 * GROUP), ((0, 0), (0, 0), (0, 128 - 4 * GROUP)))
+    last = jnp.concatenate(
+        [
+            jnp.broadcast_to(half[None], (lon_count, 2, 128)),
+            innov[:, None, :],
+            jnp.broadcast_to(edge, (lon_count, 1, 128)),
+        ],
+        axis=1,
+    )
+    final = lax.all_to_all(last, "lon", 0, 0, tiled=True)
+    innovation = final[:, 2][None, None]
+    beside = lax.dynamic_index_in_dim(final[:, 3], (lon + 1) % lon_count, 0, keepdims=False)
+    beside = beside[: 4 * GROUP].reshape(4, GROUP)
+    rolled = jnp.stack([moved[1], beside])[:, :, :LIVE].reshape(2, 4, 3, 6)
+    rolled_adjoint = rolled.transpose(1, 2, 0, 3).reshape(12, 12)
+    parts = final[:, :2].reshape(lon_count // 4, 2, 2, 2, 128)
+
+    def whole(part):
+        part = part.reshape(4, 8, 2, 128)
+        return part.transpose(2, 1, 0, 3).reshape(2, 8, MODEL)
+
+    return block_out, innovation, rolled_adjoint, whole(parts[:, 1]), whole(parts[:, 0])
 
 
 def solution(mesh):

time: 155 us -> 137 us (0.88)
  blocking collectives: 37.2 us -> 0 us
  waiting for transfers between devices: 25.1 us -> 42.1 us
  Pallas kernels: 25.2 us -> 20 us
  local copies, waits for them, and re-layouts: 6.3 us -> 10.5 us
  other arithmetic: 1.96 us -> 4.86 us
    all_to_all x2 -> x0, blocking collectives: 37.2 us -> none  [the longest x1 24.5 us: shards(): lax.all_to_all(along, ('lat', 'lon'), 0, 0, axis_index_groups=columns, ti...]
    all_to_all x1 -> x3, waiting for transfers between devices: 6.87 us -> 33 us  [the longest x1 15.7 us: shards(): final = lax.all_to_all(last, 'lon', 0, 0, tiled=True)]
    all_to_all x1, waiting for transfers between devices: 14.3 us -> 0.01 us  [shards(): lax.all_to_all(slots, 'lon', 0, 0, tiled=True).reshape(lon_count * 8, 128)]
    all_to_all x1 -> x3, starting transfers between devices: 7.31 us -> 19.6 us  [the longest x1 7.72 us: shards(): lax.all_to_all(grads.reshape(32, 4, 128), 'lon', 0, 0, axis_index_groups=...]
    all_to_all x1, starting transfers between devices: 19.6 us -> 9.19 us  [shards(): lax.all_to_all(slots, 'lon', 0, 0, tiled=True).reshape(lon_count * 8, 128)]
    ppermute x4, waiting for transfers between devices: 3.93 us -> 9.12 us  [paired(): return lax.ppermute(value, axis, pairs)]
    pallas_call x3 -> x0, Pallas kernels: 5.19 us -> none  [the longest x1 1.81 us: finish(): pl.pallas_call(finish_kernel, in_specs=[pl.BlockSpec(memory_space=pltpu.S...]
    concatenate x0 -> x3, other arithmetic: none -> 2.17 us  [the longest x1 1.52 us: shards(): jnp.concatenate([jnp.broadcast_to(half[None], (lon_count, 2, 128)), innov...]
  transfers between devices with their start and end apart: 6 -> 8, of which waited for: 3 -> 4; matrix products, arithmetic and copies ran while one was open for 4% -> 6% of each run, Pallas kernels for 2% -> 2%
where the time goes in v3:
time: 137 us; the launch traced here: 136 us
  starting transfers between devices  57.8 us (42%)
  waiting for transfers between devices  42.1 us (31%)
  Pallas kernels  20 us (15%)
  local copies, waits for them, and re-layouts  10.5 us (8%)
  other arithmetic  4.86 us (4%)
    ppermute x4, starting transfers between devices, paired(): return lax.ppermute(value, axis, pairs)  29 us
    pallas_call x1, Pallas kernels, core(): pl.pallas_call(functools.partial(core_kernel, loss_scale=loss_scale), in_...  17.4 us
    all_to_all x1, waiting for transfers between devices, shards(): final = lax.all_to_all(last, 'lon', 0, 0, tiled=True)  15.7 us
    all_to_all x1, waiting for transfers between devices, shards(): lax.all_to_all(chunk, ('lat', 'lon'), 0, 0, axis_index_groups=columns, ti...  10.6 us
    all_to_all x1, starting transfers between devices, shards(): lax.all_to_all(slots, 'lon', 0, 0, tiled=True).reshape(lon_count * 8, 128)  9.19 us
    ppermute x4, waiting for transfers between devices, paired(): return lax.ppermute(value, axis, pairs)  9.12 us
    all_to_all x1, starting transfers between devices, shards(): lax.all_to_all(grads.reshape(32, 4, 128), 'lon', 0, 0, axis_index_groups=...  7.72 us
    all_to_all x1, waiting for transfers between devices, shards(): lax.all_to_all(grads.reshape(32, 4, 128), 'lon', 0, 0, axis_index_groups=...  6.62 us
  transfers between devices with their start and end apart: 8, of which 4 were waited for; matrix products, arithmetic and copies ran while one was open for 6% of the time, Pallas kernels for 2%

profile of v3, /device:TPU:1, one launch (start us, length us, event | category | flops | bytes accessed | tf_op | source)
XLA Modules:
  0.0 136.3 jit_solution(3485606577221302497)
XLA Ops:
  0.7 1.1 reshape.157
  1.8 0.1 copy.65
  1.9 0.0 copy-start.7
  2.0 8.8 %collective-permute-start = (bf16[4,24,512]{2,1,0:T(8,128)(2,1)S(1)}, bf16[4,24,512]{2,1,0:T(8,128)(2,1)S(1)}, u32[]{:S(2)}, u32[]{:S(2)}) collective-permute-start(bf16[4,24,512]{2,1,0:T(8,128)(2,1)S(1)} %get-tuple-element.15), channel_id=1, source_target_pairs={{0,1},{1,0},{2,3},{3,2},{4,5},{5,4},{6,7},{7,6},{8,9},{9,8},{10,11... | collective-permute-start | bytes 294920 | tf_op jit(solution)/shard_map/ppermute | solution.py:423
  10.8 10.0 %collective-permute-start.1 = (bf16[4,24,512]{2,1,0:T(8,128)(2,1)S(1)}, bf16[4,24,512]{2,1,0:T(8,128)(2,1)S(1)}, u32[]{:S(2)}, u32[]{:S(2)}) collective-permute-start(bf16[4,24,512]{2,1,0:T(8,128)(2,1)S(1)} %get-tuple-element.16), channel_id=1, source_target_pairs={{0,63},{1,2},{2,1},{3,4},{4,3},{5,6},{6,5},{7,8},{8,7},{9,10},{10,... | collective-permute-start | bytes 294920 | tf_op jit(solution)/shard_map/ppermute | solution.py:423
  20.8 0.0 copy-done.1
  20.8 0.8 fusion.3
  21.6 0.4 slice.102
  22.0 0.4 slice.101
  22.5 0.1 iota_compare_fusion.1
  22.6 0.1 bitcast_select_fusion.1
  22.8 0.8 pad_maximum_fusion
  23.6 9.2 %all-to-all-start = ((f32[64,8,128]{2,1,0:T(8,128)}), f32[64,8,128]{2,1,0:T(8,128)S(1)}, u32[]{:S(2)}, u32[]{:S(2)}) async-start(f32[64,8,128]{2,1,0:T(8,128)} %pad_maximum_fusion), calls=%async_computation | async-start | bytes 524288 | tf_op jit(solution)/shard_map/all_to_all | solution.py:478
  32.8 0.6 reshape.161.readout_ref
  33.4 0.7 pad.8.own_ref
  34.1 0.7 pad_add_fusion.flags_ref
  34.8 0.0 collective-permute-done.near_lon_ref
  34.8 0.0 collective-permute-done.1.far_lon_ref
  34.9 2.6 %collective-permute-start.2 = (bf16[4,24,512]{2,1,0:T(8,128)(2,1)S(1)}, bf16[4,24,512]{2,1,0:T(8,128)(2,1)S(1)}, u32[]{:S(2)}, u32[]{:S(2)}) collective-permute-start(bf16[4,24,512]{2,1,0:T(8,128)(2,1)S(1)} %get-tuple-element.17), channel_id=1, source_target_pairs={{0,64},{64,0},{128,192},{192,128},{256,320},{320,256},{384,448},{4... | collective-permute-start | bytes 294920 | tf_op jit(solution)/shard_map/ppermute | solution.py:423
  37.5 7.6 %collective-permute-start.3 = (bf16[4,24,512]{2,1,0:T(8,128)(2,1)S(1)}, bf16[4,24,512]{2,1,0:T(8,128)(2,1)S(1)}, u32[]{:S(2)}, u32[]{:S(2)}) collective-permute-start(bf16[4,24,512]{2,1,0:T(8,128)(2,1)S(1)} %get-tuple-element.18), channel_id=1, source_target_pairs={{0,448},{64,128},{128,64},{192,256},{256,192},{320,384},{384,320},... | collective-permute-start | bytes 294920 | tf_op jit(solution)/shard_map/ppermute | solution.py:423
  45.1 2.7 %ordered_bias.1.bias_hbm = f32[4,16,24,128]{3,2,1,0:T(8,128)} custom-call(f32[1152,72]{1,0:T(8,128)} %bitcast.106), custom_call_target="tpu_custom_call" | custom-call | flops 20000000000 | bytes 2000000 | tf_op jit(solution)/shard_map/ordered_bias/pallas_call | solution.py:60
  47.8 0.0 collective-permute-done.2.near_lat_ref
  47.8 9.1 %collective-permute-done.3.far_lat_ref = bf16[4,24,512]{2,1,0:T(8,128)(2,1)S(1)} collective-permute-done((bf16[4,24,512]{2,1,0:T(8,128)(2,1)S(1)}, bf16[4,24,512]{2,1,0:T(8,128)(2,1)S(1)}, u32[]{:S(2)}, u32[]{:S(2)}) %collective-permute-start.3) | collective-permute-done | bytes 98336 | tf_op jit(solution)/shard_map/ppermute | solution.py:423
  56.9 0.0 all-to-all-done
  56.9 0.6 copy-done.9
  57.6 0.1 copy-done
  57.7 17.4 %window_and_observe.1 = (bf16[192,512]{1,0:T(8,128)(2,1)}, f32[8,256]{1,0:T(8,128)}, f32[128,128]{1,0:T(8,128)}, f32[64,128]{1,0:T(8,128)}) custom-call(s32[4]{0:T(128)} %pad_add_fusion.flags_ref, bf16[2,4,24,512]{3,2,1,0:T(8,128)(2,1)} %pad.8.own_ref, bf16[4,24,512]{2,1,0:T(8,128)(2,1)} %copy-done.3, bf16[4,24,512]{2,1,0:T(8,128)(2,1)} %copy-done.4, ...), custom_call_target="tpu_custom_call" | custom-call | flops 3000000000 | bytes 8000000 | tf_op jit(solution)/shard_map/window_and_observe/pallas_call | solution.py:380
  75.0 7.7 %all-to-all-start.1 = ((f32[32,4,128]{2,1,0:T(4,128)}), f32[32,4,128]{2,1,0:T(4,128)S(1)}, u32[]{:S(2)}, u32[]{:S(2)}) async-start(f32[32,4,128]{2,1,0:T(4,128)} %bitcast.96), calls=%async_computation.1 | async-start | bytes 131072 | tf_op jit(solution)/shard_map/all_to_all | solution.py:506
  82.8 0.7 slice.104
  83.5 6.6 %all-to-all-done.1 = f32[32,4,128]{2,1,0:T(4,128)S(1)} async-done(((f32[32,4,128]{2,1,0:T(4,128)}), f32[32,4,128]{2,1,0:T(4,128)S(1)}, u32[]{:S(2)}, u32[]{:S(2)}) %all-to-all-start.1) | async-done | bytes 65568 | tf_op jit(solution)/shard_map/all_to_all | solution.py:506
  90.1 0.6 pad_maximum_fusion.4
  90.8 5.9 %all-to-all-start.2 = ((f32[16,4,128]{2,1,0:T(4,128)}), f32[16,4,128]{2,1,0:T(4,128)S(1)}, u32[]{:S(2)}, u32[]{:S(2)}) async-start(f32[16,4,128]{2,1,0:T(4,128)} %bitcast.30), calls=%async_computation.2 | async-start | bytes 65536 | tf_op jit(solution)/shard_map/all_to_all | solution.py:518
  96.7 0.7 slice_reduce_fusion.1
  97.4 0.1 reshape_squeeze.13
  97.5 10.6 %all-to-all-done.2 = f32[16,4,128]{2,1,0:T(4,128)S(1)} async-done(((f32[16,4,128]{2,1,0:T(4,128)}), f32[16,4,128]{2,1,0:T(4,128)S(1)}, u32[]{:S(2)}, u32[]{:S(2)}) %all-to-all-start.2) | async-done | bytes 32800 | tf_op jit(solution)/shard_map/all_to_all | solution.py:518
  108.1 0.1 reshape.170
  108.2 0.1 reshape_squeeze.14
  108.4 1.5 %pad_maximum_fusion.1 = f32[64,4,128]{2,1,0:T(4,128)} fusion(f32[64,1,128]{2,1,0:T(1,128)S(1)} %broadcast_in_dim.60, f32[64,1,128]{2,1,0:T(1,128)} %bitcast.100, f32[64,2,128]{2,1,0:T(2,128)S(1)} %broadcast_in_dim.57), kind=kLoop, calls=%fused_computation.11 | loop fusion | flops 65536 | bytes 262144 | tf_op jit(solution)/shard_map/concatenate | solution.py:527
  109.9 6.0 %all-to-all-start.3 = ((f32[64,4,128]{2,1,0:T(4,128)}), f32[64,4,128]{2,1,0:T(4,128)S(1)}, u32[]{:S(2)}, u32[]{:S(2)}) async-start(f32[64,4,128]{2,1,0:T(4,128)} %pad_maximum_fusion.1), calls=%async_computation.3 | async-start | bytes 262144 | tf_op jit(solution)/shard_map/all_to_all | solution.py:535
  116.0 1.0 copy.77
  117.0 0.7 reshape.166
  117.8 15.7 %all-to-all-done.3 = f32[64,4,128]{2,1,0:T(4,128)S(1)} async-done(((f32[64,4,128]{2,1,0:T(4,128)}), f32[64,4,128]{2,1,0:T(4,128)S(1)}, u32[]{:S(2)}, u32[]{:S(2)}) %all-to-all-start.3) | async-done | bytes 131104 | tf_op jit(solution)/shard_map/all_to_all | solution.py:535
  133.5 0.7 fusion.10
  134.2 0.6 copy.80
  134.9 0.6 copy.81
  135.5 0.1 stack_reshape.3
  135.6 0.1 reshape.171
  135.7 0.7 reshape.172
  (44 shorter events, 0.6 us)
Async XLA Ops:
  0.6 20.1 %copy-start.1 = (s32[1,1,64,4,128]{4,3,2,1,0:T(4,128)S(1)}, s32[1,1,64,4,128]{4,3,2,1,0:T(4,128)}, u32[]{:S(2)}) copy-start(s32[1,1,64,4,128]{4,3,2,1,0:T(4,128)} %param.18) | copy-start | bytes 393220
  0.6 21.8 %copy-start.6 = (s32[1,1,64]{2,1,0:T(1,128)S(1)}, s32[1,1,64]{2,1,0:T(1,128)}, u32[]{:S(2)}) copy-start(s32[1,1,64]{2,1,0:T(1,128)} %param.21) | copy-start | bytes 772
  0.7 21.9 %copy-start.5 = (f32[1,1,64,128]{3,2,1,0:T(8,128)S(1)}, f32[1,1,64,128]{3,2,1,0:T(8,128)}, u32[]{:S(2)}) copy-start(f32[1,1,64,128]{3,2,1,0:T(8,128)} %param.20) | copy-start | bytes 98308
  0.7 22.0 %copy-start.2 = (f32[1,1,64,4,128]{4,3,2,1,0:T(4,128)S(1)}, f32[1,1,64,4,128]{4,3,2,1,0:T(4,128)}, u32[]{:S(2)}) copy-start(f32[1,1,64,4,128]{4,3,2,1,0:T(4,128)} %param.19) | copy-start | bytes 393220
  1.9 30.9 %copy-start.7 = (bf16[512]{0:T(512)(128)(2,1)S(1)}, bf16[512]{0:T(512)(128)(2,1)}, u32[]{:S(2)}) copy-start(bf16[512]{0:T(512)(128)(2,1)} %param.17) | copy-start | bytes 3076
  2.0 32.8 %collective-permute-start = (bf16[4,24,512]{2,1,0:T(8,128)(2,1)S(1)}, bf16[4,24,512]{2,1,0:T(8,128)(2,1)S(1)}, u32[]{:S(2)}, u32[]{:S(2)}) collective-permute-start(bf16[4,24,512]{2,1,0:T(8,128)(2,1)S(1)} %get-tuple-element.15), channel_id=1, source_target_pairs={{0,1},{1,0},{2,3},{3,2},{4,5},{5,4},{6,7},{7,6},{8,9},{9,8},{10,11... | collective-permute-start | bytes 294920 | tf_op jit(solution)/shard_map/ppermute | solution.py:423
  10.8 24.0 %collective-permute-start.1 = (bf16[4,24,512]{2,1,0:T(8,128)(2,1)S(1)}, bf16[4,24,512]{2,1,0:T(8,128)(2,1)S(1)}, u32[]{:S(2)}, u32[]{:S(2)}) collective-permute-start(bf16[4,24,512]{2,1,0:T(8,128)(2,1)S(1)} %get-tuple-element.16), channel_id=1, source_target_pairs={{0,63},{1,2},{2,1},{3,4},{4,3},{5,6},{6,5},{7,8},{8,7},{9,10},{10,... | collective-permute-start | bytes 294920 | tf_op jit(solution)/shard_map/ppermute | solution.py:423
  23.6 33.3 %all-to-all-start = ((f32[64,8,128]{2,1,0:T(8,128)}), f32[64,8,128]{2,1,0:T(8,128)S(1)}, u32[]{:S(2)}, u32[]{:S(2)}) async-start(f32[64,8,128]{2,1,0:T(8,128)} %pad_maximum_fusion), calls=%async_computation | async-start | bytes 524288 | tf_op jit(solution)/shard_map/all_to_all | solution.py:478
  34.8 13.0 %copy-start.3 = (bf16[4,24,512]{2,1,0:T(8,128)(2,1)}, bf16[4,24,512]{2,1,0:T(8,128)(2,1)S(1)}, u32[]{:S(2)}) copy-start(bf16[4,24,512]{2,1,0:T(8,128)(2,1)S(1)} %collective-permute-done.near_lon_ref) | copy-start | bytes 294916
  34.8 13.0 %copy-start.4 = (bf16[4,24,512]{2,1,0:T(8,128)(2,1)}, bf16[4,24,512]{2,1,0:T(8,128)(2,1)S(1)}, u32[]{:S(2)}) copy-start(bf16[4,24,512]{2,1,0:T(8,128)(2,1)S(1)} %collective-permute-done.1.far_lon_ref) | copy-start | bytes 294916
  34.9 12.9 %collective-permute-start.2 = (bf16[4,24,512]{2,1,0:T(8,128)(2,1)S(1)}, bf16[4,24,512]{2,1,0:T(8,128)(2,1)S(1)}, u32[]{:S(2)}, u32[]{:S(2)}) collective-permute-start(bf16[4,24,512]{2,1,0:T(8,128)(2,1)S(1)} %get-tuple-element.17), channel_id=1, source_target_pairs={{0,64},{64,0},{128,192},{192,128},{256,320},{320,256},{384,448},{4... | collective-permute-start | bytes 294920 | tf_op jit(solution)/shard_map/ppermute | solution.py:423
  37.5 19.4 %collective-permute-start.3 = (bf16[4,24,512]{2,1,0:T(8,128)(2,1)S(1)}, bf16[4,24,512]{2,1,0:T(8,128)(2,1)S(1)}, u32[]{:S(2)}, u32[]{:S(2)}) collective-permute-start(bf16[4,24,512]{2,1,0:T(8,128)(2,1)S(1)} %get-tuple-element.18), channel_id=1, source_target_pairs={{0,448},{64,128},{128,64},{192,256},{256,192},{320,384},{384,320},... | collective-permute-start | bytes 294920 | tf_op jit(solution)/shard_map/ppermute | solution.py:423
  47.8 9.1 %copy-start.8 = (bf16[4,24,512]{2,1,0:T(8,128)(2,1)}, bf16[4,24,512]{2,1,0:T(8,128)(2,1)S(1)}, u32[]{:S(2)}) copy-start(bf16[4,24,512]{2,1,0:T(8,128)(2,1)S(1)} %collective-permute-done.2.near_lat_ref) | copy-start | bytes 294916
  56.9 0.6 copy-start.9
  56.9 0.7 copy-start
  75.0 15.0 %all-to-all-start.1 = ((f32[32,4,128]{2,1,0:T(4,128)}), f32[32,4,128]{2,1,0:T(4,128)S(1)}, u32[]{:S(2)}, u32[]{:S(2)}) async-start(f32[32,4,128]{2,1,0:T(4,128)} %bitcast.96), calls=%async_computation.1 | async-start | bytes 131072 | tf_op jit(solution)/shard_map/all_to_all | solution.py:506
  90.8 17.3 %all-to-all-start.2 = ((f32[16,4,128]{2,1,0:T(4,128)}), f32[16,4,128]{2,1,0:T(4,128)S(1)}, u32[]{:S(2)}, u32[]{:S(2)}) async-start(f32[16,4,128]{2,1,0:T(4,128)} %bitcast.30), calls=%async_computation.2 | async-start | bytes 65536 | tf_op jit(solution)/shard_map/all_to_all | solution.py:518
  109.9 23.6 %all-to-all-start.3 = ((f32[64,4,128]{2,1,0:T(4,128)}), f32[64,4,128]{2,1,0:T(4,128)S(1)}, u32[]{:S(2)}, u32[]{:S(2)}) async-start(f32[64,4,128]{2,1,0:T(4,128)} %pad_maximum_fusion.1), calls=%async_computation.3 | async-start | bytes 262144 | tf_op jit(solution)/shard_map/all_to_all | solution.py:535

commit v4 on v3

--- a/solution.py
+++ b/solution.py
@@ -14,7 +14,7 @@
 HEAD_DIM = 32
 MODEL = 512
 GROUP = 24
-SLOT = 32
+WINDOW = 4 * GROUP
 LIVE = 18
 OWN = 8 * GROUP
 NORM_EPS = 1e-05
@@ -32,22 +32,16 @@
     return mm(a, b, dims, precision=lax.Precision.HIGHEST)
 
 
-def own_slot(n):
-    half, row = n // 4, n % 4
-    window_row, part = (row + 1) // 2, (row + 1) % 2
-    return ((half * 3 + window_row) * 2 + (1 - half)) * 2 + part
-
-
 def bias_kernel(bias_ref, out_ref, wide_ref):
-    shape = (72, 128)
+    shape = (72, WINDOW)
     lane = lax.broadcasted_iota(jnp.int32, shape, 1)
-    row = lane % SLOT
-    column = 12 * (3 * ((lane // SLOT) % 2) + row // 6) + 6 * (lane // 64) + row % 6
+    row = lane % GROUP
+    column = 12 * (3 * ((lane // GROUP) % 2) + row // 6) + 6 * (lane // (2 * GROUP)) + row % 6
     hit = (column == lax.broadcasted_iota(jnp.int32, shape, 0)) & (row < LIVE)
     wide = exact(bias_ref[...], hit.astype(F32))
-    lanes = lax.broadcasted_iota(jnp.int32, (1, 128), 1)
-    wide = wide + jnp.where(lanes % SLOT < LIVE, 0.0, NEG)
-    wide_ref[...] = wide.reshape(HEADS, 72, 128)
+    lanes = lax.broadcasted_iota(jnp.int32, (1, WINDOW), 1)
+    wide = wide + jnp.where(lanes % GROUP < LIVE, 0.0, NEG)
+    wide_ref[...] = wide.reshape(HEADS, 72, WINDOW)
     out_ref[...] = jnp.zeros_like(out_ref)
     for parity in range(2):
         for half in range(2):
@@ -59,15 +53,48 @@
 def ordered_bias(bias):
     return pl.pallas_call(
         bias_kernel,
-        out_shape=jax.ShapeDtypeStruct((4, HEADS, GROUP, 128), F32),
-        scratch_shapes=[pltpu.VMEM((HEADS, 72, 128), F32)],
+        out_shape=jax.ShapeDtypeStruct((4, HEADS, GROUP, WINDOW), F32),
+        scratch_shapes=[pltpu.VMEM((HEADS, 72, WINDOW), F32)],
         cost_estimate=pl.CostEstimate(flops=2 * 10**10, bytes_accessed=2 * 10**6, transcendentals=0),
         name="ordered_bias",
     )(bias.reshape(HEADS * 72, 72))
 
 
+def slots_kernel(index_ref, weight_ref, value_ref, count_ref, out_ref):
+    strips = value_ref.shape[0]
+    square = (strips, strips)
+    own_lane = lax.broadcasted_iota(jnp.int32, square, 0) == lax.broadcasted_iota(jnp.int32, square, 1)
+    counts = jnp.broadcast_to(count_ref[...].astype(F32), square)
+    counts = jnp.sum(jnp.where(own_lane, counts, 0.0), axis=1, keepdims=True).astype(jnp.int32)
+    live = lax.broadcasted_iota(jnp.int32, (strips, 128), 1) < counts
+    places = []
+    for k in range(4):
+        cell = index_ref[pl.ds(k, strips, stride=4), :]
+        row = (cell * 171) >> 11
+        col = cell - 12 * row
+        group = (row * 11) >> 5
+        half = (col >= 6).astype(jnp.int32)
+        places.append((half * 4 + group) * GROUP + (row - 3 * group) * 6 + col - 6 * half)
+        weight = weight_ref[pl.ds(k, strips, stride=4), :]
+        out_ref[pl.ds(2 + k, strips, stride=8), :] = jnp.where(live, weight, 0.0)
+    for pair in range(2):
+        packed = places[2 * pair] + 1024 * places[2 * pair + 1]
+        out_ref[pl.ds(pair, strips, stride=8), :] = packed.astype(F32)
+    out_ref[pl.ds(6, strips, stride=8), :] = jnp.where(live, value_ref[...], 0.0)
+    out_ref[pl.ds(7, strips, stride=8), :] = jnp.zeros((strips, 128), F32)
+
+
+def packed_slots(index, weight, value, count):
+    return pl.pallas_call(
+        slots_kernel,
+        out_shape=jax.ShapeDtypeStruct((value.shape[0] * 8, 128), F32),
+        cost_estimate=pl.CostEstimate(flops=10**6, bytes_accessed=5 * 10**5, transcendentals=0),
+        name="packed_slots",
+    )(index, weight, value, count)
+
+
 def forward_part(
-    flags_ref,
+    lat_count,
     own_ref,
     near_lon_ref,
     far_lon_ref,
@@ -85,6 +112,8 @@
     gq_ref,
     low_ref,
     norm_ref,
+    own_norm_ref,
+    low_own_ref,
     w_ref,
     k_ref,
     v_ref,
@@ -103,32 +132,42 @@
     ]
     for load in loads:
         load.start()
-    even_lon = flags_ref[0] == 0
-    even_lat = flags_ref[1] == 0
-    first = flags_ref[2].astype(F32)
-    last = flags_ref[3].astype(F32)
+    lat = lax.axis_index("lat")
+    even_lon = lax.axis_index("lon") % 2 == 0
+    even_lat = lat % 2 == 0
+    first = (lat == 0).astype(F32)
+    last = (lat == lat_count - 1).astype(F32)
+
+    def padded(x):
+        return jnp.concatenate([x, jnp.zeros((GROUP - LIVE, MODEL), F32)], axis=0)
 
     def pick(cond, a, b):
         return jnp.where(cond, a.astype(F32), b.astype(F32))
 
+    def piece(strip, group):
+        if group == 0:
+            return pick(even_lat, far_lat_ref[strip], near_lat_ref[strip])
+        if group == 5:
+            return pick(even_lat, near_lat_ref[strip], far_lat_ref[strip])
+        if strip == 0:
+            return pick(even_lon, far_lon_ref[group - 1], near_lon_ref[group - 1])
+        if strip == 3:
+            return pick(even_lon, near_lon_ref[group - 1], far_lon_ref[group - 1])
+        return own_ref[strip - 1, group - 1].astype(F32)
+
     for strip in range(4):
-        for group in range(6):
-            if group == 0:
-                x = pick(even_lat, far_lat_ref[strip], near_lat_ref[strip])
-            elif group == 5:
-                x = pick(even_lat, near_lat_ref[strip], far_lat_ref[strip])
-            elif strip == 0:
-                x = pick(even_lon, far_lon_ref[group - 1], near_lon_ref[group - 1])
-            elif strip == 3:
-                x = pick(even_lon, near_lon_ref[group - 1], far_lon_ref[group - 1])
-            else:
-                x = own_ref[strip - 1, group - 1].astype(F32)
+        rows = []
+        for pair in range(3):
+            x = jnp.concatenate([padded(piece(strip, 2 * pair + i)) for i in range(2)], axis=0)
             center = x - jnp.mean(x, axis=1, keepdims=True)
             spread = jnp.mean(center * center, axis=1, keepdims=True)
             y = center * lax.rsqrt(spread + NORM_EPS)
-            y = jnp.concatenate([y, jnp.zeros((SLOT - GROUP, MODEL), F32)], axis=0).astype(BF16)
-            slot = (((strip // 2) * 3 + group // 2) * 2 + strip % 2) * 2 + group % 2
-            norm_ref[slot * SLOT : (slot + 1) * SLOT, :] = y
+            at = ((strip // 2) * 3 + pair) * WINDOW + (strip % 2) * 2 * GROUP
+            norm_ref[at : at + 2 * GROUP, :] = y.astype(BF16)
+            rows.append(y)
+        if strip in (1, 2):
+            mine = jnp.concatenate([rows[0][GROUP:], rows[1], rows[2][:GROUP]], axis=0)
+            own_norm_ref[(strip - 1) * 4 * GROUP : strip * 4 * GROUP, :] = mine.astype(BF16)
 
     normed = norm_ref[...]
     for load in loads:
@@ -141,9 +180,9 @@
     low_ref[...] = low
     k_ref[...] = mm(normed, qkv_ref[:, MODEL : 2 * MODEL]).astype(BF16)
     v_ref[...] = (mm(normed, qkv_ref[:, 2 * MODEL :]) + mm(low, up_value)).astype(BF16)
-    own_rows = [slice(own_slot(n) * SLOT, (own_slot(n) + 1) * SLOT) for n in range(8)]
-    normed_own = jnp.concatenate([norm_ref[rows, :] for rows in own_rows], axis=0)
-    low_own = jnp.concatenate([low_ref[rows, :] for rows in own_rows], axis=0)
+    normed_own = own_norm_ref[...]
+    low_own = mm(normed_own, down_ref[...], NT).astype(BF16)
+    low_own_ref[...] = low_own.astype(F32)
     query = mm(normed_own, qkv_ref[:, :MODEL]) + mm(low_own, up_query)
     q_ref[...] = query.astype(BF16).astype(F32)
 
@@ -154,9 +193,11 @@
     scale = 1.0 / math.sqrt(HEAD_DIM)
     head_of = lax.broadcasted_iota(jnp.int32, (8, 1, 256), 2) // HEAD_DIM
     head_mask = head_of == lax.broadcasted_iota(jnp.int32, (8, 1, 256), 0)
-    lane_part = (lax.broadcasted_iota(jnp.int32, (1, 128), 1) // SLOT) % 2
+    lane_part = (lax.broadcasted_iota(jnp.int32, (1, WINDOW), 1) // GROUP) % 2
     masked_first = jnp.where(lane_part == 0, NEG * first, 0.0)
     masked_last = jnp.where(lane_part == 1, NEG * last, 0.0)
+
+    ones = jnp.ones((WINDOW, WINDOW), BF16)
 
     def fold(rows):
         return jnp.sum(jnp.where(head_mask, rows.reshape(8, GROUP, 256), 0.0), axis=0)
@@ -164,13 +205,13 @@
     for n in range(8):
         half, row = n // 4, n % 4
         window = half * 3 + (row + 1) // 2
-        keys = slice(window * 128, (window + 1) * 128)
+        keys = slice(window * WINDOW, (window + 1) * WINDOW)
         for part in range(2):
             cols = slice(256 * part, 256 * (part + 1))
             k_win, v_win = k_ref[keys, cols], v_ref[keys, cols]
-            q_own = q_ref[n * SLOT : n * SLOT + GROUP, cols]
+            q_own = q_ref[n * GROUP : (n + 1) * GROUP, cols]
             lhs = jnp.where(head_mask, q_own[None], 0.0).reshape(8 * GROUP, 256).astype(BF16)
-            bias = bias_ref[(row % 2) * 2 + half, 8 * part : 8 * part + 8].reshape(8 * GROUP, 128)
+            bias = bias_ref[(row % 2) * 2 + half, 8 * part : 8 * part + 8].reshape(8 * GROUP, WINDOW)
             scores = mm(lhs, k_win, NT) * scale + bias
             if row == 0:
                 scores = scores + masked_first
@@ -185,13 +226,17 @@
             w_high = w_masked.astype(BF16).astype(F32)
             w_pair = jnp.concatenate([w_high, w_masked - w_high], axis=0).astype(BF16)
             v_pair = mm(w_pair, v_win, NT)
-            v_w = (v_pair[:8] + v_pair[8:]).reshape(8, 1, 128)
-            probs3 = probs.reshape(8, GROUP, 128)
-            mean = jnp.sum(probs3 * v_w, axis=2, keepdims=True)
-            slope = (probs3 * (v_w - mean) * scale).reshape(8 * GROUP, 128).astype(BF16)
+            v_w = (v_pair[:8] + v_pair[8:]).reshape(8, 1, WINDOW)
+            v_w = jnp.broadcast_to(v_w, (8, GROUP, WINDOW)).reshape(8 * GROUP, WINDOW)
+            share = probs * v_w
+            share_high = share.astype(BF16)
+            share_low = (share - share_high.astype(F32)).astype(BF16)
+            mean = jnp.sum(share, axis=1, keepdims=True)
+            slope = (probs * (v_w - mean) * scale).astype(BF16)
             gq_ref[n * GROUP : (n + 1) * GROUP, cols] = fold(mm(slope, k_win))
 
-    x_own = own_ref[...].astype(F32).reshape(OWN, MODEL)
+    x_own = [padded(own_ref[n // 4, n % 4].astype(F32)) for n in range(8)]
+    x_own = jnp.concatenate(x_own, axis=0)
     out = (x_own + mm(att_ref[...].astype(BF16), wo_ref[...])).astype(BF16)
     block_ref[...] = out
     field_ref[...] = jnp.zeros_like(field_ref)
@@ -205,6 +250,8 @@
     gq_ref,
     low_ref,
     norm_ref,
+    own_norm_ref,
+    low_own_ref,
     w_ref,
     up_ref,
     adjoint_ref,
@@ -234,49 +281,67 @@
     innov = predicted - slots_ref[pl.ds(6, sources, stride=8), :]
     innov_ref[...] = innov
     for k in range(4):
-        term_ref[k * sources : (k + 1) * sources, :] = weights[k] * innov
-        place_ref[k * sources : (k + 1) * sources, :] = places[k]
-
-    cell = lax.broadcasted_iota(jnp.int32, (OWN, 128), 0)
+        rows = slice(k * sources, (k + 1) * sources)
+        term = weights[k] * innov
+        high = term.astype(BF16).astype(F32)
+        term_ref[0, rows, :] = high
+        term_ref[1, rows, :] = term - high
+        place_ref[0, rows, :] = places[k] >> 4
+        place_ref[1, rows, :] = places[k] & 15
+
+    digit = lax.broadcasted_iota(jnp.int32, (16, 128), 0)
+    per_step = 32
 
     def add_rows(step, total):
-        for inner in range(8):
-            at = step * 8 + inner
-            hit = cell == place_ref[pl.ds(at, 1), :]
-            total = total + jnp.where(hit, term_ref[pl.ds(at, 1), :], 0.0)
-        return total
-
-    total = lax.fori_loop(0, 4 * sources // 8, add_rows, jnp.zeros((OWN, 128), F32))
-    adjoint = jnp.sum(total, axis=1, keepdims=True)
+        left, right = [], []
+        for inner in range(per_step):
+            at = pl.ds(step * per_step + inner, 1)
+            left.append(jnp.where(digit == place_ref[0, at, :], 1.0, 0.0).astype(BF16))
+            hit = digit == place_ref[1, at, :]
+            terms = [jnp.where(hit, term_ref[i, at, :], 0.0) for i in range(2)]
+            right.append(jnp.concatenate(terms, axis=0).astype(BF16))
+        return total + mm(jnp.concatenate(left, axis=1), jnp.concatenate(right, axis=1), NT)
+
+    total = lax.fori_loop(0, 4 * sources // per_step, add_rows, jnp.zeros((16, 32), F32))
+    total = total[:, :16] + total[:, 16:]
+
+    def cells(shape, axis):
+        cell = lax.broadcasted_iota(jnp.int32, shape, axis)
+        digits = lax.broadcasted_iota(jnp.int32, shape, 1 - axis)
+        return cell // 16 == digits, cell % 16 == digits
+
+    high, low = cells((OWN, 16), 0)
+    column = exact(high.astype(F32), total)
+    adjoint = jnp.sum(jnp.where(low, column, 0.0), axis=1, keepdims=True)
+    high, low = cells((16, OWN), 1)
+    row = jnp.sum(jnp.where(high, exact(total, low.astype(F32)), 0.0), axis=0, keepdims=True)
     adjoint_ref[...] = jnp.zeros_like(adjoint_ref)
-    adjoint_ref[:, :OWN] = exact(jnp.ones((8, 128), F32), total, NT)
-
-    def own_of(ref):
-        blocks = [ref[own_slot(n) * SLOT : (own_slot(n) + 1) * SLOT, :].astype(F32)[:GROUP] for n in range(8)]
-        return jnp.concatenate(blocks, axis=0)
+    adjoint_ref[0:1, :OWN] = row
 
     factor = 0.5 * loss_scale
     g_query = gq_ref[...].astype(BF16)
     up = up_ref[...]
     grad_low = mm(g_query, up, NT)
-    up_query = mm((own_of(low_ref) * adjoint).astype(BF16), g_query, TN)
-    down_query = mm((grad_low * adjoint).astype(BF16), own_of(norm_ref).astype(BF16), TN)
+    up_query = mm((low_own_ref[...] * adjoint).astype(BF16), g_query, TN)
+    down_query = mm((grad_low * adjoint).astype(BF16), own_norm_ref[...], TN)
 
     weighted = [None] * 6
     for n in range(8):
         window = (n // 4) * 3 + (n % 4 + 1) // 2
-        probs = probs_ref[n].astype(F32).reshape(HEADS, GROUP, 128)
+        probs = probs_ref[n].astype(F32).reshape(HEADS, GROUP, WINDOW)
         part = jnp.sum(probs * adjoint[n * GROUP : (n + 1) * GROUP].reshape(1, GROUP, 1), axis=1)
         weighted[window] = part if weighted[window] is None else weighted[window] + part
-    weighted = jnp.concatenate(weighted, axis=1)
     head = lax.broadcasted_iota(jnp.int32, (HEADS, MODEL), 0)
     of_head = head == lax.broadcasted_iota(jnp.int32, (HEADS, MODEL), 1) // HEAD_DIM
     w_masked = jnp.where(of_head, jnp.broadcast_to(w_ref[0:1, :], (HEADS, MODEL)), 0.0)
     rank_head = exact(up.astype(F32), w_masked, NT)
-    weighted_bf = weighted.astype(BF16)
-    sums = mm(weighted_bf, low_ref[...])
+    sums, down_value = jnp.zeros((HEADS, 16), F32), jnp.zeros((16, MODEL), F32)
+    for window in range(6):
+        keys = slice(window * WINDOW, (window + 1) * WINDOW)
+        sums = sums + mm(weighted[window].astype(BF16), low_ref[keys, :])
+        of_rank = exact(rank_head, weighted[window])
+        down_value = down_value + mm(of_rank.astype(BF16), norm_ref[keys, :])
     up_value = exact(sums, w_masked, TN)
-    down_value = mm(exact(rank_head, weighted).astype(BF16), norm_ref[...])
 
     parts = (up_query[:8], up_value[8:], down_query[:8], down_value[8:])
     for m, part in enumerate(parts):
@@ -286,7 +351,6 @@
 
 
 def core_kernel(
-    flags_ref,
     own_ref,
     near_lon_ref,
     far_lon_ref,
@@ -308,6 +372,8 @@
     gq_ref,
     low_ref,
     norm_ref,
+    own_norm_ref,
+    low_own_ref,
     w_ref,
     k_ref,
     v_ref,
@@ -321,12 +387,13 @@
     place_ref,
     slots_ref,
     loss_scale,
+    lat_count,
 ):
     slot_load = pltpu.make_async_copy(slots_hbm, slots_ref, copy_sems.at[3])
     slot_load.start()
     forward_part(
-        flags_ref,
-        own_ref,
+        lat_count,
+            own_ref,
         near_lon_ref,
         far_lon_ref,
         near_lat_ref,
@@ -343,6 +410,8 @@
         gq_ref,
         low_ref,
         norm_ref,
+        own_norm_ref,
+        low_own_ref,
         w_ref,
         k_ref,
         v_ref,
@@ -361,6 +430,8 @@
         gq_ref,
         low_ref,
         norm_ref,
+        own_norm_ref,
+        low_own_ref,
         w_ref,
         up_ref,
         adjoint_ref,
@@ -372,14 +443,13 @@
     )
 
 
-def core(flags, own, halos, qkv, wo, down, up, readout, bias, slots, loss_scale):
+def core(own, halos, qkv, wo, down, up, readout, bias, slots, loss_scale, lat_count):
     sources = slots.shape[0] // 8
     shape = jax.ShapeDtypeStruct
     vmem, far = pl.BlockSpec(memory_space=pltpu.VMEM), pl.BlockSpec(memory_space=pl.ANY)
-    smem = pl.BlockSpec(memory_space=pltpu.SMEM)
     return pl.pallas_call(
-        functools.partial(core_kernel, loss_scale=loss_scale),
-        in_specs=[smem] + [vmem] * 5 + [far] * 2 + [vmem] * 3 + [far] * 2,
+        functools.partial(core_kernel, loss_scale=loss_scale, lat_count=lat_count),
+        in_specs=[vmem] * 5 + [far] * 2 + [vmem] * 3 + [far] * 2,
         out_specs=[vmem] * 4,
         out_shape=[
             shape((OWN, MODEL), BF16),
@@ -389,21 +459,23 @@
         ],
         scratch_shapes=[
             pltpu.VMEM((8, 256), F32),
-            pltpu.VMEM((8, HEADS * GROUP, 128), BF16),
+            pltpu.VMEM((8, HEADS * GROUP, WINDOW), BF16),
             pltpu.VMEM((OWN, MODEL), F32),
-            pltpu.VMEM((24 * SLOT, 16), BF16),
-            pltpu.VMEM((24 * SLOT, MODEL), BF16),
+            pltpu.VMEM((6 * WINDOW, 16), BF16),
+            pltpu.VMEM((6 * WINDOW, MODEL), BF16),
+            pltpu.VMEM((OWN, MODEL), BF16),
+            pltpu.VMEM((OWN, 16), F32),
             pltpu.VMEM((8, MODEL), F32),
-            pltpu.VMEM((24 * SLOT, MODEL), BF16),
-            pltpu.VMEM((24 * SLOT, MODEL), BF16),
-            pltpu.VMEM((8 * SLOT, MODEL), F32),
+            pltpu.VMEM((6 * WINDOW, MODEL), BF16),
+            pltpu.VMEM((6 * WINDOW, MODEL), BF16),
+            pltpu.VMEM((OWN, MODEL), F32),
             pltpu.VMEM((OWN, MODEL), F32),
             pltpu.VMEM((MODEL, 3 * MODEL), BF16),
             pltpu.VMEM((MODEL, MODEL), BF16),
-            pltpu.VMEM((4, HEADS, GROUP, 128), F32),
+            pltpu.VMEM((4, HEADS, GROUP, WINDOW), F32),
             pltpu.SemaphoreType.DMA((4,)),
-            pltpu.VMEM((4 * sources, 128), F32),
-            pltpu.VMEM((4 * sources, 128), jnp.int32),
+            pltpu.VMEM((2, 4 * sources, 128), F32),
+            pltpu.VMEM((2, 4 * sources, 128), jnp.int32),
             pltpu.VMEM((sources * 8, 128), F32),
         ],
         compiler_params=pltpu.CompilerParams(vmem_limit_bytes=58 * 1024 * 1024),
@@ -411,7 +483,7 @@
             flops=3 * 10**9, bytes_accessed=8 * 10**6, transcendentals=4 * 10**5
         ),
         name="window_and_observe",
-    )(flags, own, *halos, qkv, wo, down, up, readout, bias, slots)
+    )(own, *halos, qkv, wo, down, up, readout, bias, slots)
 
 
 def paired(value, axis, odd_first):
@@ -441,7 +513,7 @@
     even_lat, even_lon = lat % 2 == 0, lon % 2 == 0
 
     own = tokens.reshape(4, 3, 2, 6, MODEL).transpose(2, 0, 1, 3, 4).reshape(2, 4, LIVE, MODEL)
-    own = jnp.pad(own, ((0, 0), (0, 0), (0, GROUP - LIVE), (0, 0)))
+    own = lax.optimization_barrier(own)
     near_send, far_send, observation_index = lax.optimization_barrier(
         (
             jnp.where(even_lon, own[1], own[0]),
@@ -452,37 +524,30 @@
     near_lon = paired(near_send, "lon", False)
     far_lon = paired(far_send, "lon", True)
 
-    patch_row, patch_col = observation_index[0, 0] // 12, observation_index[0, 0] % 12
-    place = ((patch_col // 6) * 4 + patch_row // 3) * GROUP + (patch_row % 3) * 6 + patch_col % 6
-    live = jnp.arange(128, dtype=jnp.int32)[None, :] < observation_count[0, 0][:, None]
-    slots = jnp.concatenate(
-        [
-            (place[:, 0::2] + 1024 * place[:, 1::2]).astype(F32),
-            jnp.where(live[:, None, :], observation_weight[0, 0], 0.0),
-            jnp.where(live[:, None, :], observation_value[0, 0][:, None, :], 0.0),
-            jnp.zeros((lon_count, 1, 128), F32),
-        ],
-        axis=1,
-    )
+    slots = packed_slots(
+        observation_index.reshape(lon_count * 4, 128),
+        observation_weight.reshape(lon_count * 4, 128),
+        observation_value.reshape(lon_count, 128),
+        observation_count.reshape(1, lon_count),
+    ).reshape(lon_count, 8, 128)
+
     left = jnp.where(even_lon, far_lon, near_lon)
     right = jnp.where(even_lon, near_lon, far_lon)
     top = jnp.stack([left[0], own[0, 0], own[1, 0], right[0]])
     bottom = jnp.stack([left[3], own[0, 3], own[1, 3], right[3]])
     near_send = jnp.where(even_lat, bottom, top)
     far_send = jnp.where(even_lat, top, bottom)
-    near_send, far_send, bias = lax.optimization_barrier(
-        (near_send, far_send, relative_position_bias)
+    near_send, far_send, bias, readout = lax.optimization_barrier(
+        (near_send, far_send, relative_position_bias, readout)
     )
     near_lat = paired(near_send, "lat", False)
     far_lat = paired(far_send, "lat", True)
     slots = lax.all_to_all(slots, "lon", 0, 0, tiled=True).reshape(lon_count * 8, 128)
 
-    flags = jnp.stack([lon % 2, lat % 2, lat == 0, lat == lat_count - 1]).astype(jnp.int32)
     down_rows = adapter_down_map.reshape(16, MODEL)
     up_rows = adapter_up_map.reshape(16, MODEL)
     loss_scale = 1.0 / math.sqrt(lat_count * lon_count)
     block, adjoint, grads, innov = core(
-        flags,
         own,
         (near_lon, far_lon, near_lat, far_lat),
         query_key_value_weight,
@@ -493,6 +558,7 @@
         ordered_bias(bias),
         slots,
         loss_scale,
+        lat_count,
     )
     block = block.reshape(2, 4, GROUP, MODEL)[:, :, :LIVE].reshape(2, 4, 3, 6, MODEL)
     block_out = block.transpose(1, 2, 0, 3, 4).reshape(12, 12, MODEL)

time: 137 us -> 132 us (0.964)
  starting transfers between devices: 57.8 us -> 60.9 us
  waiting for transfers between devices: 42.1 us -> 39.1 us
  other arithmetic: 4.86 us -> 2.32 us
  local copies, waits for them, and re-layouts: 10.5 us -> 8.86 us
    ppermute x4, waiting for transfers between devices: 9.12 us -> 6.1 us  [paired(): return lax.ppermute(value, axis, pairs)]
    all_to_all x1, starting transfers between devices: 7.72 us -> 10.4 us  [shards(): lax.all_to_all(grads.reshape(32, 4, 128), 'lon', 0, 0, axis_index_groups=...]
    pallas_call x1 -> x2, Pallas kernels: 17.4 us -> 16.2 us  [the longest x1 14.3 us: core(): pl.pallas_call(functools.partial(core_kernel, loss_scale=loss_scale, lat_...]
  transfers between devices with their start and end apart: 8 -> 8, of which waited for: 4 -> 5; matrix products, arithmetic and copies ran while one was open for 6% -> 3% of each run, Pallas kernels for 2% -> 3%
where the time goes in v4:
time: 132 us; the launch traced here: 131 us
  starting transfers between devices  60.9 us (46%)
  waiting for transfers between devices  39.1 us (30%)
  Pallas kernels  18.9 us (14%)
  local copies, waits for them, and re-layouts  8.86 us (7%)
  other arithmetic  2.32 us (2%)
    ppermute x4, starting transfers between devices, paired(): return lax.ppermute(value, axis, pairs)  29 us
    all_to_all x1, waiting for transfers between devices, shards(): final = lax.all_to_all(last, 'lon', 0, 0, tiled=True)  15.7 us
    pallas_call x1, Pallas kernels, core(): pl.pallas_call(functools.partial(core_kernel, loss_scale=loss_scale, lat_...  14.3 us
    all_to_all x1, waiting for transfers between devices, shards(): lax.all_to_all(chunk, ('lat', 'lon'), 0, 0, axis_index_groups=columns, ti...  10.6 us
    all_to_all x1, starting transfers between devices, shards(): lax.all_to_all(grads.reshape(32, 4, 128), 'lon', 0, 0, axis_index_groups=...  10.4 us
    all_to_all x1, starting transfers between devices, shards(): lax.all_to_all(slots, 'lon', 0, 0, tiled=True).reshape(lon_count * 8, 128)  9.18 us
    all_to_all x1, waiting for transfers between devices, shards(): lax.all_to_all(grads.reshape(32, 4, 128), 'lon', 0, 0, axis_index_groups=...  6.62 us
    all_to_all x1, starting transfers between devices, shards(): lax.all_to_all(chunk, ('lat', 'lon'), 0, 0, axis_index_groups=columns, ti...  6.36 us
  transfers between devices with their start and end apart: 8, of which 5 were waited for; matrix products, arithmetic and copies ran while one was open for 3% of the time, Pallas kernels for 3%

profile of v4, /device:TPU:1, one launch (start us, length us, event | category | flops | bytes accessed | tf_op | source)
XLA Modules:
  0.0 131.0 jit_solution(16953925739770114055)
XLA Ops:
  0.6 1.0 reshape.98
  1.6 0.1 copy.83
  1.8 0.0 copy-start
  1.8 8.8 %collective-permute-start = (bf16[4,18,512]{2,1,0:T(8,128)(2,1)S(1)}, bf16[4,18,512]{2,1,0:T(8,128)(2,1)S(1)}, u32[]{:S(2)}, u32[]{:S(2)}) collective-permute-start(bf16[4,18,512]{2,1,0:T(8,128)(2,1)S(1)} %get-tuple-element.16), channel_id=1, source_target_pairs={{0,1},{1,0},{2,3},{3,2},{4,5},{5,4},{6,7},{7,6},{8,9},{9,8},{10,11... | collective-permute-start | bytes 221192 | tf_op jit(solution)/shard_map/ppermute | solution.py:495
  10.6 10.0 %collective-permute-start.1 = (bf16[4,18,512]{2,1,0:T(8,128)(2,1)S(1)}, bf16[4,18,512]{2,1,0:T(8,128)(2,1)S(1)}, u32[]{:S(2)}, u32[]{:S(2)}) collective-permute-start(bf16[4,18,512]{2,1,0:T(8,128)(2,1)S(1)} %get-tuple-element.17), channel_id=1, source_target_pairs={{0,63},{1,2},{2,1},{3,4},{4,3},{5,6},{6,5},{7,8},{8,7},{9,10},{10,... | collective-permute-start | bytes 221192 | tf_op jit(solution)/shard_map/ppermute | solution.py:495
  20.6 1.8 %packed_slots.1 = f32[512,128]{1,0:T(8,128)} custom-call(s32[256,128]{1,0:T(8,128)} %bitcast.62, f32[256,128]{1,0:T(8,128)} %bitcast.63, f32[64,128]{1,0:T(8,128)} %bitcast.68, s32[1,64]{1,0:T(1,128)} %bitcast.76), custom_call_target="tpu_custom_call" | custom-call | flops 1000000 | bytes 500000 | tf_op jit(solution)/shard_map/packed_slots/pallas_call | solution.py:88
  22.4 9.2 %all-to-all-start = ((f32[64,8,128]{2,1,0:T(8,128)}), f32[64,8,128]{2,1,0:T(8,128)S(1)}, u32[]{:S(2)}, u32[]{:S(2)}) async-start(f32[64,8,128]{2,1,0:T(8,128)} %bitcast.55), calls=%async_computation | async-start | bytes 524288 | tf_op jit(solution)/shard_map/all_to_all | solution.py:545
  31.7 0.0 collective-permute-done.near_lon_ref
  31.7 0.0 copy-start.2
  31.7 0.0 collective-permute-done.1.far_lon_ref
  31.7 0.0 copy-start.3
  31.8 2.6 %collective-permute-start.2 = (bf16[4,18,512]{2,1,0:T(8,128)(2,1)S(1)}, bf16[4,18,512]{2,1,0:T(8,128)(2,1)S(1)}, u32[]{:S(2)}, u32[]{:S(2)}) collective-permute-start(bf16[4,18,512]{2,1,0:T(8,128)(2,1)S(1)} %get-tuple-element.18), channel_id=1, source_target_pairs={{0,64},{64,0},{128,192},{192,128},{256,320},{320,256},{384,448},{4... | collective-permute-start | bytes 221192 | tf_op jit(solution)/shard_map/ppermute | solution.py:495
  34.5 7.6 %collective-permute-start.3 = (bf16[4,18,512]{2,1,0:T(8,128)(2,1)S(1)}, bf16[4,18,512]{2,1,0:T(8,128)(2,1)S(1)}, u32[]{:S(2)}, u32[]{:S(2)}) collective-permute-start(bf16[4,18,512]{2,1,0:T(8,128)(2,1)S(1)} %get-tuple-element.19), channel_id=1, source_target_pairs={{0,448},{64,128},{128,64},{192,256},{256,192},{320,384},{384,320},... | collective-permute-start | bytes 221192 | tf_op jit(solution)/shard_map/ppermute | solution.py:495
  42.0 0.0 copy-start.4
  42.0 2.7 %ordered_bias.1.bias_hbm = f32[4,16,24,96]{3,2,1,0:T(8,128)} custom-call(f32[1152,72]{1,0:T(8,128)} %bitcast.77), custom_call_target="tpu_custom_call" | custom-call | flops 20000000000 | bytes 2000000 | tf_op jit(solution)/shard_map/ordered_bias/pallas_call | solution.py:54
  44.7 0.0 copy-done
  44.7 0.0 copy-done.2
  44.7 0.0 copy-done.3
  44.7 0.0 copy-done.4
  44.7 0.6 reshape.102.readout_ref
  45.3 0.9 collective-permute-done.2.near_lat_ref
  46.2 5.2 %collective-permute-done.3.far_lat_ref = bf16[4,18,512]{2,1,0:T(8,128)(2,1)S(1)} collective-permute-done((bf16[4,18,512]{2,1,0:T(8,128)(2,1)S(1)}, bf16[4,18,512]{2,1,0:T(8,128)(2,1)S(1)}, u32[]{:S(2)}, u32[]{:S(2)}) %collective-permute-start.3) | collective-permute-done | bytes 73760 | tf_op jit(solution)/shard_map/ppermute | solution.py:495
  51.4 0.0 all-to-all-done
  51.4 0.0 copy-done.5
  51.4 0.6 copy-done.6
  52.1 0.1 copy-done.1
  52.2 14.3 %window_and_observe.1 = (bf16[192,512]{1,0:T(8,128)(2,1)}, f32[8,256]{1,0:T(8,128)}, f32[128,128]{1,0:T(8,128)}, f32[64,128]{1,0:T(8,128)}) custom-call(bf16[2,4,18,512]{3,2,1,0:T(8,128)(2,1)} %copy-done, bf16[4,18,512]{2,1,0:T(8,128)(2,1)} %copy-done.2, bf16[4,18,512]{2,1,0:T(8,128)(2,1)} %copy-done.3, bf16[4,18,512]{2,1,0:T(8,128)(2,1)} %copy-done.5, ...), custom_call_target="tpu_custom_call" | custom-call | flops 3000000000 | bytes 8000000 | tf_op jit(solution)/shard_map/window_and_observe/pallas_call | solution.py:450
  66.6 10.4 %all-to-all-start.1 = ((f32[32,4,128]{2,1,0:T(4,128)}), f32[32,4,128]{2,1,0:T(4,128)S(1)}, u32[]{:S(2)}, u32[]{:S(2)}) async-start(f32[32,4,128]{2,1,0:T(4,128)} %bitcast.67), calls=%async_computation.1 | async-start | bytes 131072 | tf_op jit(solution)/shard_map/all_to_all | solution.py:572
  76.9 0.7 slice.96
  77.6 6.6 %all-to-all-done.1 = f32[32,4,128]{2,1,0:T(4,128)S(1)} async-done(((f32[32,4,128]{2,1,0:T(4,128)}), f32[32,4,128]{2,1,0:T(4,128)S(1)}, u32[]{:S(2)}, u32[]{:S(2)}) %all-to-all-start.1) | async-done | bytes 65568 | tf_op jit(solution)/shard_map/all_to_all | solution.py:572
  84.3 0.6 pad_maximum_fusion.3
  84.9 6.4 %all-to-all-start.2 = ((f32[16,4,128]{2,1,0:T(4,128)}), f32[16,4,128]{2,1,0:T(4,128)S(1)}, u32[]{:S(2)}, u32[]{:S(2)}) async-start(f32[16,4,128]{2,1,0:T(4,128)} %bitcast.23), calls=%async_computation.2 | async-start | bytes 65536 | tf_op jit(solution)/shard_map/all_to_all | solution.py:584
  91.4 0.7 slice_reduce_fusion.1
  92.1 0.1 reshape_squeeze.13
  92.2 10.6 %all-to-all-done.2 = f32[16,4,128]{2,1,0:T(4,128)S(1)} async-done(((f32[16,4,128]{2,1,0:T(4,128)}), f32[16,4,128]{2,1,0:T(4,128)S(1)}, u32[]{:S(2)}, u32[]{:S(2)}) %all-to-all-start.2) | async-done | bytes 32800 | tf_op jit(solution)/shard_map/all_to_all | solution.py:584
  102.8 0.1 reshape.116
  102.9 0.1 reshape_squeeze.14
  103.1 1.5 %pad_maximum_fusion = f32[64,4,128]{2,1,0:T(4,128)} fusion(f32[64,1,128]{2,1,0:T(1,128)S(1)} %broadcast_in_dim.37, f32[64,1,128]{2,1,0:T(1,128)} %bitcast.72, f32[64,2,128]{2,1,0:T(2,128)S(1)} %broadcast_in_dim.34), kind=kLoop, calls=%fused_computation | loop fusion | flops 65536 | bytes 262144 | tf_op jit(solution)/shard_map/concatenate | solution.py:593
  104.6 6.0 %all-to-all-start.3 = ((f32[64,4,128]{2,1,0:T(4,128)}), f32[64,4,128]{2,1,0:T(4,128)S(1)}, u32[]{:S(2)}, u32[]{:S(2)}) async-start(f32[64,4,128]{2,1,0:T(4,128)} %pad_maximum_fusion), calls=%async_computation.3 | async-start | bytes 262144 | tf_op jit(solution)/shard_map/all_to_all | solution.py:601
  110.7 1.0 copy.99
  111.7 0.7 reshape.112
  112.4 15.7 %all-to-all-done.3 = f32[64,4,128]{2,1,0:T(4,128)S(1)} async-done(((f32[64,4,128]{2,1,0:T(4,128)}), f32[64,4,128]{2,1,0:T(4,128)S(1)}, u32[]{:S(2)}, u32[]{:S(2)}) %all-to-all-start.3) | async-done | bytes 131104 | tf_op jit(solution)/shard_map/all_to_all | solution.py:601
  128.2 0.7 fusion.1
  128.9 0.6 copy.102
  129.5 0.6 copy.103
  130.1 0.1 stack_reshape.3
  130.2 0.1 reshape.117
  130.3 0.7 reshape.118
  (28 shorter events, 0.4 us)
Async XLA Ops:
  1.8 42.9 %copy-start = (bf16[2,4,18,512]{3,2,1,0:T(8,128)(2,1)}, bf16[2,4,18,512]{3,2,1,0:T(8,128)(2,1)S(1)}, u32[]{:S(2)}) copy-start(bf16[2,4,18,512]{3,2,1,0:T(8,128)(2,1)S(1)} %copy.90.own_ref) | copy-start | bytes 442372
  1.8 29.8 %collective-permute-start = (bf16[4,18,512]{2,1,0:T(8,128)(2,1)S(1)}, bf16[4,18,512]{2,1,0:T(8,128)(2,1)S(1)}, u32[]{:S(2)}, u32[]{:S(2)}) collective-permute-start(bf16[4,18,512]{2,1,0:T(8,128)(2,1)S(1)} %get-tuple-element.16), channel_id=1, source_target_pairs={{0,1},{1,0},{2,3},{3,2},{4,5},{5,4},{6,7},{7,6},{8,9},{9,8},{10,11... | collective-permute-start | bytes 221192 | tf_op jit(solution)/shard_map/ppermute | solution.py:495
  10.6 21.1 %collective-permute-start.1 = (bf16[4,18,512]{2,1,0:T(8,128)(2,1)S(1)}, bf16[4,18,512]{2,1,0:T(8,128)(2,1)S(1)}, u32[]{:S(2)}, u32[]{:S(2)}) collective-permute-start(bf16[4,18,512]{2,1,0:T(8,128)(2,1)S(1)} %get-tuple-element.17), channel_id=1, source_target_pairs={{0,63},{1,2},{2,1},{3,4},{4,3},{5,6},{6,5},{7,8},{8,7},{9,10},{10,... | collective-permute-start | bytes 221192 | tf_op jit(solution)/shard_map/ppermute | solution.py:495
  22.4 29.0 %all-to-all-start = ((f32[64,8,128]{2,1,0:T(8,128)}), f32[64,8,128]{2,1,0:T(8,128)S(1)}, u32[]{:S(2)}, u32[]{:S(2)}) async-start(f32[64,8,128]{2,1,0:T(8,128)} %bitcast.55), calls=%async_computation | async-start | bytes 524288 | tf_op jit(solution)/shard_map/all_to_all | solution.py:545
  31.7 13.1 %copy-start.2 = (bf16[4,18,512]{2,1,0:T(8,128)(2,1)}, bf16[4,18,512]{2,1,0:T(8,128)(2,1)S(1)}, u32[]{:S(2)}) copy-start(bf16[4,18,512]{2,1,0:T(8,128)(2,1)S(1)} %collective-permute-done.near_lon_ref) | copy-start | bytes 221188
  31.7 13.0 %copy-start.3 = (bf16[4,18,512]{2,1,0:T(8,128)(2,1)}, bf16[4,18,512]{2,1,0:T(8,128)(2,1)S(1)}, u32[]{:S(2)}) copy-start(bf16[4,18,512]{2,1,0:T(8,128)(2,1)S(1)} %collective-permute-done.1.far_lon_ref) | copy-start | bytes 221188
  31.8 14.4 %collective-permute-start.2 = (bf16[4,18,512]{2,1,0:T(8,128)(2,1)S(1)}, bf16[4,18,512]{2,1,0:T(8,128)(2,1)S(1)}, u32[]{:S(2)}, u32[]{:S(2)}) collective-permute-start(bf16[4,18,512]{2,1,0:T(8,128)(2,1)S(1)} %get-tuple-element.18), channel_id=1, source_target_pairs={{0,64},{64,0},{128,192},{192,128},{256,320},{320,256},{384,448},{4... | collective-permute-start | bytes 221192 | tf_op jit(solution)/shard_map/ppermute | solution.py:495
  34.5 17.0 %collective-permute-start.3 = (bf16[4,18,512]{2,1,0:T(8,128)(2,1)S(1)}, bf16[4,18,512]{2,1,0:T(8,128)(2,1)S(1)}, u32[]{:S(2)}, u32[]{:S(2)}) collective-permute-start(bf16[4,18,512]{2,1,0:T(8,128)(2,1)S(1)} %get-tuple-element.19), channel_id=1, source_target_pairs={{0,448},{64,128},{128,64},{192,256},{256,192},{320,384},{384,320},... | collective-permute-start | bytes 221192 | tf_op jit(solution)/shard_map/ppermute | solution.py:495
  42.0 2.7 %copy-start.4 = (bf16[512]{0:T(512)(128)(2,1)S(1)}, bf16[512]{0:T(512)(128)(2,1)}, u32[]{:S(2)}) copy-start(bf16[512]{0:T(512)(128)(2,1)} %param.17) | copy-start | bytes 3076
  46.2 5.2 %copy-start.5 = (bf16[4,18,512]{2,1,0:T(8,128)(2,1)}, bf16[4,18,512]{2,1,0:T(8,128)(2,1)S(1)}, u32[]{:S(2)}) copy-start(bf16[4,18,512]{2,1,0:T(8,128)(2,1)S(1)} %collective-permute-done.2.near_lat_ref) | copy-start | bytes 221188
  51.4 0.6 copy-start.6
  51.4 0.8 copy-start.1
  66.6 17.7 %all-to-all-start.1 = ((f32[32,4,128]{2,1,0:T(4,128)}), f32[32,4,128]{2,1,0:T(4,128)S(1)}, u32[]{:S(2)}, u32[]{:S(2)}) async-start(f32[32,4,128]{2,1,0:T(4,128)} %bitcast.67), calls=%async_computation.1 | async-start | bytes 131072 | tf_op jit(solution)/shard_map/all_to_all | solution.py:572
  84.9 17.8 %all-to-all-start.2 = ((f32[16,4,128]{2,1,0:T(4,128)}), f32[16,4,128]{2,1,0:T(4,128)S(1)}, u32[]{:S(2)}, u32[]{:S(2)}) async-start(f32[16,4,128]{2,1,0:T(4,128)} %bitcast.23), calls=%async_computation.2 | async-start | bytes 65536 | tf_op jit(solution)/shard_map/all_to_all | solution.py:584
  104.6 23.6 %all-to-all-start.3 = ((f32[64,4,128]{2,1,0:T(4,128)}), f32[64,4,128]{2,1,0:T(4,128)S(1)}, u32[]{:S(2)}, u32[]{:S(2)}) async-start(f32[64,4,128]{2,1,0:T(4,128)} %pad_maximum_fusion), calls=%async_computation.3 | async-start | bytes 262144 | tf_op jit(solution)/shard_map/all_to_all | solution.py:601

commit v5 on v4

--- a/solution.py
+++ b/solution.py
@@ -563,54 +563,78 @@
     block = block.reshape(2, 4, GROUP, MODEL)[:, :, :LIVE].reshape(2, 4, 3, 6, MODEL)
     block_out = block.transpose(1, 2, 0, 3, 4).reshape(12, 12, MODEL)
 
+    members = lon_count // 2
+    plane = (lon // 2) % 2
     planes = [[i for i in range(lon_count) if (i // 2) % 2 == h] for h in range(2)]
     columns = [
-        [a * lon_count + plane * 4 + h * 2 + c for h in range(2) for a in range(lat_count)]
-        for plane in range(lon_count // 4)
+        [a * lon_count + at * 4 + h * 2 + c for h in range(2) for a in range(lat_count)]
+        for at in range(members // 2)
         for c in range(2)
     ]
+
+    def by_plane(rows):
+        split = rows.reshape(members // 2, 2, 2, 128)
+        low, high = split[:, 0].reshape(members, 128), split[:, 1].reshape(members, 128)
+        return jnp.where(plane == 0, low, high), jnp.where(plane == 0, high, low)
+
     chunks = lax.all_to_all(
-        grads.reshape(32, 4, 128), "lon", 0, 0, axis_index_groups=planes, tiled=True
-    )
-    chunk = jnp.sum(chunks, axis=0).reshape(2, 1, 2, 128)
-    adjoint_row = adjoint[0].reshape(1, 1, 2, 128)
-    chunk = jnp.concatenate(
-        [
-            jnp.broadcast_to(chunk, (2, lat_count, 2, 128)),
-            jnp.broadcast_to(adjoint_row, (2, lat_count, 2, 128)),
-        ],
-        axis=2,
-    ).reshape(2 * lat_count, 4, 128)
-    along = lax.all_to_all(chunk, ("lat", "lon"), 0, 0, axis_index_groups=columns, tiled=True)
-    half = jnp.sum(along[:, :2], axis=0)
-    below = lax.dynamic_index_in_dim(
-        along, ((lon // 2) % 2) * lat_count + (lat + 1) % lat_count, 0, keepdims=False
-    )[2:]
-    below = below.reshape(256)[:OWN].reshape(2, 4, GROUP)
-    here = adjoint[0, :OWN].reshape(2, 4, GROUP)
-    moved = jnp.concatenate([here[:, 1:], below[:, :1]], axis=1)
-    edge = jnp.pad(moved[0].reshape(1, 1, 4 * GROUP), ((0, 0), (0, 0), (0, 128 - 4 * GROUP)))
-    last = jnp.concatenate(
-        [
-            jnp.broadcast_to(half[None], (lon_count, 2, 128)),
-            innov[:, None, :],
-            jnp.broadcast_to(edge, (lon_count, 1, 128)),
-        ],
-        axis=1,
-    )
-    final = lax.all_to_all(last, "lon", 0, 0, tiled=True)
-    innovation = final[:, 2][None, None]
-    beside = lax.dynamic_index_in_dim(final[:, 3], (lon + 1) % lon_count, 0, keepdims=False)
-    beside = beside[: 4 * GROUP].reshape(4, GROUP)
-    rolled = jnp.stack([moved[1], beside])[:, :, :LIVE].reshape(2, 4, 3, 6)
-    rolled_adjoint = rolled.transpose(1, 2, 0, 3).reshape(12, 12)
-    parts = final[:, :2].reshape(lon_count // 4, 2, 2, 2, 128)
+        grads.reshape(members, 4, 128), "lon", 0, 0, axis_index_groups=planes, tiled=True
+    )
+    mine, other = by_plane(innov)
+    other = lax.ppermute(other, "lon", [(i, i ^ 2) for i in range(lon_count)])
+
+    chunk = jnp.concatenate([jnp.sum(chunks, axis=0), adjoint[:1, :128]], axis=0)
+    along = lax.all_to_all(
+        jnp.broadcast_to(chunk[None], (2 * lat_count, 5, 128)),
+        ("lat", "lon"),
+        0,
+        0,
+        axis_index_groups=columns,
+        tiled=True,
+    )
+    total = jnp.sum(along[:, :4], axis=0)
+    edges = along[:, 4]
+    below_at = (lat + 1) % lat_count
+
+    def edge_of(h, a):
+        return lax.dynamic_index_in_dim(edges, h * lat_count + a, 0, keepdims=False)
+
+    def moved_up(here, below):
+        kept = here[: 4 * GROUP].reshape(4, GROUP)[1:]
+        return jnp.concatenate([kept.reshape(3 * GROUP), below[:GROUP]])
+
+    below = edge_of(plane, below_at)
+    edge = moved_up(adjoint[0], below)
+    twin_edge = moved_up(edge_of(1 - plane, lat), edge_of(1 - plane, below_at))
+    shared = jnp.concatenate(
+        [total, jnp.pad(jnp.stack([edge, twin_edge]), ((0, 0), (0, 128 - 4 * GROUP)))], axis=0
+    )
+    final = jnp.concatenate(
+        [jnp.broadcast_to(shared[None], (members, 6, 128)), mine[:, None], other[:, None]], axis=1
+    )
+    final = lax.all_to_all(final, "lon", 0, 0, axis_index_groups=planes, tiled=True)
+
+    near, far = final[:, 6].reshape(-1, 2, 128), final[:, 7].reshape(-1, 2, 128)
+    low, high = jnp.where(plane == 0, near, far), jnp.where(plane == 0, far, near)
+    innovation = jnp.stack([low, high], axis=1).reshape(1, 1, lon_count, 128)
+
+    member = lon // 4 * 2 + lon % 2
+    across = (member - 1 + 2 * plane) % members
+    beside = lax.dynamic_index_in_dim(
+        final[:, 4:6].reshape(2 * members, 128),
+        jnp.where(lon % 2 == 0, 2 * (member + 1), 2 * across + 1),
+        0,
+        keepdims=False,
+    )
+    kept = adjoint[0, 4 * GROUP : OWN]
+    moved = jnp.concatenate([kept[GROUP:], below[4 * GROUP : 5 * GROUP]])
+    rolled = jnp.stack([moved, beside[: 4 * GROUP]]).reshape(2, 4, GROUP)[:, :, :LIVE]
+    rolled_adjoint = rolled.reshape(2, 4, 3, 6).transpose(1, 2, 0, 3).reshape(12, 12)
 
     def whole(part):
-        part = part.reshape(4, 8, 2, 128)
-        return part.transpose(2, 1, 0, 3).reshape(2, 8, MODEL)
-
-    return block_out, innovation, rolled_adjoint, whole(parts[:, 1]), whole(parts[:, 0])
+        return part.reshape(4, 8, 2, 128).transpose(2, 1, 0, 3).reshape(2, 8, MODEL)
+
+    return block_out, innovation, rolled_adjoint, whole(final[:, 2:4]), whole(final[:, 0:2])
 
 
 def solution(mesh):

time: 132 us -> 127 us (0.962)
  waiting for transfers between devices: 39.1 us -> 22.4 us
  starting transfers between devices: 60.9 us -> 72.1 us
    all_to_all x3, waiting for transfers between devices: 33 us -> 16.4 us  [the longest x1 10.7 us: shards(): lax.all_to_all(jnp.broadcast_to(chunk[None], (2 * lat_count, 5, 128)), ('...]
    ppermute x0 -> x1, starting transfers between devices: none -> 6.71 us  [shards(): other = lax.ppermute(other, 'lon', [(i, i ^ 2) for i in range(lon_count)])]
    all_to_all x3, starting transfers between devices: 22.8 us -> 27.3 us  [the longest x1 10.4 us: shards(): lax.all_to_all(grads.reshape(members, 4, 128), 'lon', 0, 0, axis_index_gr...]
    concatenate x3 -> x4, other arithmetic: 2.16 us -> 0.8 us  [the longest x1 0.7 us: shards(): jnp.concatenate([jnp.broadcast_to(shared[None], (members, 6, 128)), mine[...]
    another operation x5 -> x2, local copies, waits for them, and re-layouts: 1.49 us -> 0.17 us  [shards(): jnp.stack([moved, beside[:4 * GROUP]]).reshape(2, 4, GROUP)[:, :, :LIVE]]
    slice x8 -> x9, local copies, waits for them, and re-layouts: 2.16 us -> 2.9 us  [the longest x2 0.91 us: shards(): moved = jnp.concatenate([kept[GROUP:], below[4 * GROUP:5 * GROUP]])]
  transfers between devices with their start and end apart: 8 -> 9, of which waited for: 5 -> 4; matrix products, arithmetic and copies ran while one was open for 3% -> 5% of each run, Pallas kernels for 3% -> 4%
where the time goes in v5:
time: 127 us; the launch traced here: 126 us
  starting transfers between devices  72.1 us (57%)
  waiting for transfers between devices  22.4 us (18%)
  Pallas kernels  18.8 us (15%)
  local copies, waits for them, and re-layouts  8.84 us (7%)
  other arithmetic  2.53 us (2%)
    ppermute x4, starting transfers between devices, paired(): return lax.ppermute(value, axis, pairs)  29 us
    pallas_call x1, Pallas kernels, core(): pl.pallas_call(functools.partial(core_kernel, loss_scale=loss_scale, lat_...  14.3 us
    all_to_all x1, waiting for transfers between devices, shards(): lax.all_to_all(jnp.broadcast_to(chunk[None], (2 * lat_count, 5, 128)), ('...  10.7 us
    all_to_all x1, starting transfers between devices, shards(): lax.all_to_all(grads.reshape(members, 4, 128), 'lon', 0, 0, axis_index_gr...  10.4 us
    all_to_all x1, starting transfers between devices, shards(): lax.all_to_all(final, 'lon', 0, 0, axis_index_groups=planes, tiled=True)  9.2 us
    all_to_all x1, starting transfers between devices, shards(): lax.all_to_all(slots, 'lon', 0, 0, tiled=True).reshape(lon_count * 8, 128)  9.18 us
    all_to_all x1, starting transfers between devices, shards(): lax.all_to_all(jnp.broadcast_to(chunk[None], (2 * lat_count, 5, 128)), ('...  7.66 us
    ppermute x1, starting transfers between devices, shards(): other = lax.ppermute(other, 'lon', [(i, i ^ 2) for i in range(lon_count)])  6.71 us
  transfers between devices with their start and end apart: 9, of which 4 were waited for; matrix products, arithmetic and copies ran while one was open for 5% of the time, Pallas kernels for 4%

profile of v5, /device:TPU:1, one launch (start us, length us, event | category | flops | bytes accessed | tf_op | source)
XLA Modules:
  0.0 125.8 jit_solution(12575094951493538743)
XLA Ops:
  0.6 1.0 reshape.182
  1.6 0.1 copy.35
  1.8 0.0 copy-start
  1.8 8.8 %collective-permute-start = (bf16[4,18,512]{2,1,0:T(8,128)(2,1)S(1)}, bf16[4,18,512]{2,1,0:T(8,128)(2,1)S(1)}, u32[]{:S(2)}, u32[]{:S(2)}) collective-permute-start(bf16[4,18,512]{2,1,0:T(8,128)(2,1)S(1)} %get-tuple-element.16), channel_id=1, source_target_pairs={{0,1},{1,0},{2,3},{3,2},{4,5},{5,4},{6,7},{7,6},{8,9},{9,8},{10,11... | collective-permute-start | bytes 221192 | tf_op jit(solution)/shard_map/ppermute | solution.py:495
  10.6 10.0 %collective-permute-start.1 = (bf16[4,18,512]{2,1,0:T(8,128)(2,1)S(1)}, bf16[4,18,512]{2,1,0:T(8,128)(2,1)S(1)}, u32[]{:S(2)}, u32[]{:S(2)}) collective-permute-start(bf16[4,18,512]{2,1,0:T(8,128)(2,1)S(1)} %get-tuple-element.17), channel_id=1, source_target_pairs={{0,63},{1,2},{2,1},{3,4},{4,3},{5,6},{6,5},{7,8},{8,7},{9,10},{10,... | collective-permute-start | bytes 221192 | tf_op jit(solution)/shard_map/ppermute | solution.py:495
  20.6 1.8 %packed_slots.1 = f32[512,128]{1,0:T(8,128)} custom-call(s32[256,128]{1,0:T(8,128)} %bitcast.76, f32[256,128]{1,0:T(8,128)} %bitcast.77, f32[64,128]{1,0:T(8,128)} %bitcast.83, s32[1,64]{1,0:T(1,128)} %bitcast.91), custom_call_target="tpu_custom_call" | custom-call | flops 1000000 | bytes 500000 | tf_op jit(solution)/shard_map/packed_slots/pallas_call | solution.py:88
  22.4 9.2 %all-to-all-start = ((f32[64,8,128]{2,1,0:T(8,128)}), f32[64,8,128]{2,1,0:T(8,128)S(1)}, u32[]{:S(2)}, u32[]{:S(2)}) async-start(f32[64,8,128]{2,1,0:T(8,128)} %bitcast.70), calls=%async_computation | async-start | bytes 524288 | tf_op jit(solution)/shard_map/all_to_all | solution.py:545
  31.7 0.0 collective-permute-done.near_lon_ref
  31.7 0.0 collective-permute-done.1.far_lon_ref
  31.7 0.0 copy-start.3
  31.8 2.6 %collective-permute-start.2 = (bf16[4,18,512]{2,1,0:T(8,128)(2,1)S(1)}, bf16[4,18,512]{2,1,0:T(8,128)(2,1)S(1)}, u32[]{:S(2)}, u32[]{:S(2)}) collective-permute-start(bf16[4,18,512]{2,1,0:T(8,128)(2,1)S(1)} %get-tuple-element.18), channel_id=1, source_target_pairs={{0,64},{64,0},{128,192},{192,128},{256,320},{320,256},{384,448},{4... | collective-permute-start | bytes 221192 | tf_op jit(solution)/shard_map/ppermute | solution.py:495
  34.5 7.6 %collective-permute-start.3 = (bf16[4,18,512]{2,1,0:T(8,128)(2,1)S(1)}, bf16[4,18,512]{2,1,0:T(8,128)(2,1)S(1)}, u32[]{:S(2)}, u32[]{:S(2)}) collective-permute-start(bf16[4,18,512]{2,1,0:T(8,128)(2,1)S(1)} %get-tuple-element.19), channel_id=1, source_target_pairs={{0,448},{64,128},{128,64},{192,256},{256,192},{320,384},{384,320},... | collective-permute-start | bytes 221192 | tf_op jit(solution)/shard_map/ppermute | solution.py:495
  42.1 0.0 copy-start.4
  42.1 2.7 %ordered_bias.1.bias_hbm = f32[4,16,24,96]{3,2,1,0:T(8,128)} custom-call(f32[1152,72]{1,0:T(8,128)} %bitcast.92), custom_call_target="tpu_custom_call" | custom-call | flops 20000000000 | bytes 2000000 | tf_op jit(solution)/shard_map/ordered_bias/pallas_call | solution.py:54
  44.8 0.6 reshape.186.readout_ref
  45.3 0.9 collective-permute-done.2.near_lat_ref
  46.2 5.1 %collective-permute-done.3.far_lat_ref = bf16[4,18,512]{2,1,0:T(8,128)(2,1)S(1)} collective-permute-done((bf16[4,18,512]{2,1,0:T(8,128)(2,1)S(1)}, bf16[4,18,512]{2,1,0:T(8,128)(2,1)S(1)}, u32[]{:S(2)}, u32[]{:S(2)}) %collective-permute-start.3) | collective-permute-done | bytes 73760 | tf_op jit(solution)/shard_map/ppermute | solution.py:495
  51.4 0.0 all-to-all-done
  51.4 0.6 copy-done.6
  52.0 0.1 copy-done.1
  52.1 14.3 %window_and_observe.1 = (bf16[192,512]{1,0:T(8,128)(2,1)}, f32[8,256]{1,0:T(8,128)}, f32[128,128]{1,0:T(8,128)}, f32[64,128]{1,0:T(8,128)}) custom-call(bf16[2,4,18,512]{3,2,1,0:T(8,128)(2,1)} %copy-done, bf16[4,18,512]{2,1,0:T(8,128)(2,1)} %copy-done.2, bf16[4,18,512]{2,1,0:T(8,128)(2,1)} %copy-done.3, bf16[4,18,512]{2,1,0:T(8,128)(2,1)} %copy-done.5, ...), custom_call_target="tpu_custom_call" | custom-call | flops 3000000000 | bytes 8000000 | tf_op jit(solution)/shard_map/window_and_observe/pallas_call | solution.py:450
  66.5 10.4 %all-to-all-start.1 = ((f32[32,4,128]{2,1,0:T(4,128)}), f32[32,4,128]{2,1,0:T(4,128)S(1)}, u32[]{:S(2)}, u32[]{:S(2)}) async-start(f32[32,4,128]{2,1,0:T(4,128)} %bitcast.79), calls=%async_computation.1 | async-start | bytes 131072 | tf_op jit(solution)/shard_map/all_to_all | solution.py:580
  76.9 0.8 broadcast_select_fusion.7
  77.6 0.7 slice.125
  78.3 6.7 %collective-permute-start.4 = (f32[32,128]{1,0:T(8,128)S(1)}, f32[32,128]{1,0:T(8,128)S(1)}, u32[]{:S(2)}, u32[]{:S(2)}) collective-permute-start(f32[32,128]{1,0:T(8,128)S(1)} %bitcast.90), channel_id=1, source_target_pairs={{0,2},{1,3},{2,0},{3,1},{4,6},{5,7},{6,4},{7,5},{8,10},{9,11},{10,... | collective-permute-start | bytes 49160 | tf_op jit(solution)/shard_map/ppermute | solution.py:584
  85.0 0.0 all-to-all-done.1
  85.1 0.6 broadcast_in_dim.6
  85.7 7.7 %all-to-all-start.2 = ((f32[16,5,128]{2,1,0:T(8,128)}), f32[16,5,128]{2,1,0:T(8,128)S(1)}, u32[]{:S(2)}, u32[]{:S(2)}) async-start(f32[16,5,128]{2,1,0:T(8,128)} %broadcast_in_dim.6), calls=%async_computation.2 | async-start | bytes 131072 | tf_op jit(solution)/shard_map/all_to_all | solution.py:587
  93.4 0.8 slice_bitcast_fusion.5
  94.2 10.7 %all-to-all-done.2 = f32[16,5,128]{2,1,0:T(8,128)S(1)} async-done(((f32[16,5,128]{2,1,0:T(8,128)}), f32[16,5,128]{2,1,0:T(8,128)S(1)}, u32[]{:S(2)}, u32[]{:S(2)}) %all-to-all-start.2) | async-done | bytes 40992 | tf_op jit(solution)/shard_map/all_to_all | solution.py:587
  105.0 0.1 slice_bitcast_fusion.7
  105.1 0.1 slice_bitcast_fusion.4
  105.2 0.1 maximum_bitcast_fusion.1
  105.2 0.1 maximum_bitcast_fusion
  105.4 0.0 collective-permute-done.4
  105.4 0.7 pad_maximum_fusion
  106.1 9.2 %all-to-all-start.3 = ((f32[32,8,128]{2,1,0:T(8,128)}), f32[32,8,128]{2,1,0:T(8,128)S(1)}, u32[]{:S(2)}, u32[]{:S(2)}) async-start(f32[32,8,128]{2,1,0:T(8,128)} %pad_maximum_fusion), calls=%async_computation.3 | async-start | bytes 262144 | tf_op jit(solution)/shard_map/all_to_all | solution.py:615
  115.3 1.0 copy.49
  116.4 0.7 reshape.196
  117.1 0.1 pad_maximum_fusion.7
  117.2 0.1 stack.35
  117.3 5.6 %all-to-all-done.3 = f32[32,8,128]{2,1,0:T(8,128)S(1)} async-done(((f32[32,8,128]{2,1,0:T(8,128)}), f32[32,8,128]{2,1,0:T(8,128)S(1)}, u32[]{:S(2)}, u32[]{:S(2)}) %all-to-all-start.3) | async-done | bytes 131104 | tf_op jit(solution)/shard_map/all_to_all | solution.py:615
  123.0 0.6 copy.52
  123.6 0.1 stack.36
  123.7 0.1 reshape.203
  123.8 0.7 reshape.204
  124.5 0.6 copy.53
  125.1 0.6 pad_maximum_fusion.3
  (31 shorter events, 0.4 us)
Async XLA Ops:
  1.8 42.9 %copy-start = (bf16[2,4,18,512]{3,2,1,0:T(8,128)(2,1)}, bf16[2,4,18,512]{3,2,1,0:T(8,128)(2,1)S(1)}, u32[]{:S(2)}) copy-start(bf16[2,4,18,512]{3,2,1,0:T(8,128)(2,1)S(1)} %copy.42.own_ref) | copy-start | bytes 442372
  1.8 29.9 %collective-permute-start = (bf16[4,18,512]{2,1,0:T(8,128)(2,1)S(1)}, bf16[4,18,512]{2,1,0:T(8,128)(2,1)S(1)}, u32[]{:S(2)}, u32[]{:S(2)}) collective-permute-start(bf16[4,18,512]{2,1,0:T(8,128)(2,1)S(1)} %get-tuple-element.16), channel_id=1, source_target_pairs={{0,1},{1,0},{2,3},{3,2},{4,5},{5,4},{6,7},{7,6},{8,9},{9,8},{10,11... | collective-permute-start | bytes 221192 | tf_op jit(solution)/shard_map/ppermute | solution.py:495
  10.6 21.1 %collective-permute-start.1 = (bf16[4,18,512]{2,1,0:T(8,128)(2,1)S(1)}, bf16[4,18,512]{2,1,0:T(8,128)(2,1)S(1)}, u32[]{:S(2)}, u32[]{:S(2)}) collective-permute-start(bf16[4,18,512]{2,1,0:T(8,128)(2,1)S(1)} %get-tuple-element.17), channel_id=1, source_target_pairs={{0,63},{1,2},{2,1},{3,4},{4,3},{5,6},{6,5},{7,8},{8,7},{9,10},{10,... | collective-permute-start | bytes 221192 | tf_op jit(solution)/shard_map/ppermute | solution.py:495
  22.4 29.0 %all-to-all-start = ((f32[64,8,128]{2,1,0:T(8,128)}), f32[64,8,128]{2,1,0:T(8,128)S(1)}, u32[]{:S(2)}, u32[]{:S(2)}) async-start(f32[64,8,128]{2,1,0:T(8,128)} %bitcast.70), calls=%async_computation | async-start | bytes 524288 | tf_op jit(solution)/shard_map/all_to_all | solution.py:545
  31.7 13.0 %copy-start.2 = (bf16[4,18,512]{2,1,0:T(8,128)(2,1)}, bf16[4,18,512]{2,1,0:T(8,128)(2,1)S(1)}, u32[]{:S(2)}) copy-start(bf16[4,18,512]{2,1,0:T(8,128)(2,1)S(1)} %collective-permute-done.near_lon_ref) | copy-start | bytes 221188
  31.7 13.0 %copy-start.3 = (bf16[4,18,512]{2,1,0:T(8,128)(2,1)}, bf16[4,18,512]{2,1,0:T(8,128)(2,1)S(1)}, u32[]{:S(2)}) copy-start(bf16[4,18,512]{2,1,0:T(8,128)(2,1)S(1)} %collective-permute-done.1.far_lon_ref) | copy-start | bytes 221188
  31.8 14.4 %collective-permute-start.2 = (bf16[4,18,512]{2,1,0:T(8,128)(2,1)S(1)}, bf16[4,18,512]{2,1,0:T(8,128)(2,1)S(1)}, u32[]{:S(2)}, u32[]{:S(2)}) collective-permute-start(bf16[4,18,512]{2,1,0:T(8,128)(2,1)S(1)} %get-tuple-element.18), channel_id=1, source_target_pairs={{0,64},{64,0},{128,192},{192,128},{256,320},{320,256},{384,448},{4... | collective-permute-start | bytes 221192 | tf_op jit(solution)/shard_map/ppermute | solution.py:495
  34.5 16.9 %collective-permute-start.3 = (bf16[4,18,512]{2,1,0:T(8,128)(2,1)S(1)}, bf16[4,18,512]{2,1,0:T(8,128)(2,1)S(1)}, u32[]{:S(2)}, u32[]{:S(2)}) collective-permute-start(bf16[4,18,512]{2,1,0:T(8,128)(2,1)S(1)} %get-tuple-element.19), channel_id=1, source_target_pairs={{0,448},{64,128},{128,64},{192,256},{256,192},{320,384},{384,320},... | collective-permute-start | bytes 221192 | tf_op jit(solution)/shard_map/ppermute | solution.py:495
  42.1 2.7 %copy-start.4 = (bf16[512]{0:T(512)(128)(2,1)S(1)}, bf16[512]{0:T(512)(128)(2,1)}, u32[]{:S(2)}) copy-start(bf16[512]{0:T(512)(128)(2,1)} %param.17) | copy-start | bytes 3076
  46.2 5.2 %copy-start.5 = (bf16[4,18,512]{2,1,0:T(8,128)(2,1)}, bf16[4,18,512]{2,1,0:T(8,128)(2,1)S(1)}, u32[]{:S(2)}) copy-start(bf16[4,18,512]{2,1,0:T(8,128)(2,1)S(1)} %collective-permute-done.2.near_lat_ref) | copy-start | bytes 221188
  51.4 0.6 copy-start.6
  51.4 0.7 copy-start.1
  66.5 18.6 %all-to-all-start.1 = ((f32[32,4,128]{2,1,0:T(4,128)}), f32[32,4,128]{2,1,0:T(4,128)S(1)}, u32[]{:S(2)}, u32[]{:S(2)}) async-start(f32[32,4,128]{2,1,0:T(4,128)} %bitcast.79), calls=%async_computation.1 | async-start | bytes 131072 | tf_op jit(solution)/shard_map/all_to_all | solution.py:580
  78.3 27.1 %collective-permute-start.4 = (f32[32,128]{1,0:T(8,128)S(1)}, f32[32,128]{1,0:T(8,128)S(1)}, u32[]{:S(2)}, u32[]{:S(2)}) collective-permute-start(f32[32,128]{1,0:T(8,128)S(1)} %bitcast.90), channel_id=1, source_target_pairs={{0,2},{1,3},{2,0},{3,1},{4,6},{5,7},{6,4},{7,5},{8,10},{9,11},{10,... | collective-permute-start | bytes 49160 | tf_op jit(solution)/shard_map/ppermute | solution.py:584
  85.7 19.2 %all-to-all-start.2 = ((f32[16,5,128]{2,1,0:T(8,128)}), f32[16,5,128]{2,1,0:T(8,128)S(1)}, u32[]{:S(2)}, u32[]{:S(2)}) async-start(f32[16,5,128]{2,1,0:T(8,128)} %broadcast_in_dim.6), calls=%async_computation.2 | async-start | bytes 131072 | tf_op jit(solution)/shard_map/all_to_all | solution.py:587
  106.1 16.8 %all-to-all-start.3 = ((f32[32,8,128]{2,1,0:T(8,128)}), f32[32,8,128]{2,1,0:T(8,128)S(1)}, u32[]{:S(2)}, u32[]{:S(2)}) async-start(f32[32,8,128]{2,1,0:T(8,128)} %pad_maximum_fusion), calls=%async_computation.3 | async-start | bytes 262144 | tf_op jit(solution)/shard_map/all_to_all | solution.py:615

commit v6 on v5

--- a/solution.py
+++ b/solution.py
@@ -255,7 +255,10 @@
     w_ref,
     up_ref,
     adjoint_ref,
+    edge_ref,
     grads_ref,
+    mine_ref,
+    other_ref,
     innov_ref,
     term_ref,
     place_ref,
@@ -315,8 +318,14 @@
     adjoint = jnp.sum(jnp.where(low, column, 0.0), axis=1, keepdims=True)
     high, low = cells((16, OWN), 1)
     row = jnp.sum(jnp.where(high, exact(total, low.astype(F32)), 0.0), axis=0, keepdims=True)
-    adjoint_ref[...] = jnp.zeros_like(adjoint_ref)
-    adjoint_ref[0:1, :OWN] = row
+    adjoint_ref[...] = jnp.concatenate([row, jnp.zeros((1, 256 - OWN), F32)], axis=1)
+    edge_ref[...] = row[:, :128]
+    low_plane = (lax.axis_index("lon") // 2) % 2 == 0
+    for side in range(2):
+        by_plane = [innov_ref[pl.ds(2 * h + side, sources // 4, stride=4), :] for h in range(2)]
+        place = pl.ds(side, sources // 4, stride=2)
+        mine_ref[place, :] = jnp.where(low_plane, by_plane[0], by_plane[1])
+        other_ref[place, :] = jnp.where(low_plane, by_plane[1], by_plane[0])
 
     factor = 0.5 * loss_scale
     g_query = gq_ref[...].astype(BF16)
@@ -354,8 +363,8 @@
     own_ref,
     near_lon_ref,
     far_lon_ref,
+    far_lat_ref,
     near_lat_ref,
-    far_lat_ref,
     qkv_hbm,
     wo_hbm,
     down_ref,
@@ -365,8 +374,10 @@
     slots_hbm,
     block_ref,
     adjoint_ref,
+    edge_ref,
     grads_ref,
-    innov_ref,
+    mine_ref,
+    other_ref,
     field_ref,
     probs_ref,
     gq_ref,
@@ -383,6 +394,7 @@
     wo_ref,
     bias_ref,
     copy_sems,
+    innov_ref,
     term_ref,
     place_ref,
     slots_ref,
@@ -393,7 +405,7 @@
     slot_load.start()
     forward_part(
         lat_count,
-            own_ref,
+        own_ref,
         near_lon_ref,
         far_lon_ref,
         near_lat_ref,
@@ -435,7 +447,10 @@
         w_ref,
         up_ref,
         adjoint_ref,
+        edge_ref,
         grads_ref,
+        mine_ref,
+        other_ref,
         innov_ref,
         term_ref,
         place_ref,
@@ -450,12 +465,14 @@
     return pl.pallas_call(
         functools.partial(core_kernel, loss_scale=loss_scale, lat_count=lat_count),
         in_specs=[vmem] * 5 + [far] * 2 + [vmem] * 3 + [far] * 2,
-        out_specs=[vmem] * 4,
+        out_specs=[vmem] * 6,
         out_shape=[
             shape((OWN, MODEL), BF16),
-            shape((8, 256), F32),
+            shape((1, 256), F32),
+            shape((1, 128), F32),
             shape((128, 128), F32),
-            shape((sources, 128), F32),
+            shape((sources // 2, 128), F32),
+            shape((sources // 2, 128), F32),
         ],
         scratch_shapes=[
             pltpu.VMEM((8, 256), F32),
@@ -474,6 +491,7 @@
             pltpu.VMEM((MODEL, MODEL), BF16),
             pltpu.VMEM((4, HEADS, GROUP, WINDOW), F32),
             pltpu.SemaphoreType.DMA((4,)),
+            pltpu.VMEM((sources, 128), F32),
             pltpu.VMEM((2, 4 * sources, 128), F32),
             pltpu.VMEM((2, 4 * sources, 128), jnp.int32),
             pltpu.VMEM((sources * 8, 128), F32),
@@ -484,6 +502,48 @@
         ),
         name="window_and_observe",
     )(own, *halos, qkv, wo, down, up, readout, bias, slots)
+
+
+def finish_kernel(final_ref, moved_ref, up_ref, down_ref, innov_ref, rolled_ref, rows_ref):
+    members = final_ref.shape[0] // 8
+    rows_ref[...] = final_ref[...].astype(F32)
+    for m, (ref, which) in enumerate(((up_ref, 0), (up_ref, 1), (down_ref, 0), (down_ref, 1))):
+        for q in range(4):
+            ref[which, :, 128 * q : 128 * (q + 1)] = rows_ref[pl.ds(q * 64 + m, 8, stride=8), :]
+    lon = lax.axis_index("lon")
+    plane, member = (lon // 2) % 2, lon // 4 * 2 + lon % 2
+    for side in range(2):
+        near, far = [rows_ref[pl.ds(8 * side + i, members // 2, stride=16), :] for i in (6, 7)]
+        for h in range(2):
+            innov_ref[pl.ds(2 * h + side, members // 2, stride=4), :] = jnp.where(plane == h, near, far)
+
+    across = member - 1 + 2 * plane
+    across = jnp.where(across >= members, 0, across)
+    row = jnp.where(lon % 2 == 0, (member + 1) * 8 + 4, across * 8 + 5)
+    lane = lax.broadcasted_iota(jnp.int32, (16, 128), 1)
+    patch_row = lax.broadcasted_iota(jnp.int32, (16, 128), 0)
+    source = (patch_row // 3 * GROUP + patch_row % 3 * 6 + lane % 6) & 127
+    halves = [
+        jnp.take_along_axis(jnp.broadcast_to(values, (16, 128)), source, axis=1)
+        for values in (moved_ref[...], rows_ref[pl.ds(row, 1), :])
+    ]
+    rolled_ref[...] = jnp.where(lane < 6, halves[0], halves[1])[:12, :12]
+
+
+def finish(final, moved):
+    members = final.shape[0] // 8
+    shape = jax.ShapeDtypeStruct
+    return pl.pallas_call(
+        finish_kernel,
+        out_shape=[
+            shape((2, 8, MODEL), F32),
+            shape((2, 8, MODEL), F32),
+            shape((2 * members, 128), F32),
+            shape((12, 12), F32),
+        ],
+        scratch_shapes=[pltpu.VMEM((members * 8, 128), F32)],
+        name="finish",
+    )(final, moved)
 
 
 def paired(value, axis, odd_first):
@@ -521,7 +581,6 @@
             observation_index,
         )
     )
-    near_lon = paired(near_send, "lon", False)
     far_lon = paired(far_send, "lon", True)
 
     slots = packed_slots(
@@ -530,31 +589,34 @@
         observation_value.reshape(lon_count, 128),
         observation_count.reshape(1, lon_count),
     ).reshape(lon_count, 8, 128)
+    near_send, slots = lax.optimization_barrier((near_send, slots))
+    near_lon = paired(near_send, "lon", False)
 
     left = jnp.where(even_lon, far_lon, near_lon)
     right = jnp.where(even_lon, near_lon, far_lon)
     top = jnp.stack([left[0], own[0, 0], own[1, 0], right[0]])
     bottom = jnp.stack([left[3], own[0, 3], own[1, 3], right[3]])
-    near_send = jnp.where(even_lat, bottom, top)
-    far_send = jnp.where(even_lat, top, bottom)
-    near_send, far_send, bias, readout = lax.optimization_barrier(
-        (near_send, far_send, relative_position_bias, readout)
-    )
+    near_send, far_send, readout = lax.optimization_barrier(
+        (jnp.where(even_lat, bottom, top), jnp.where(even_lat, top, bottom), readout)
+    )
+    far_send, readout, bias = lax.optimization_barrier(
+        (far_send, readout.reshape(1, MODEL), relative_position_bias)
+    )
+    far_lat = paired(far_send, "lat", True)
     near_lat = paired(near_send, "lat", False)
-    far_lat = paired(far_send, "lat", True)
     slots = lax.all_to_all(slots, "lon", 0, 0, tiled=True).reshape(lon_count * 8, 128)
 
     down_rows = adapter_down_map.reshape(16, MODEL)
     up_rows = adapter_up_map.reshape(16, MODEL)
     loss_scale = 1.0 / math.sqrt(lat_count * lon_count)
-    block, adjoint, grads, innov = core(
+    block, adjoint, edge_row, grads, mine, other = core(
         own,
-        (near_lon, far_lon, near_lat, far_lat),
+        (near_lon, far_lon, far_lat, near_lat),
         query_key_value_weight,
         output_weight,
         down_rows,
         up_rows,
-        readout.reshape(1, MODEL),
+        readout,
         ordered_bias(bias),
         slots,
         loss_scale,
@@ -572,18 +634,12 @@
         for c in range(2)
     ]
 
-    def by_plane(rows):
-        split = rows.reshape(members // 2, 2, 2, 128)
-        low, high = split[:, 0].reshape(members, 128), split[:, 1].reshape(members, 128)
-        return jnp.where(plane == 0, low, high), jnp.where(plane == 0, high, low)
-
     chunks = lax.all_to_all(
         grads.reshape(members, 4, 128), "lon", 0, 0, axis_index_groups=planes, tiled=True
     )
-    mine, other = by_plane(innov)
     other = lax.ppermute(other, "lon", [(i, i ^ 2) for i in range(lon_count)])
 
-    chunk = jnp.concatenate([jnp.sum(chunks, axis=0), adjoint[:1, :128]], axis=0)
+    chunk = jnp.concatenate([jnp.sum(chunks, axis=0), edge_row], axis=0)
     along = lax.all_to_all(
         jnp.broadcast_to(chunk[None], (2 * lat_count, 5, 128)),
         ("lat", "lon"),
@@ -612,29 +668,16 @@
     final = jnp.concatenate(
         [jnp.broadcast_to(shared[None], (members, 6, 128)), mine[:, None], other[:, None]], axis=1
     )
-    final = lax.all_to_all(final, "lon", 0, 0, axis_index_groups=planes, tiled=True)
-
-    near, far = final[:, 6].reshape(-1, 2, 128), final[:, 7].reshape(-1, 2, 128)
-    low, high = jnp.where(plane == 0, near, far), jnp.where(plane == 0, far, near)
-    innovation = jnp.stack([low, high], axis=1).reshape(1, 1, lon_count, 128)
-
-    member = lon // 4 * 2 + lon % 2
-    across = (member - 1 + 2 * plane) % members
-    beside = lax.dynamic_index_in_dim(
-        final[:, 4:6].reshape(2 * members, 128),
-        jnp.where(lon % 2 == 0, 2 * (member + 1), 2 * across + 1),
-        0,
-        keepdims=False,
-    )
+    final = lax.all_to_all(
+        final.astype(BF16), "lon", 0, 0, axis_index_groups=planes, tiled=True
+    )
+
     kept = adjoint[0, 4 * GROUP : OWN]
-    moved = jnp.concatenate([kept[GROUP:], below[4 * GROUP : 5 * GROUP]])
-    rolled = jnp.stack([moved, beside[: 4 * GROUP]]).reshape(2, 4, GROUP)[:, :, :LIVE]
-    rolled_adjoint = rolled.reshape(2, 4, 3, 6).transpose(1, 2, 0, 3).reshape(12, 12)
-
-    def whole(part):
-        return part.reshape(4, 8, 2, 128).transpose(2, 1, 0, 3).reshape(2, 8, MODEL)
-
-    return block_out, innovation, rolled_adjoint, whole(final[:, 2:4]), whole(final[:, 0:2])
+    moved = jnp.concatenate([kept[GROUP:], below[4 * GROUP : 5 * GROUP], jnp.zeros((GROUP + 8,), F32)])
+    up_gradient, down_gradient, innovation, rolled_adjoint = finish(
+        final.reshape(members * 8, 128), moved.reshape(1, 128)
+    )
+    return block_out, innovation[None, None], rolled_adjoint, down_gradient, up_gradient
 
 
 def solution(mesh):

time: 127 us -> 125 us (0.984)
  starting transfers between devices: 72.1 us -> 69.6 us
  local copies, waits for them, and re-layouts: 8.84 us -> 7.2 us
  Pallas kernels: 18.8 us -> 20.4 us
    all_to_all x1, starting transfers between devices: 10.4 us -> 7.44 us  [shards(): lax.all_to_all(grads.reshape(members, 4, 128), 'lon', 0, 0, axis_index_gr...]
    slice x7 -> x2, local copies, waits for them, and re-layouts: 2.89 us -> 0.82 us  [the longest x1 0.75 us: shards(): kept[GROUP:]]
    all_to_all x1, waiting for transfers between devices: 10.7 us -> 9.02 us  [shards(): lax.all_to_all(jnp.broadcast_to(chunk[None], (2 * lat_count, 5, 128)), ('...]
    pallas_call x0 -> x1, Pallas kernels: none -> 1.54 us  [finish(): pl.pallas_call(finish_kernel, out_shape=[shape((2, 8, MODEL), F32), shape...]
    ppermute x1, starting transfers between devices: 6.71 us -> 8.06 us  [shards(): other = lax.ppermute(other, 'lon', [(i, i ^ 2) for i in range(lon_count)])]
  transfers between devices with their start and end apart: 9 -> 9, of which waited for: 4 -> 5; matrix products, arithmetic and copies ran while one was open for 5% -> 5% of each run, Pallas kernels for 4% -> 4%
where the time goes in v6:
time: 125 us; the launch traced here: 124 us
  starting transfers between devices  69.6 us (56%)
  waiting for transfers between devices  22.4 us (18%)
  Pallas kernels  20.4 us (16%)
  local copies, waits for them, and re-layouts  7.2 us (6%)
  other arithmetic  3.72 us (3%)
    ppermute x4, starting transfers between devices, paired(): return lax.ppermute(value, axis, pairs)  30.1 us
    pallas_call x1, Pallas kernels, core(): pl.pallas_call(functools.partial(core_kernel, loss_scale=loss_scale, lat_...  14.3 us
    all_to_all x1, starting transfers between devices, shards(): lax.all_to_all(final.astype(BF16), 'lon', 0, 0, axis_index_groups=planes,...  9.08 us
    all_to_all x1, waiting for transfers between devices, shards(): lax.all_to_all(jnp.broadcast_to(chunk[None], (2 * lat_count, 5, 128)), ('...  9.02 us
    all_to_all x1, starting transfers between devices, shards(): lax.all_to_all(slots, 'lon', 0, 0, tiled=True).reshape(lon_count * 8, 128)  8.52 us
    ppermute x1, starting transfers between devices, shards(): other = lax.ppermute(other, 'lon', [(i, i ^ 2) for i in range(lon_count)])  8.06 us
    all_to_all x1, starting transfers between devices, shards(): lax.all_to_all(grads.reshape(members, 4, 128), 'lon', 0, 0, axis_index_gr...  7.44 us
    ppermute x4, waiting for transfers between devices, paired(): return lax.ppermute(value, axis, pairs)  6.75 us
  transfers between devices with their start and end apart: 9, of which 5 were waited for; matrix products, arithmetic and copies ran while one was open for 5% of the time, Pallas kernels for 4%

profile of v6, /device:TPU:1, one launch (start us, length us, event | category | flops | bytes accessed | tf_op | source)
XLA Modules:
  0.0 124.2 jit_solution(4626309686223992099)
XLA Ops:
  0.6 1.0 reshape.96
  1.6 0.1 copy.20
  1.8 0.0 copy-start.5
  1.8 0.0 copy-start
  1.8 16.8 %collective-permute-start.1 = (bf16[4,18,512]{2,1,0:T(8,128)(2,1)S(1)}, bf16[4,18,512]{2,1,0:T(8,128)(2,1)S(1)}, u32[]{:S(2)}, u32[]{:S(2)}) collective-permute-start(bf16[4,18,512]{2,1,0:T(8,128)(2,1)S(1)} %get-tuple-element.29), channel_id=1, source_target_pairs={{0,63},{1,2},{2,1},{3,4},{4,3},{5,6},{6,5},{7,8},{8,7},{9,10},{10,... | collective-permute-start | bytes 221192 | tf_op jit(solution)/shard_map/ppermute | solution.py:555
  18.7 1.8 %packed_slots.1 = f32[512,128]{1,0:T(8,128)} custom-call(s32[256,128]{1,0:T(8,128)} %bitcast.61, f32[256,128]{1,0:T(8,128)} %bitcast.62, f32[64,128]{1,0:T(8,128)} %bitcast.64, s32[1,64]{1,0:T(1,128)} %bitcast.66), custom_call_target="tpu_custom_call" | custom-call | flops 1000000 | bytes 500000 | tf_op jit(solution)/shard_map/packed_slots/pallas_call | solution.py:88
  20.5 8.5 %all-to-all-start = ((f32[64,8,128]{2,1,0:T(8,128)}), f32[64,8,128]{2,1,0:T(8,128)S(1)}, u32[]{:S(2)}, u32[]{:S(2)}) async-start(f32[64,8,128]{2,1,0:T(8,128)} %bitcast.54), calls=%async_computation | async-start | bytes 524288 | tf_op jit(solution)/shard_map/all_to_all | solution.py:607
  29.0 2.5 %collective-permute-start = (bf16[4,18,512]{2,1,0:T(8,128)(2,1)S(1)}, bf16[4,18,512]{2,1,0:T(8,128)(2,1)S(1)}, u32[]{:S(2)}, u32[]{:S(2)}) collective-permute-start(bf16[4,18,512]{2,1,0:T(8,128)(2,1)S(1)} %get-tuple-element.28), channel_id=1, source_target_pairs={{0,1},{1,0},{2,3},{3,2},{4,5},{5,4},{6,7},{7,6},{8,9},{9,8},{10,11... | collective-permute-start | bytes 221192 | tf_op jit(solution)/shard_map/ppermute | solution.py:555
  31.6 0.0 collective-permute-done.1.far_lon_ref
  31.6 0.0 copy-start.3
  31.6 0.8 collective-permute-done.near_lon_ref
  32.5 0.0 copy-done.5
  32.5 0.6 reshape.103.readout_ref
  33.1 8.8 %collective-permute-start.2 = (bf16[4,18,512]{2,1,0:T(8,128)(2,1)S(1)}, bf16[4,18,512]{2,1,0:T(8,128)(2,1)S(1)}, u32[]{:S(2)}, u32[]{:S(2)}) collective-permute-start(bf16[4,18,512]{2,1,0:T(8,128)(2,1)S(1)} %get-tuple-element.32), channel_id=1, source_target_pairs={{0,448},{64,128},{128,64},{192,256},{256,192},{320,384},{384,320},... | collective-permute-start | bytes 221192 | tf_op jit(solution)/shard_map/ppermute | solution.py:555
  42.0 1.9 %collective-permute-start.3 = (bf16[4,18,512]{2,1,0:T(8,128)(2,1)S(1)}, bf16[4,18,512]{2,1,0:T(8,128)(2,1)S(1)}, u32[]{:S(2)}, u32[]{:S(2)}) collective-permute-start(bf16[4,18,512]{2,1,0:T(8,128)(2,1)S(1)} %get-tuple-element.33), channel_id=1, source_target_pairs={{0,64},{64,0},{128,192},{192,128},{256,320},{320,256},{384,448},{4... | collective-permute-start | bytes 221192 | tf_op jit(solution)/shard_map/ppermute | solution.py:555
  43.9 2.7 %ordered_bias.1.bias_hbm = f32[4,16,24,96]{3,2,1,0:T(8,128)} custom-call(f32[1152,72]{1,0:T(8,128)} %bitcast.67), custom_call_target="tpu_custom_call" | custom-call | flops 20000000000 | bytes 2000000 | tf_op jit(solution)/shard_map/ordered_bias/pallas_call | solution.py:54
  46.5 0.0 copy-done
  46.5 0.0 copy-done.3
  46.6 3.8 %collective-permute-done.2.far_lat_ref = bf16[4,18,512]{2,1,0:T(8,128)(2,1)S(1)} collective-permute-done((bf16[4,18,512]{2,1,0:T(8,128)(2,1)S(1)}, bf16[4,18,512]{2,1,0:T(8,128)(2,1)S(1)}, u32[]{:S(2)}, u32[]{:S(2)}) %collective-permute-start.2) | collective-permute-done | bytes 73760 | tf_op jit(solution)/shard_map/ppermute | solution.py:555
  50.4 2.1 %collective-permute-done.3.near_lat_ref = bf16[4,18,512]{2,1,0:T(8,128)(2,1)S(1)} collective-permute-done((bf16[4,18,512]{2,1,0:T(8,128)(2,1)S(1)}, bf16[4,18,512]{2,1,0:T(8,128)(2,1)S(1)}, u32[]{:S(2)}, u32[]{:S(2)}) %collective-permute-start.3) | collective-permute-done | bytes 73760 | tf_op jit(solution)/shard_map/ppermute | solution.py:555
  52.5 0.0 all-to-all-done
  52.5 0.6 copy-done.7
  53.1 0.1 copy-done.1
  53.2 14.3 %window_and_observe.1 = (bf16[192,512]{1,0:T(8,128)(2,1)}, f32[1,256]{1,0:T(1,128)}, f32[1,128]{1,0:T(1,128)}, f32[128,128]{1,0:T(8,128)}, f32[32,128]{1,0:T(8,128)}, /*index=5*/f32[32,128]{1,0:T(8,128)}) custom-call(bf16[2,4,18,512]{3,2,1,0:T(8,128)(2,1)} %copy-done, bf16[4,18,512]{2,1,0:T(8,128)(2,1)} %copy-done.4, bf16[4,18,512]{2,1,0:T(8,128)(2,1)} %copy-done.3, ...), custom_call_target="tpu_custom_call" | custom-call | flops 3000000000 | bytes 8000000 | tf_op jit(solution)/shard_map/window_and_observe/pallas_call | solution.py:465
  67.6 0.7 convert_bitcast_fusion.1
  68.3 7.4 %all-to-all-start.1 = ((f32[32,4,128]{2,1,0:T(4,128)}), f32[32,4,128]{2,1,0:T(4,128)S(1)}, u32[]{:S(2)}, u32[]{:S(2)}) async-start(f32[32,4,128]{2,1,0:T(4,128)} %bitcast.63), calls=%async_computation.1 | async-start | bytes 131072 | tf_op jit(solution)/shard_map/all_to_all | solution.py:637
  75.7 0.8 slice_bitcast_fusion.5
  76.5 0.7 convert.18
  77.2 8.1 %collective-permute-start.4 = (bf16[32,128]{1,0:T(8,128)(2,1)S(1)}, bf16[32,128]{1,0:T(8,128)(2,1)S(1)}, u32[]{:S(2)}, u32[]{:S(2)}) collective-permute-start(bf16[32,128]{1,0:T(8,128)(2,1)S(1)} %convert.18), channel_id=1, source_target_pairs={{0,2},{1,3},{2,0},{3,1},{4,6},{5,7},{6,4},{7,5},{8,10},{9,11},{10,... | collective-permute-start | bytes 24584 | tf_op jit(solution)/shard_map/ppermute | solution.py:640
  85.3 0.0 all-to-all-done.1
  85.3 0.6 pad_maximum_fusion.3
  86.0 0.6 broadcast_in_dim.26
  86.6 6.4 %all-to-all-start.2 = ((f32[16,5,128]{2,1,0:T(8,128)}), f32[16,5,128]{2,1,0:T(8,128)S(1)}, u32[]{:S(2)}, u32[]{:S(2)}) async-start(f32[16,5,128]{2,1,0:T(8,128)} %broadcast_in_dim.26), calls=%async_computation.2 | async-start | bytes 131072 | tf_op jit(solution)/shard_map/all_to_all | solution.py:643
  93.0 0.7 slice_bitcast_fusion.9
  93.7 1.0 copy.32
  94.8 0.7 reshape.110
  95.5 0.0 collective-permute-done.4
  95.5 9.0 %all-to-all-done.2 = f32[16,5,128]{2,1,0:T(8,128)S(1)} async-done(((f32[16,5,128]{2,1,0:T(8,128)}), f32[16,5,128]{2,1,0:T(8,128)S(1)}, u32[]{:S(2)}, u32[]{:S(2)}) %all-to-all-start.2) | async-done | bytes 40992 | tf_op jit(solution)/shard_map/all_to_all | solution.py:643
  104.6 0.1 slice_bitcast_fusion.4
  104.7 0.1 slice_bitcast_fusion.7
  104.8 0.1 maximum_bitcast_fusion.1
  104.8 0.1 maximum_bitcast_fusion
  105.0 0.7 pad_maximum_fusion.2
  105.7 9.1 %all-to-all-start.3 = ((bf16[32,8,128]{2,1,0:T(8,128)(2,1)}), bf16[32,8,128]{2,1,0:T(8,128)(2,1)S(1)}, u32[]{:S(2)}, u32[]{:S(2)}) async-start(bf16[32,8,128]{2,1,0:T(8,128)(2,1)} %pad_maximum_fusion.2), calls=%async_computation.3 | async-start | bytes 131072 | tf_op jit(solution)/shard_map/all_to_all | solution.py:671
  114.8 0.7 maximum_bitcast_fusion.2.moved_ref
  115.4 6.7 %all-to-all-done.3 = bf16[32,8,128]{2,1,0:T(8,128)(2,1)S(1)} async-done(((bf16[32,8,128]{2,1,0:T(8,128)(2,1)}), bf16[32,8,128]{2,1,0:T(8,128)(2,1)S(1)}, u32[]{:S(2)}, u32[]{:S(2)}) %all-to-all-start.3) | async-done | bytes 65568 | tf_op jit(solution)/shard_map/all_to_all | solution.py:671
  122.1 0.6 copy-done.2
  122.7 1.5 %finish.1 = (f32[2,8,512]{2,1,0:T(8,128)}, f32[2,8,512]{2,1,0:T(8,128)}, f32[64,128]{1,0:T(8,128)}, f32[12,12]{1,0:T(8,128)}) custom-call(bf16[256,128]{1,0:T(8,128)(2,1)} %bitcast.59, f32[1,128]{1,0:T(1,128)} %maximum_bitcast_fusion.2.moved_ref), custom_call_target="tpu_custom_call" | custom-call | tf_op jit(solution)/shard_map/finish/pallas_call | solution.py:536
  (27 shorter events, 0.3 us)
Async XLA Ops:
  1.8 30.8 %copy-start.5 = (bf16[512]{0:T(512)(128)(2,1)S(1)}, bf16[512]{0:T(512)(128)(2,1)}, u32[]{:S(2)}) copy-start(bf16[512]{0:T(512)(128)(2,1)} %param.17) | copy-start | bytes 3076
  1.8 44.7 %copy-start = (bf16[2,4,18,512]{3,2,1,0:T(8,128)(2,1)}, bf16[2,4,18,512]{3,2,1,0:T(8,128)(2,1)S(1)}, u32[]{:S(2)}) copy-start(bf16[2,4,18,512]{3,2,1,0:T(8,128)(2,1)S(1)} %copy.27.own_ref) | copy-start | bytes 442372
  1.8 29.8 %collective-permute-start.1 = (bf16[4,18,512]{2,1,0:T(8,128)(2,1)S(1)}, bf16[4,18,512]{2,1,0:T(8,128)(2,1)S(1)}, u32[]{:S(2)}, u32[]{:S(2)}) collective-permute-start(bf16[4,18,512]{2,1,0:T(8,128)(2,1)S(1)} %get-tuple-element.29), channel_id=1, source_target_pairs={{0,63},{1,2},{2,1},{3,4},{4,3},{5,6},{6,5},{7,8},{8,7},{9,10},{10,... | collective-permute-start | bytes 221192 | tf_op jit(solution)/shard_map/ppermute | solution.py:555
  20.5 32.0 %all-to-all-start = ((f32[64,8,128]{2,1,0:T(8,128)}), f32[64,8,128]{2,1,0:T(8,128)S(1)}, u32[]{:S(2)}, u32[]{:S(2)}) async-start(f32[64,8,128]{2,1,0:T(8,128)} %bitcast.54), calls=%async_computation | async-start | bytes 524288 | tf_op jit(solution)/shard_map/all_to_all | solution.py:607
  29.0 3.4 %collective-permute-start = (bf16[4,18,512]{2,1,0:T(8,128)(2,1)S(1)}, bf16[4,18,512]{2,1,0:T(8,128)(2,1)S(1)}, u32[]{:S(2)}, u32[]{:S(2)}) collective-permute-start(bf16[4,18,512]{2,1,0:T(8,128)(2,1)S(1)} %get-tuple-element.28), channel_id=1, source_target_pairs={{0,1},{1,0},{2,3},{3,2},{4,5},{5,4},{6,7},{7,6},{8,9},{9,8},{10,11... | collective-permute-start | bytes 221192 | tf_op jit(solution)/shard_map/ppermute | solution.py:555
  31.6 14.9 %copy-start.3 = (bf16[4,18,512]{2,1,0:T(8,128)(2,1)}, bf16[4,18,512]{2,1,0:T(8,128)(2,1)S(1)}, u32[]{:S(2)}) copy-start(bf16[4,18,512]{2,1,0:T(8,128)(2,1)S(1)} %collective-permute-done.1.far_lon_ref) | copy-start | bytes 221188
  32.4 14.1 %copy-start.4 = (bf16[4,18,512]{2,1,0:T(8,128)(2,1)}, bf16[4,18,512]{2,1,0:T(8,128)(2,1)S(1)}, u32[]{:S(2)}) copy-start(bf16[4,18,512]{2,1,0:T(8,128)(2,1)S(1)} %collective-permute-done.near_lon_ref) | copy-start | bytes 221188
  33.1 17.3 %collective-permute-start.2 = (bf16[4,18,512]{2,1,0:T(8,128)(2,1)S(1)}, bf16[4,18,512]{2,1,0:T(8,128)(2,1)S(1)}, u32[]{:S(2)}, u32[]{:S(2)}) collective-permute-start(bf16[4,18,512]{2,1,0:T(8,128)(2,1)S(1)} %get-tuple-element.32), channel_id=1, source_target_pairs={{0,448},{64,128},{128,64},{192,256},{256,192},{320,384},{384,320},... | collective-permute-start | bytes 221192 | tf_op jit(solution)/shard_map/ppermute | solution.py:555
  42.0 10.5 %collective-permute-start.3 = (bf16[4,18,512]{2,1,0:T(8,128)(2,1)S(1)}, bf16[4,18,512]{2,1,0:T(8,128)(2,1)S(1)}, u32[]{:S(2)}, u32[]{:S(2)}) collective-permute-start(bf16[4,18,512]{2,1,0:T(8,128)(2,1)S(1)} %get-tuple-element.33), channel_id=1, source_target_pairs={{0,64},{64,0},{128,192},{192,128},{256,320},{320,256},{384,448},{4... | collective-permute-start | bytes 221192 | tf_op jit(solution)/shard_map/ppermute | solution.py:555
  50.4 2.1 %copy-start.6 = (bf16[4,18,512]{2,1,0:T(8,128)(2,1)}, bf16[4,18,512]{2,1,0:T(8,128)(2,1)S(1)}, u32[]{:S(2)}) copy-start(bf16[4,18,512]{2,1,0:T(8,128)(2,1)S(1)} %collective-permute-done.2.far_lat_ref) | copy-start | bytes 221188
  52.5 0.6 copy-start.7
  52.5 0.7 copy-start.1
  68.3 17.0 %all-to-all-start.1 = ((f32[32,4,128]{2,1,0:T(4,128)}), f32[32,4,128]{2,1,0:T(4,128)S(1)}, u32[]{:S(2)}, u32[]{:S(2)}) async-start(f32[32,4,128]{2,1,0:T(4,128)} %bitcast.63), calls=%async_computation.1 | async-start | bytes 131072 | tf_op jit(solution)/shard_map/all_to_all | solution.py:637
  77.2 18.3 %collective-permute-start.4 = (bf16[32,128]{1,0:T(8,128)(2,1)S(1)}, bf16[32,128]{1,0:T(8,128)(2,1)S(1)}, u32[]{:S(2)}, u32[]{:S(2)}) collective-permute-start(bf16[32,128]{1,0:T(8,128)(2,1)S(1)} %convert.18), channel_id=1, source_target_pairs={{0,2},{1,3},{2,0},{3,1},{4,6},{5,7},{6,4},{7,5},{8,10},{9,11},{10,... | collective-permute-start | bytes 24584 | tf_op jit(solution)/shard_map/ppermute | solution.py:640
  86.6 18.0 %all-to-all-start.2 = ((f32[16,5,128]{2,1,0:T(8,128)}), f32[16,5,128]{2,1,0:T(8,128)S(1)}, u32[]{:S(2)}, u32[]{:S(2)}) async-start(f32[16,5,128]{2,1,0:T(8,128)} %broadcast_in_dim.26), calls=%async_computation.2 | async-start | bytes 131072 | tf_op jit(solution)/shard_map/all_to_all | solution.py:643
  105.7 16.4 %all-to-all-start.3 = ((bf16[32,8,128]{2,1,0:T(8,128)(2,1)}), bf16[32,8,128]{2,1,0:T(8,128)(2,1)S(1)}, u32[]{:S(2)}, u32[]{:S(2)}) async-start(bf16[32,8,128]{2,1,0:T(8,128)(2,1)} %pad_maximum_fusion.2), calls=%async_computation.3 | async-start | bytes 131072 | tf_op jit(solution)/shard_map/all_to_all | solution.py:671
  122.1 0.6 copy-start.2

commit v7 on v6

--- a/solution.py
+++ b/solution.py
@@ -138,27 +138,31 @@
     first = (lat == 0).astype(F32)
     last = (lat == lat_count - 1).astype(F32)
 
-    def padded(x):
-        return jnp.concatenate([x, jnp.zeros((GROUP - LIVE, MODEL), F32)], axis=0)
-
     def pick(cond, a, b):
         return jnp.where(cond, a.astype(F32), b.astype(F32))
 
+    gap = jnp.zeros((GROUP - LIVE, MODEL), F32)
+
     def piece(strip, group):
-        if group == 0:
-            return pick(even_lat, far_lat_ref[strip], near_lat_ref[strip])
-        if group == 5:
-            return pick(even_lat, near_lat_ref[strip], far_lat_ref[strip])
-        if strip == 0:
-            return pick(even_lon, far_lon_ref[group - 1], near_lon_ref[group - 1])
-        if strip == 3:
-            return pick(even_lon, near_lon_ref[group - 1], far_lon_ref[group - 1])
-        return own_ref[strip - 1, group - 1].astype(F32)
+        rows = []
+        for i in range(3):
+            at = 3 * (group - 1) + i
+            if group == 0:
+                rows.append(pick(even_lat, far_lat_ref[strip, i], near_lat_ref[strip, i]))
+            elif group == 5:
+                rows.append(pick(even_lat, near_lat_ref[strip, i], far_lat_ref[strip, i]))
+            elif strip == 0:
+                rows.append(pick(even_lon, far_lon_ref[at], near_lon_ref[at]))
+            elif strip == 3:
+                rows.append(pick(even_lon, near_lon_ref[at], far_lon_ref[at]))
+            else:
+                rows.append(own_ref[at].astype(F32)[6 * (strip - 1) : 6 * strip])
+        return jnp.concatenate(rows + [gap], axis=0)
 
     for strip in range(4):
         rows = []
         for pair in range(3):
-            x = jnp.concatenate([padded(piece(strip, 2 * pair + i)) for i in range(2)], axis=0)
+            x = jnp.concatenate([piece(strip, 2 * pair + i) for i in range(2)], axis=0)
             center = x - jnp.mean(x, axis=1, keepdims=True)
             spread = jnp.mean(center * center, axis=1, keepdims=True)
             y = center * lax.rsqrt(spread + NORM_EPS)
@@ -235,10 +239,13 @@
             slope = (probs * (v_w - mean) * scale).astype(BF16)
             gq_ref[n * GROUP : (n + 1) * GROUP, cols] = fold(mm(slope, k_win))
 
-    x_own = [padded(own_ref[n // 4, n % 4].astype(F32)) for n in range(8)]
-    x_own = jnp.concatenate(x_own, axis=0)
+    x_own = jnp.concatenate([piece(1 + n // 4, 1 + n % 4) for n in range(8)], axis=0)
     out = (x_own + mm(att_ref[...].astype(BF16), wo_ref[...])).astype(BF16)
-    block_ref[...] = out
+    wide = out.astype(F32)
+    for row in range(12):
+        starts = [(half * 4 + row // 3) * GROUP + 6 * (row % 3) for half in range(2)]
+        pair = jnp.concatenate([wide[start : start + 6] for start in starts], axis=0)
+        block_ref[row] = pair.astype(BF16)
     field_ref[...] = jnp.zeros_like(field_ref)
     field_ref[:, :OWN] = mm(readout, out, NT)
 
@@ -467,7 +474,7 @@
         in_specs=[vmem] * 5 + [far] * 2 + [vmem] * 3 + [far] * 2,
         out_specs=[vmem] * 6,
         out_shape=[
-            shape((OWN, MODEL), BF16),
+            shape((12, 12, MODEL), BF16),
             shape((1, 256), F32),
             shape((1, 128), F32),
             shape((128, 128), F32),
@@ -504,16 +511,15 @@
     )(own, *halos, qkv, wo, down, up, readout, bias, slots)
 
 
-def finish_kernel(final_ref, moved_ref, up_ref, down_ref, innov_ref, rolled_ref, rows_ref):
+def finish_kernel(final_ref, moved_ref, up_ref, down_ref, innov_ref, rolled_ref):
     members = final_ref.shape[0] // 8
-    rows_ref[...] = final_ref[...].astype(F32)
     for m, (ref, which) in enumerate(((up_ref, 0), (up_ref, 1), (down_ref, 0), (down_ref, 1))):
         for q in range(4):
-            ref[which, :, 128 * q : 128 * (q + 1)] = rows_ref[pl.ds(q * 64 + m, 8, stride=8), :]
+            ref[which, :, 128 * q : 128 * (q + 1)] = final_ref[pl.ds(q * 64 + m, 8, stride=8), :]
     lon = lax.axis_index("lon")
     plane, member = (lon // 2) % 2, lon // 4 * 2 + lon % 2
     for side in range(2):
-        near, far = [rows_ref[pl.ds(8 * side + i, members // 2, stride=16), :] for i in (6, 7)]
+        near, far = [final_ref[pl.ds(8 * side + i, members // 2, stride=16), :] for i in (6, 7)]
         for h in range(2):
             innov_ref[pl.ds(2 * h + side, members // 2, stride=4), :] = jnp.where(plane == h, near, far)
 
@@ -525,7 +531,7 @@
     source = (patch_row // 3 * GROUP + patch_row % 3 * 6 + lane % 6) & 127
     halves = [
         jnp.take_along_axis(jnp.broadcast_to(values, (16, 128)), source, axis=1)
-        for values in (moved_ref[...], rows_ref[pl.ds(row, 1), :])
+        for values in (moved_ref[...], final_ref[pl.ds(row, 1), :])
     ]
     rolled_ref[...] = jnp.where(lane < 6, halves[0], halves[1])[:12, :12]
 
@@ -541,7 +547,6 @@
             shape((2 * members, 128), F32),
             shape((12, 12), F32),
         ],
-        scratch_shapes=[pltpu.VMEM((members * 8, 128), F32)],
         name="finish",
     )(final, moved)
 
@@ -572,8 +577,7 @@
     lat, lon = lax.axis_index("lat"), lax.axis_index("lon")
     even_lat, even_lon = lat % 2 == 0, lon % 2 == 0
 
-    own = tokens.reshape(4, 3, 2, 6, MODEL).transpose(2, 0, 1, 3, 4).reshape(2, 4, LIVE, MODEL)
-    own = lax.optimization_barrier(own)
+    own = (tokens[:, :6], tokens[:, 6:])
     near_send, far_send, observation_index = lax.optimization_barrier(
         (
             jnp.where(even_lon, own[1], own[0]),
@@ -594,8 +598,9 @@
 
     left = jnp.where(even_lon, far_lon, near_lon)
     right = jnp.where(even_lon, near_lon, far_lon)
-    top = jnp.stack([left[0], own[0, 0], own[1, 0], right[0]])
-    bottom = jnp.stack([left[3], own[0, 3], own[1, 3], right[3]])
+    strips = (left, own[0], own[1], right)
+    top = jnp.stack([strip[:3] for strip in strips])
+    bottom = jnp.stack([strip[9:] for strip in strips])
     near_send, far_send, readout = lax.optimization_barrier(
         (jnp.where(even_lat, bottom, top), jnp.where(even_lat, top, bottom), readout)
     )
@@ -609,8 +614,8 @@
     down_rows = adapter_down_map.reshape(16, MODEL)
     up_rows = adapter_up_map.reshape(16, MODEL)
     loss_scale = 1.0 / math.sqrt(lat_count * lon_count)
-    block, adjoint, edge_row, grads, mine, other = core(
-        own,
+    block_out, adjoint, edge_row, grads, mine, other = core(
+        tokens,
         (near_lon, far_lon, far_lat, near_lat),
         query_key_value_weight,
         output_weight,
@@ -622,9 +627,6 @@
         loss_scale,
         lat_count,
     )
-    block = block.reshape(2, 4, GROUP, MODEL)[:, :, :LIVE].reshape(2, 4, 3, 6, MODEL)
-    block_out = block.transpose(1, 2, 0, 3, 4).reshape(12, 12, MODEL)
-
     members = lon_count // 2
     plane = (lon // 2) % 2
     planes = [[i for i in range(lon_count) if (i // 2) % 2 == h] for h in range(2)]
@@ -640,6 +642,7 @@
     other = lax.ppermute(other, "lon", [(i, i ^ 2) for i in range(lon_count)])
 
     chunk = jnp.concatenate([jnp.sum(chunks, axis=0), edge_row], axis=0)
+    chunk, adjoint = lax.optimization_barrier((chunk, adjoint))
     along = lax.all_to_all(
         jnp.broadcast_to(chunk[None], (2 * lat_count, 5, 128)),
         ("lat", "lon"),
@@ -668,9 +671,7 @@
     final = jnp.concatenate(
         [jnp.broadcast_to(shared[None], (members, 6, 128)), mine[:, None], other[:, None]], axis=1
     )
-    final = lax.all_to_all(
-        final.astype(BF16), "lon", 0, 0, axis_index_groups=planes, tiled=True
-    )
+    final = lax.all_to_all(final, "lon", 0, 0, axis_index_groups=planes, tiled=True)
 
     kept = adjoint[0, 4 * GROUP : OWN]
     moved = jnp.concatenate([kept[GROUP:], below[4 * GROUP : 5 * GROUP], jnp.zeros((GROUP + 8,), F32)])

time: 125 us -> 124 us (level)
  local copies, waits for them, and re-layouts: 7.2 us -> 3.63 us
  waiting for transfers between devices: 22.4 us -> 24.5 us
    all_to_all x1, waiting for transfers between devices: 9.02 us -> 10.8 us  [shards(): lax.all_to_all(jnp.broadcast_to(chunk[None], (2 * lat_count, 5, 128)), ('...]
    reshape x2 -> x0, local copies, waits for them, and re-layouts: 1.71 us -> none  [the longest x1 0.98 us: shards(): tokens.reshape(4, 3, 2, 6, MODEL).transpose(2, 0, 1, 3, 4)]
  transfers between devices with their start and end apart: 9 -> 9, of which waited for: 5 -> 5; matrix products, arithmetic and copies ran while one was open for 5% -> 3% of each run, Pallas kernels for 4% -> 4%
where the time goes in v7:
time: 124 us; the launch traced here: 123 us
  starting transfers between devices  69.6 us (56%)
  waiting for transfers between devices  24.5 us (20%)
  Pallas kernels  20.4 us (16%)
  other arithmetic  4.08 us (3%)
  local copies, waits for them, and re-layouts  3.63 us (3%)
    ppermute x4, starting transfers between devices, paired(): return lax.ppermute(value, axis, pairs)  30.1 us
    pallas_call x1, Pallas kernels, core(): pl.pallas_call(functools.partial(core_kernel, loss_scale=loss_scale, lat_...  14.4 us
    all_to_all x1, waiting for transfers between devices, shards(): lax.all_to_all(jnp.broadcast_to(chunk[None], (2 * lat_count, 5, 128)), ('...  10.8 us
    all_to_all x1, starting transfers between devices, shards(): lax.all_to_all(slots, 'lon', 0, 0, tiled=True).reshape(lon_count * 8, 128)  8.52 us
    all_to_all x1, starting transfers between devices, shards(): lax.all_to_all(final, 'lon', 0, 0, axis_index_groups=planes, tiled=True)  8.11 us
    ppermute x1, starting transfers between devices, shards(): other = lax.ppermute(other, 'lon', [(i, i ^ 2) for i in range(lon_count)])  8.09 us
    all_to_all x1, starting transfers between devices, shards(): lax.all_to_all(grads.reshape(members, 4, 128), 'lon', 0, 0, axis_index_gr...  7.45 us
    all_to_all x1, starting transfers between devices, shards(): lax.all_to_all(jnp.broadcast_to(chunk[None], (2 * lat_count, 5, 128)), ('...  7.33 us
  transfers between devices with their start and end apart: 9, of which 5 were waited for; matrix products, arithmetic and copies ran while one was open for 3% of the time, Pallas kernels for 4%

profile of v7, /device:TPU:1, one launch (start us, length us, event | category | flops | bytes accessed | tf_op | source)
XLA Modules:
  0.0 123.2 jit_solution(16359778212249012900)
XLA Ops:
  0.6 0.0 copy-start.1
  0.6 0.0 copy-start.5
  0.7 1.1 broadcast_select_fusion.4
  1.8 16.8 %collective-permute-start.1 = (bf16[12,6,512]{2,1,0:T(8,128)(2,1)S(1)}, bf16[12,6,512]{2,1,0:T(8,128)(2,1)S(1)}, u32[]{:S(2)}, u32[]{:S(2)}) collective-permute-start(bf16[12,6,512]{2,1,0:T(8,128)(2,1)S(1)} %get-tuple-element.31), channel_id=1, source_target_pairs={{0,63},{1,2},{2,1},{3,4},{4,3},{5,6},{6,5},{7,8},{8,7},{9,10},{10,... | collective-permute-start | bytes 221192 | tf_op jit(solution)/shard_map/ppermute | solution.py:560
  18.6 1.8 %packed_slots.1 = f32[512,128]{1,0:T(8,128)} custom-call(s32[256,128]{1,0:T(8,128)} %bitcast.55, f32[256,128]{1,0:T(8,128)} %bitcast.56, f32[64,128]{1,0:T(8,128)} %bitcast.58, s32[1,64]{1,0:T(1,128)} %bitcast.61), custom_call_target="tpu_custom_call" | custom-call | flops 1000000 | bytes 500000 | tf_op jit(solution)/shard_map/packed_slots/pallas_call | solution.py:88
  20.4 8.5 %all-to-all-start = ((f32[64,8,128]{2,1,0:T(8,128)}), f32[64,8,128]{2,1,0:T(8,128)S(1)}, u32[]{:S(2)}, u32[]{:S(2)}) async-start(f32[64,8,128]{2,1,0:T(8,128)} %bitcast.52), calls=%async_computation | async-start | bytes 524288 | tf_op jit(solution)/shard_map/all_to_all | solution.py:612
  28.9 2.5 %collective-permute-start = (bf16[12,6,512]{2,1,0:T(8,128)(2,1)S(1)}, bf16[12,6,512]{2,1,0:T(8,128)(2,1)S(1)}, u32[]{:S(2)}, u32[]{:S(2)}) collective-permute-start(bf16[12,6,512]{2,1,0:T(8,128)(2,1)S(1)} %get-tuple-element.30), channel_id=1, source_target_pairs={{0,1},{1,0},{2,3},{3,2},{4,5},{5,4},{6,7},{7,6},{8,9},{9,8},{10,11... | collective-permute-start | bytes 221192 | tf_op jit(solution)/shard_map/ppermute | solution.py:560
  31.4 0.0 copy-done.1
  31.5 0.0 collective-permute-done.1.far_lon_ref
  31.5 0.0 copy-start.3
  31.5 0.8 collective-permute-done.near_lon_ref
  32.4 0.0 copy-start.4
  32.4 0.1 broadcast_select_fusion
  32.5 0.0 copy-done.5
  32.5 0.6 reshape.82.readout_ref
  33.1 8.8 %collective-permute-start.2 = (bf16[4,3,6,512]{3,2,1,0:T(8,128)(2,1)S(1)}, bf16[4,3,6,512]{3,2,1,0:T(8,128)(2,1)S(1)}, u32[]{:S(2)}, u32[]{:S(2)}) collective-permute-start(bf16[4,3,6,512]{3,2,1,0:T(8,128)(2,1)S(1)} %get-tuple-element.34), channel_id=1, source_target_pairs={{0,448},{64,128},{128,64},{192,256},{256,192},{320,384},{384,320},... | collective-permute-start | bytes 221192 | tf_op jit(solution)/shard_map/ppermute | solution.py:560
  41.9 1.9 %collective-permute-start.3 = (bf16[4,3,6,512]{3,2,1,0:T(8,128)(2,1)S(1)}, bf16[4,3,6,512]{3,2,1,0:T(8,128)(2,1)S(1)}, u32[]{:S(2)}, u32[]{:S(2)}) collective-permute-start(bf16[4,3,6,512]{3,2,1,0:T(8,128)(2,1)S(1)} %get-tuple-element.35), channel_id=1, source_target_pairs={{0,64},{64,0},{128,192},{192,128},{256,320},{320,256},{384,448},{4... | collective-permute-start | bytes 221192 | tf_op jit(solution)/shard_map/ppermute | solution.py:560
  43.8 2.6 %ordered_bias.1.bias_hbm = f32[4,16,24,96]{3,2,1,0:T(8,128)} custom-call(f32[1152,72]{1,0:T(8,128)} %bitcast.62), custom_call_target="tpu_custom_call" | custom-call | flops 20000000000 | bytes 2000000 | tf_op jit(solution)/shard_map/ordered_bias/pallas_call | solution.py:54
  46.5 0.0 copy-done.3
  46.5 0.0 copy-done.4
  46.5 3.8 %collective-permute-done.2.far_lat_ref = bf16[4,3,6,512]{3,2,1,0:T(8,128)(2,1)S(1)} collective-permute-done((bf16[4,3,6,512]{3,2,1,0:T(8,128)(2,1)S(1)}, bf16[4,3,6,512]{3,2,1,0:T(8,128)(2,1)S(1)}, u32[]{:S(2)}, u32[]{:S(2)}) %collective-permute-start.2) | collective-permute-done | bytes 73760 | tf_op jit(solution)/shard_map/ppermute | solution.py:560
  50.3 0.0 copy-start.6
  50.3 2.1 %collective-permute-done.3.near_lat_ref = bf16[4,3,6,512]{3,2,1,0:T(8,128)(2,1)S(1)} collective-permute-done((bf16[4,3,6,512]{3,2,1,0:T(8,128)(2,1)S(1)}, bf16[4,3,6,512]{3,2,1,0:T(8,128)(2,1)S(1)}, u32[]{:S(2)}, u32[]{:S(2)}) %collective-permute-start.3) | collective-permute-done | bytes 73760 | tf_op jit(solution)/shard_map/ppermute | solution.py:560
  52.4 0.0 copy-start.7
  52.4 0.0 all-to-all-done
  52.4 0.0 copy-done.6
  52.4 0.6 copy-done.7
  53.0 0.1 copy-done.2
  53.2 14.4 %window_and_observe.1 = (bf16[12,12,512]{2,1,0:T(8,128)(2,1)}, f32[1,256]{1,0:T(1,128)}, f32[1,128]{1,0:T(1,128)}, f32[128,128]{1,0:T(8,128)}, f32[32,128]{1,0:T(8,128)}, /*index=5*/f32[32,128]{1,0:T(8,128)}) custom-call(bf16[12,12,512]{2,1,0:T(8,128)(2,1)} %own_ref.1, bf16[12,6,512]{2,1,0:T(8,128)(2,1)} %copy-done.4, bf16[12,6,512]{2,1,0:T(8,128)(2,1)} %copy-done.3, ...), custom_call_target="tpu_custom_call" | custom-call | flops 3000000000 | bytes 8000000 | tf_op jit(solution)/shard_map/window_and_observe/pallas_call | solution.py:472
  67.5 7.4 %all-to-all-start.1 = ((f32[32,4,128]{2,1,0:T(4,128)}), f32[32,4,128]{2,1,0:T(4,128)S(1)}, u32[]{:S(2)}, u32[]{:S(2)}) async-start(f32[32,4,128]{2,1,0:T(4,128)} %bitcast.57), calls=%async_computation.1 | async-start | bytes 131072 | tf_op jit(solution)/shard_map/all_to_all | solution.py:639
  75.0 8.1 %collective-permute-start.4 = (f32[32,128]{1,0:T(8,128)}, f32[32,128]{1,0:T(8,128)S(1)}, u32[]{:S(2)}, u32[]{:S(2)}) collective-permute-start(f32[32,128]{1,0:T(8,128)} %get-tuple-element.46), channel_id=1, source_target_pairs={{0,2},{1,3},{2,0},{3,1},{4,6},{5,7},{6,4},{7,5},{8,10},{9,11},{10,... | collective-permute-start | bytes 49160 | tf_op jit(solution)/shard_map/ppermute | solution.py:642
  83.1 0.0 all-to-all-done.1
  83.2 0.6 pad_maximum_fusion.3
  83.8 0.6 broadcast_in_dim.24
  84.4 7.3 %all-to-all-start.2 = ((f32[16,5,128]{2,1,0:T(8,128)}), f32[16,5,128]{2,1,0:T(8,128)S(1)}, u32[]{:S(2)}, u32[]{:S(2)}) async-start(f32[16,5,128]{2,1,0:T(8,128)} %broadcast_in_dim.24), calls=%async_computation.2 | async-start | bytes 131072 | tf_op jit(solution)/shard_map/all_to_all | solution.py:646
  91.8 0.8 slice_bitcast_fusion.9
  92.6 10.8 %all-to-all-done.2 = f32[16,5,128]{2,1,0:T(8,128)S(1)} async-done(((f32[16,5,128]{2,1,0:T(8,128)}), f32[16,5,128]{2,1,0:T(8,128)S(1)}, u32[]{:S(2)}, u32[]{:S(2)}) %all-to-all-start.2) | async-done | bytes 40992 | tf_op jit(solution)/shard_map/all_to_all | solution.py:646
  103.4 0.1 slice_bitcast_fusion.11
  103.5 0.1 slice_bitcast_fusion.8
  103.5 0.1 maximum_bitcast_fusion.1
  103.6 0.1 maximum_bitcast_fusion
  103.7 0.0 collective-permute-done.4
  103.8 1.4 %pad_maximum_fusion = f32[32,8,128]{2,1,0:T(8,128)} fusion(f32[32,1,128]{2,1,0:T(1,128)S(1)} %bitcast.60, f32[32,1,128]{2,1,0:T(1,128)} %bitcast.59, f32[32,6,128]{2,1,0:T(8,128)S(1)} %broadcast_in_dim.25), kind=kLoop, calls=%fused_computation | loop fusion | flops 65536 | bytes 262144 | tf_op jit(solution)/shard_map/concatenate | solution.py:671
  105.2 8.1 %all-to-all-start.3 = ((f32[32,8,128]{2,1,0:T(8,128)}), f32[32,8,128]{2,1,0:T(8,128)S(1)}, u32[]{:S(2)}, u32[]{:S(2)}) async-start(f32[32,8,128]{2,1,0:T(8,128)} %pad_maximum_fusion), calls=%async_computation.3 | async-start | bytes 262144 | tf_op jit(solution)/shard_map/all_to_all | solution.py:674
  113.3 0.7 maximum_bitcast_fusion.2.moved_ref
  114.0 7.0 %all-to-all-done.3 = f32[32,8,128]{2,1,0:T(8,128)S(1)} async-done(((f32[32,8,128]{2,1,0:T(8,128)}), f32[32,8,128]{2,1,0:T(8,128)S(1)}, u32[]{:S(2)}, u32[]{:S(2)}) %all-to-all-start.3) | async-done | bytes 131104 | tf_op jit(solution)/shard_map/all_to_all | solution.py:674
  120.9 0.6 copy-done
  121.6 1.6 %finish.1 = (f32[2,8,512]{2,1,0:T(8,128)}, f32[2,8,512]{2,1,0:T(8,128)}, f32[64,128]{1,0:T(8,128)}, f32[12,12]{1,0:T(8,128)}) custom-call(f32[256,128]{1,0:T(8,128)} %bitcast.53, f32[1,128]{1,0:T(1,128)} %maximum_bitcast_fusion.2.moved_ref), custom_call_target="tpu_custom_call" | custom-call | tf_op jit(solution)/shard_map/finish/pallas_call | solution.py:542
  (14 shorter events, 0.2 us)
Async XLA Ops:
  0.6 30.8 %copy-start.1 = (bf16[12,12,512]{2,1,0:T(8,128)(2,1)S(1)}, bf16[12,12,512]{2,1,0:T(8,128)(2,1)}, u32[]{:S(2)}) copy-start(bf16[12,12,512]{2,1,0:T(8,128)(2,1)} %own_ref.1) | copy-start | bytes 442372
  0.6 31.8 %copy-start.5 = (bf16[512]{0:T(512)(128)(2,1)S(1)}, bf16[512]{0:T(512)(128)(2,1)}, u32[]{:S(2)}) copy-start(bf16[512]{0:T(512)(128)(2,1)} %param.17) | copy-start | bytes 3076
  1.8 29.7 %collective-permute-start.1 = (bf16[12,6,512]{2,1,0:T(8,128)(2,1)S(1)}, bf16[12,6,512]{2,1,0:T(8,128)(2,1)S(1)}, u32[]{:S(2)}, u32[]{:S(2)}) collective-permute-start(bf16[12,6,512]{2,1,0:T(8,128)(2,1)S(1)} %get-tuple-element.31), channel_id=1, source_target_pairs={{0,63},{1,2},{2,1},{3,4},{4,3},{5,6},{6,5},{7,8},{8,7},{9,10},{10,... | collective-permute-start | bytes 221192 | tf_op jit(solution)/shard_map/ppermute | solution.py:560
  20.4 32.0 %all-to-all-start = ((f32[64,8,128]{2,1,0:T(8,128)}), f32[64,8,128]{2,1,0:T(8,128)S(1)}, u32[]{:S(2)}, u32[]{:S(2)}) async-start(f32[64,8,128]{2,1,0:T(8,128)} %bitcast.52), calls=%async_computation | async-start | bytes 524288 | tf_op jit(solution)/shard_map/all_to_all | solution.py:612
  28.9 3.4 %collective-permute-start = (bf16[12,6,512]{2,1,0:T(8,128)(2,1)S(1)}, bf16[12,6,512]{2,1,0:T(8,128)(2,1)S(1)}, u32[]{:S(2)}, u32[]{:S(2)}) collective-permute-start(bf16[12,6,512]{2,1,0:T(8,128)(2,1)S(1)} %get-tuple-element.30), channel_id=1, source_target_pairs={{0,1},{1,0},{2,3},{3,2},{4,5},{5,4},{6,7},{7,6},{8,9},{9,8},{10,11... | collective-permute-start | bytes 221192 | tf_op jit(solution)/shard_map/ppermute | solution.py:560
  31.5 15.0 %copy-start.3 = (bf16[12,6,512]{2,1,0:T(8,128)(2,1)}, bf16[12,6,512]{2,1,0:T(8,128)(2,1)S(1)}, u32[]{:S(2)}) copy-start(bf16[12,6,512]{2,1,0:T(8,128)(2,1)S(1)} %collective-permute-done.1.far_lon_ref) | copy-start | bytes 221188
  32.4 14.1 %copy-start.4 = (bf16[12,6,512]{2,1,0:T(8,128)(2,1)}, bf16[12,6,512]{2,1,0:T(8,128)(2,1)S(1)}, u32[]{:S(2)}) copy-start(bf16[12,6,512]{2,1,0:T(8,128)(2,1)S(1)} %collective-permute-done.near_lon_ref) | copy-start | bytes 221188
  33.1 17.2 %collective-permute-start.2 = (bf16[4,3,6,512]{3,2,1,0:T(8,128)(2,1)S(1)}, bf16[4,3,6,512]{3,2,1,0:T(8,128)(2,1)S(1)}, u32[]{:S(2)}, u32[]{:S(2)}) collective-permute-start(bf16[4,3,6,512]{3,2,1,0:T(8,128)(2,1)S(1)} %get-tuple-element.34), channel_id=1, source_target_pairs={{0,448},{64,128},{128,64},{192,256},{256,192},{320,384},{384,320},... | collective-permute-start | bytes 221192 | tf_op jit(solution)/shard_map/ppermute | solution.py:560
  41.9 10.5 %collective-permute-start.3 = (bf16[4,3,6,512]{3,2,1,0:T(8,128)(2,1)S(1)}, bf16[4,3,6,512]{3,2,1,0:T(8,128)(2,1)S(1)}, u32[]{:S(2)}, u32[]{:S(2)}) collective-permute-start(bf16[4,3,6,512]{3,2,1,0:T(8,128)(2,1)S(1)} %get-tuple-element.35), channel_id=1, source_target_pairs={{0,64},{64,0},{128,192},{192,128},{256,320},{320,256},{384,448},{4... | collective-permute-start | bytes 221192 | tf_op jit(solution)/shard_map/ppermute | solution.py:560
  50.3 2.1 %copy-start.6 = (bf16[4,3,6,512]{3,2,1,0:T(8,128)(2,1)}, bf16[4,3,6,512]{3,2,1,0:T(8,128)(2,1)S(1)}, u32[]{:S(2)}) copy-start(bf16[4,3,6,512]{3,2,1,0:T(8,128)(2,1)S(1)} %collective-permute-done.2.far_lat_ref) | copy-start | bytes 221188
  52.4 0.6 copy-start.7
  52.4 0.7 copy-start.2
  67.5 15.6 %all-to-all-start.1 = ((f32[32,4,128]{2,1,0:T(4,128)}), f32[32,4,128]{2,1,0:T(4,128)S(1)}, u32[]{:S(2)}, u32[]{:S(2)}) async-start(f32[32,4,128]{2,1,0:T(4,128)} %bitcast.57), calls=%async_computation.1 | async-start | bytes 131072 | tf_op jit(solution)/shard_map/all_to_all | solution.py:639
  75.0 28.7 %collective-permute-start.4 = (f32[32,128]{1,0:T(8,128)}, f32[32,128]{1,0:T(8,128)S(1)}, u32[]{:S(2)}, u32[]{:S(2)}) collective-permute-start(f32[32,128]{1,0:T(8,128)} %get-tuple-element.46), channel_id=1, source_target_pairs={{0,2},{1,3},{2,0},{3,1},{4,6},{5,7},{6,4},{7,5},{8,10},{9,11},{10,... | collective-permute-start | bytes 49160 | tf_op jit(solution)/shard_map/ppermute | solution.py:642
  84.4 18.9 %all-to-all-start.2 = ((f32[16,5,128]{2,1,0:T(8,128)}), f32[16,5,128]{2,1,0:T(8,128)S(1)}, u32[]{:S(2)}, u32[]{:S(2)}) async-start(f32[16,5,128]{2,1,0:T(8,128)} %broadcast_in_dim.24), calls=%async_computation.2 | async-start | bytes 131072 | tf_op jit(solution)/shard_map/all_to_all | solution.py:646
  105.2 15.7 %all-to-all-start.3 = ((f32[32,8,128]{2,1,0:T(8,128)}), f32[32,8,128]{2,1,0:T(8,128)S(1)}, u32[]{:S(2)}, u32[]{:S(2)}) async-start(f32[32,8,128]{2,1,0:T(8,128)} %pad_maximum_fusion), calls=%async_computation.3 | async-start | bytes 262144 | tf_op jit(solution)/shard_map/all_to_all | solution.py:674
  120.9 0.6 copy-start

commit v8 on v7

--- a/solution.py
+++ b/solution.py
@@ -32,7 +32,7 @@
     return mm(a, b, dims, precision=lax.Precision.HIGHEST)
 
 
-def bias_kernel(bias_ref, out_ref, wide_ref):
+def bias_kernel(bias_ref, out_hbm, wide_ref, out_ref, sem):
     shape = (72, WINDOW)
     lane = lax.broadcasted_iota(jnp.int32, shape, 1)
     row = lane % GROUP
@@ -48,13 +48,22 @@
             for m in range(3):
                 start = 12 * (3 * (1 - parity) + m) + 6 * (1 - half)
                 out_ref[parity * 2 + half, :, 6 * m : 6 * m + 6, :] = wide_ref[:, start : start + 6, :]
+    store = pltpu.make_async_copy(out_ref, out_hbm.at[pl.ds(0, 4)], sem)
+    store.start()
+    store.wait()
 
 
 def ordered_bias(bias):
     return pl.pallas_call(
         bias_kernel,
-        out_shape=jax.ShapeDtypeStruct((4, HEADS, GROUP, WINDOW), F32),
-        scratch_shapes=[pltpu.VMEM((HEADS, 72, WINDOW), F32)],
+        out_shape=jax.ShapeDtypeStruct((64, HEADS, GROUP, WINDOW), F32),
+        out_specs=pl.BlockSpec(memory_space=pl.ANY),
+        scratch_shapes=[
+            pltpu.VMEM((HEADS, 72, WINDOW), F32),
+            pltpu.VMEM((4, HEADS, GROUP, WINDOW), F32),
+            pltpu.SemaphoreType.DMA,
+        ],
+        compiler_params=pltpu.CompilerParams(vmem_limit_bytes=58 * 1024 * 1024),
         cost_estimate=pl.CostEstimate(flops=2 * 10**10, bytes_accessed=2 * 10**6, transcendentals=0),
         name="ordered_bias",
     )(bias.reshape(HEADS * 72, 72))
@@ -94,18 +103,19 @@
 
 
 def forward_part(
+    bias_load,
     lat_count,
     own_ref,
     near_lon_ref,
     far_lon_ref,
     near_lat_ref,
     far_lat_ref,
-    qkv_hbm,
-    wo_hbm,
+    qkv_ref,
+    wo_ref,
     down_ref,
     up_ref,
     readout_ref,
-    bias_hbm,
+    bias_ref,
     block_ref,
     field_ref,
     probs_ref,
@@ -119,19 +129,7 @@
     v_ref,
     q_ref,
     att_ref,
-    qkv_ref,
-    wo_ref,
-    bias_ref,
-    copy_sems,
 ):
-    loads = [
-        pltpu.make_async_copy(source, target, copy_sems.at[i])
-        for i, (source, target) in enumerate(
-            ((qkv_hbm, qkv_ref), (bias_hbm, bias_ref), (wo_hbm, wo_ref))
-        )
-    ]
-    for load in loads:
-        load.start()
     lat = lax.axis_index("lat")
     even_lon = lax.axis_index("lon") % 2 == 0
     even_lat = lat % 2 == 0
@@ -174,8 +172,6 @@
             own_norm_ref[(strip - 1) * 4 * GROUP : strip * 4 * GROUP, :] = mine.astype(BF16)
 
     normed = norm_ref[...]
-    for load in loads:
-        load.wait()
     rank_row = lax.broadcasted_iota(jnp.int32, (16, MODEL), 0)
     up_half = 0.5 * up_ref[...].astype(F32)
     up_query = jnp.where(rank_row < 8, up_half, 0.0).astype(BF16)
@@ -206,6 +202,7 @@
     def fold(rows):
         return jnp.sum(jnp.where(head_mask, rows.reshape(8, GROUP, 256), 0.0), axis=0)
 
+    bias_load.wait()
     for n in range(8):
         half, row = n // 4, n % 4
         window = half * 3 + (row + 1) // 2
@@ -372,13 +369,13 @@
     far_lon_ref,
     far_lat_ref,
     near_lat_ref,
-    qkv_hbm,
-    wo_hbm,
+    qkv_ref,
+    wo_ref,
     down_ref,
     up_ref,
     readout_ref,
     bias_hbm,
-    slots_hbm,
+    slots_ref,
     block_ref,
     adjoint_ref,
     edge_ref,
@@ -397,32 +394,30 @@
     v_ref,
     q_ref,
     att_ref,
-    qkv_ref,
-    wo_ref,
     bias_ref,
-    copy_sems,
+    bias_sem,
     innov_ref,
     term_ref,
     place_ref,
-    slots_ref,
     loss_scale,
     lat_count,
 ):
-    slot_load = pltpu.make_async_copy(slots_hbm, slots_ref, copy_sems.at[3])
-    slot_load.start()
+    bias_load = pltpu.make_async_copy(bias_hbm.at[pl.ds(0, 4)], bias_ref, bias_sem)
+    bias_load.start()
     forward_part(
+        bias_load,
         lat_count,
         own_ref,
         near_lon_ref,
         far_lon_ref,
         near_lat_ref,
         far_lat_ref,
-        qkv_hbm,
-        wo_hbm,
+        qkv_ref,
+        wo_ref,
         down_ref,
         up_ref,
         readout_ref,
-        bias_hbm,
+        bias_ref,
         block_ref,
         field_ref,
         probs_ref,
@@ -436,12 +431,7 @@
         v_ref,
         q_ref,
         att_ref,
-        qkv_ref,
-        wo_ref,
-        bias_ref,
-        copy_sems,
-    )
-    slot_load.wait()
+    )
     observe_part(
         slots_ref,
         field_ref,
@@ -468,10 +458,10 @@
 def core(own, halos, qkv, wo, down, up, readout, bias, slots, loss_scale, lat_count):
     sources = slots.shape[0] // 8
     shape = jax.ShapeDtypeStruct
-    vmem, far = pl.BlockSpec(memory_space=pltpu.VMEM), pl.BlockSpec(memory_space=pl.ANY)
+    vmem = pl.BlockSpec(memory_space=pltpu.VMEM)
     return pl.pallas_call(
         functools.partial(core_kernel, loss_scale=loss_scale, lat_count=lat_count),
-        in_specs=[vmem] * 5 + [far] * 2 + [vmem] * 3 + [far] * 2,
+        in_specs=[vmem] * 10 + [pl.BlockSpec(memory_space=pl.ANY), vmem],
         out_specs=[vmem] * 6,
         out_shape=[
             shape((12, 12, MODEL), BF16),
@@ -494,16 +484,13 @@
             pltpu.VMEM((6 * WINDOW, MODEL), BF16),
             pltpu.VMEM((OWN, MODEL), F32),
             pltpu.VMEM((OWN, MODEL), F32),
-            pltpu.VMEM((MODEL, 3 * MODEL), BF16),
-            pltpu.VMEM((MODEL, MODEL), BF16),
             pltpu.VMEM((4, HEADS, GROUP, WINDOW), F32),
-            pltpu.SemaphoreType.DMA((4,)),
+            pltpu.SemaphoreType.DMA,
             pltpu.VMEM((sources, 128), F32),
             pltpu.VMEM((2, 4 * sources, 128), F32),
             pltpu.VMEM((2, 4 * sources, 128), jnp.int32),
-            pltpu.VMEM((sources * 8, 128), F32),
         ],
-        compiler_params=pltpu.CompilerParams(vmem_limit_bytes=58 * 1024 * 1024),
+        compiler_params=pltpu.CompilerParams(vmem_limit_bytes=49 * 1024 * 1024),
         cost_estimate=pl.CostEstimate(
             flops=3 * 10**9, bytes_accessed=8 * 10**6, transcendentals=4 * 10**5
         ),
@@ -547,6 +534,8 @@
             shape((2 * members, 128), F32),
             shape((12, 12), F32),
         ],
+        compiler_params=pltpu.CompilerParams(vmem_limit_bytes=4 * 1024 * 1024),
+        cost_estimate=pl.CostEstimate(flops=10**4, bytes_accessed=10**5, transcendentals=0),
         name="finish",
     )(final, moved)
 
@@ -578,13 +567,10 @@
     even_lat, even_lon = lat % 2 == 0, lon % 2 == 0
 
     own = (tokens[:, :6], tokens[:, 6:])
-    near_send, far_send, observation_index = lax.optimization_barrier(
-        (
-            jnp.where(even_lon, own[1], own[0]),
-            jnp.where(even_lon, own[0], own[1]),
-            observation_index,
-        )
-    )
+    far_send, observation_index, own_later = lax.optimization_barrier(
+        (jnp.where(even_lon, own[0], own[1]), observation_index, tokens)
+    )
+    near_send = jnp.where(even_lon, own_later[:, 6:], own_later[:, :6])
     far_lon = paired(far_send, "lon", True)
 
     slots = packed_slots(

time: 124 us -> 119 us (0.960)
  Pallas kernels: 20.4 us -> 17.2 us
    pallas_call x1, Pallas kernels: 14.4 us -> 11.9 us  [core(): pl.pallas_call(functools.partial(core_kernel, loss_scale=loss_scale, lat_...]
    unnamed x16 -> x10, local copies, waits for them, and re-layouts: 1.41 us -> 0.03 us
  transfers between devices with their start and end apart: 9 -> 9, of which waited for: 5 -> 4; matrix products, arithmetic and copies ran while one was open for 3% -> 3% of each run, Pallas kernels for 4% -> 4%
where the time goes in v8:
time: 119 us; the launch traced here: 118 us
  starting transfers between devices  69.6 us (58%)
  waiting for transfers between devices  24.7 us (21%)
  Pallas kernels  17.2 us (14%)
  other arithmetic  3.18 us (3%)
  local copies, waits for them, and re-layouts  2.52 us (2%)
    ppermute x4, starting transfers between devices, paired(): return lax.ppermute(value, axis, pairs)  30.1 us
    pallas_call x1, Pallas kernels, core(): pl.pallas_call(functools.partial(core_kernel, loss_scale=loss_scale, lat_...  11.9 us
    all_to_all x1, waiting for transfers between devices, shards(): lax.all_to_all(jnp.broadcast_to(chunk[None], (2 * lat_count, 5, 128)), ('...  11.5 us
    all_to_all x1, starting transfers between devices, shards(): lax.all_to_all(slots, 'lon', 0, 0, tiled=True).reshape(lon_count * 8, 128)  8.52 us
    ppermute x1, starting transfers between devices, shards(): other = lax.ppermute(other, 'lon', [(i, i ^ 2) for i in range(lon_count)])  8.19 us
    all_to_all x1, starting transfers between devices, shards(): lax.all_to_all(final, 'lon', 0, 0, axis_index_groups=planes, tiled=True)  8.14 us
    all_to_all x1, waiting for transfers between devices, shards(): lax.all_to_all(final, 'lon', 0, 0, axis_index_groups=planes, tiled=True)  7.54 us
    all_to_all x1, starting transfers between devices, shards(): lax.all_to_all(grads.reshape(members, 4, 128), 'lon', 0, 0, axis_index_gr...  7.45 us
  transfers between devices with their start and end apart: 9, of which 4 were waited for; matrix products, arithmetic and copies ran while one was open for 3% of the time, Pallas kernels for 4%

profile of v8, /device:TPU:1, one launch (start us, length us, event | category | flops | bytes accessed | tf_op | source)
XLA Modules:
  0.0 118.1 jit_solution(17538016398199283863)
XLA Ops:
  0.6 1.0 slice_select_fusion.1
  1.7 16.8 %collective-permute-start.1 = (bf16[12,6,512]{2,1,0:T(8,128)(2,1)S(1)}, bf16[12,6,512]{2,1,0:T(8,128)(2,1)S(1)}, u32[]{:S(2)}, u32[]{:S(2)}) collective-permute-start(bf16[12,6,512]{2,1,0:T(8,128)(2,1)S(1)} %slice_select_fusion.1), channel_id=1, source_target_pairs={{0,63},{1,2},{2,1},{3,4},{4,3},{5,6},{6,5},{7,8},{8,7},{9,10},{10,... | collective-permute-start | bytes 221192 | tf_op jit(solution)/shard_map/ppermute | solution.py:549
  18.5 1.0 slice_select_fusion
  19.6 1.9 %packed_slots.1 = f32[512,128]{1,0:T(8,128)} custom-call(s32[256,128]{1,0:T(8,128)} %bitcast.58, f32[256,128]{1,0:T(8,128)} %bitcast.59, f32[64,128]{1,0:T(8,128)} %bitcast.60, s32[1,64]{1,0:T(1,128)} %bitcast.62), custom_call_target="tpu_custom_call" | custom-call | flops 1000000 | bytes 500000 | tf_op jit(solution)/shard_map/packed_slots/pallas_call | solution.py:97
  21.4 8.5 %all-to-all-start = ((f32[64,8,128]{2,1,0:T(8,128)}), f32[64,8,128]{2,1,0:T(8,128)S(1)}, u32[]{:S(2)}, u32[]{:S(2)}) async-start(f32[64,8,128]{2,1,0:T(8,128)} %bitcast.57), calls=%async_computation | async-start | bytes 524288 | tf_op jit(solution)/shard_map/all_to_all | solution.py:598
  29.9 2.5 %collective-permute-start = (bf16[12,6,512]{2,1,0:T(8,128)(2,1)S(1)}, bf16[12,6,512]{2,1,0:T(8,128)(2,1)S(1)}, u32[]{:S(2)}, u32[]{:S(2)}) collective-permute-start(bf16[12,6,512]{2,1,0:T(8,128)(2,1)S(1)} %slice_select_fusion), channel_id=1, source_target_pairs={{0,1},{1,0},{2,3},{3,2},{4,5},{5,4},{6,7},{7,6},{8,9},{9,8},{10,11... | collective-permute-start | bytes 221192 | tf_op jit(solution)/shard_map/ppermute | solution.py:549
  32.4 0.9 slice_bitcast_fusion.7
  33.4 0.0 collective-permute-done.1.far_lon_ref
  33.4 0.0 collective-permute-done.near_lon_ref
  33.4 0.1 broadcast_select_fusion
  33.5 0.7 reshape.82.readout_ref
  34.2 8.8 %collective-permute-start.2 = (bf16[4,3,6,512]{3,2,1,0:T(8,128)(2,1)S(1)}, bf16[4,3,6,512]{3,2,1,0:T(8,128)(2,1)S(1)}, u32[]{:S(2)}, u32[]{:S(2)}) collective-permute-start(bf16[4,3,6,512]{3,2,1,0:T(8,128)(2,1)S(1)} %get-tuple-element.34), channel_id=1, source_target_pairs={{0,448},{64,128},{128,64},{192,256},{256,192},{320,384},{384,320},... | collective-permute-start | bytes 221192 | tf_op jit(solution)/shard_map/ppermute | solution.py:549
  43.0 1.9 %collective-permute-start.3 = (bf16[4,3,6,512]{3,2,1,0:T(8,128)(2,1)S(1)}, bf16[4,3,6,512]{3,2,1,0:T(8,128)(2,1)S(1)}, u32[]{:S(2)}, u32[]{:S(2)}) collective-permute-start(bf16[4,3,6,512]{3,2,1,0:T(8,128)(2,1)S(1)} %get-tuple-element.35), channel_id=1, source_target_pairs={{0,64},{64,0},{128,192},{192,128},{256,320},{320,256},{384,448},{4... | collective-permute-start | bytes 221192 | tf_op jit(solution)/shard_map/ppermute | solution.py:549
  44.9 0.0 copy-start
  45.0 0.0 copy-start.1
  45.0 0.0 copy-start.2
  45.0 0.0 copy-start.3
  45.0 0.0 copy-start.4
  45.0 2.8 %ordered_bias.1.bias_hbm = f32[64,16,24,96]{3,2,1,0:T(8,128)} custom-call(f32[1152,72]{1,0:T(8,128)} %bitcast.63), custom_call_target="tpu_custom_call" | custom-call | flops 20000000000 | bytes 2000000 | tf_op jit(solution)/shard_map/ordered_bias/pallas_call | solution.py:57
  47.8 3.5 %collective-permute-done.2.far_lat_ref = bf16[4,3,6,512]{3,2,1,0:T(8,128)(2,1)S(1)} collective-permute-done((bf16[4,3,6,512]{3,2,1,0:T(8,128)(2,1)S(1)}, bf16[4,3,6,512]{3,2,1,0:T(8,128)(2,1)S(1)}, u32[]{:S(2)}, u32[]{:S(2)}) %collective-permute-start.2) | collective-permute-done | bytes 73760 | tf_op jit(solution)/shard_map/ppermute | solution.py:549
  51.3 2.1 %collective-permute-done.3.near_lat_ref = bf16[4,3,6,512]{3,2,1,0:T(8,128)(2,1)S(1)} collective-permute-done((bf16[4,3,6,512]{3,2,1,0:T(8,128)(2,1)S(1)}, bf16[4,3,6,512]{3,2,1,0:T(8,128)(2,1)S(1)}, u32[]{:S(2)}, u32[]{:S(2)}) %collective-permute-start.3) | collective-permute-done | bytes 73760 | tf_op jit(solution)/shard_map/ppermute | solution.py:549
  53.4 0.0 all-to-all-done
  53.4 0.0 copy-done
  53.4 0.0 copy-done.1
  53.4 0.0 copy-done.2
  53.4 0.0 copy-done.3
  53.4 0.0 copy-done.4
  53.4 11.9 %window_and_observe.1 = (bf16[12,12,512]{2,1,0:T(8,128)(2,1)}, f32[1,256]{1,0:T(1,128)S(1)}, f32[1,128]{1,0:T(1,128)S(1)}, f32[128,128]{1,0:T(8,128)}, f32[32,128]{1,0:T(8,128)S(1)}, /*index=5*/f32[32,128]{1,0:T(8,128)S(1)}) custom-call(bf16[12,12,512]{2,1,0:T(8,128)(2,1)S(1)} %copy-done, bf16[12,6,512]{2,1,0:T(8,128)(2,1)S(1)} %collective-permute-done.near_lon_ref, ...), custom_call_target="tpu_custom_call" | custom-call | flops 3000000000 | bytes 8000000 | tf_op jit(solution)/shard_map/window_and_observe/pallas_call | solution.py:462
  65.3 7.4 %all-to-all-start.1 = ((f32[32,4,128]{2,1,0:T(4,128)}), f32[32,4,128]{2,1,0:T(4,128)S(1)}, u32[]{:S(2)}, u32[]{:S(2)}) async-start(f32[32,4,128]{2,1,0:T(4,128)} %bitcast.17), calls=%async_computation.1 | async-start | bytes 131072 | tf_op jit(solution)/shard_map/all_to_all | solution.py:625
  72.8 8.2 %collective-permute-start.4 = (f32[32,128]{1,0:T(8,128)S(1)}, f32[32,128]{1,0:T(8,128)S(1)}, u32[]{:S(2)}, u32[]{:S(2)}) collective-permute-start(f32[32,128]{1,0:T(8,128)S(1)} %get-tuple-element.46), channel_id=1, source_target_pairs={{0,2},{1,3},{2,0},{3,1},{4,6},{5,7},{6,4},{7,5},{8,10},{9,11},{10,... | collective-permute-start | bytes 49160 | tf_op jit(solution)/shard_map/ppermute | solution.py:628
  81.0 0.0 all-to-all-done.1
  81.1 0.6 broadcast_in_dim.24
  81.7 7.2 %all-to-all-start.2 = ((f32[16,5,128]{2,1,0:T(8,128)}), f32[16,5,128]{2,1,0:T(8,128)S(1)}, u32[]{:S(2)}, u32[]{:S(2)}) async-start(f32[16,5,128]{2,1,0:T(8,128)} %broadcast_in_dim.24), calls=%async_computation.2 | async-start | bytes 131072 | tf_op jit(solution)/shard_map/all_to_all | solution.py:632
  89.0 0.1 slice_bitcast_fusion.9
  89.0 11.5 %all-to-all-done.2 = f32[16,5,128]{2,1,0:T(8,128)S(1)} async-done(((f32[16,5,128]{2,1,0:T(8,128)}), f32[16,5,128]{2,1,0:T(8,128)S(1)}, u32[]{:S(2)}, u32[]{:S(2)}) %all-to-all-start.2) | async-done | bytes 40992 | tf_op jit(solution)/shard_map/all_to_all | solution.py:632
  100.6 0.1 slice_bitcast_fusion.11
  100.7 0.1 slice_bitcast_fusion.8
  100.7 0.1 maximum_bitcast_fusion.1
  100.8 0.1 maximum_bitcast_fusion
  100.9 0.0 collective-permute-done.4
  101.0 0.7 pad_maximum_fusion
  101.7 8.1 %all-to-all-start.3 = ((f32[32,8,128]{2,1,0:T(8,128)}), f32[32,8,128]{2,1,0:T(8,128)S(1)}, u32[]{:S(2)}, u32[]{:S(2)}) async-start(f32[32,8,128]{2,1,0:T(8,128)} %pad_maximum_fusion), calls=%async_computation.3 | async-start | bytes 262144 | tf_op jit(solution)/shard_map/all_to_all | solution.py:660
  109.8 0.1 maximum_bitcast_fusion.2.moved_ref
  109.9 7.5 %all-to-all-done.3 = f32[32,8,128]{2,1,0:T(8,128)S(1)} async-done(((f32[32,8,128]{2,1,0:T(8,128)}), f32[32,8,128]{2,1,0:T(8,128)S(1)}, u32[]{:S(2)}, u32[]{:S(2)}) %all-to-all-start.3) | async-done | bytes 131104 | tf_op jit(solution)/shard_map/all_to_all | solution.py:660
  117.4 0.7 finish.1
  (12 shorter events, 0.2 us)
Async XLA Ops:
  1.7 31.7 %collective-permute-start.1 = (bf16[12,6,512]{2,1,0:T(8,128)(2,1)S(1)}, bf16[12,6,512]{2,1,0:T(8,128)(2,1)S(1)}, u32[]{:S(2)}, u32[]{:S(2)}) collective-permute-start(bf16[12,6,512]{2,1,0:T(8,128)(2,1)S(1)} %slice_select_fusion.1), channel_id=1, source_target_pairs={{0,63},{1,2},{2,1},{3,4},{4,3},{5,6},{6,5},{7,8},{8,7},{9,10},{10,... | collective-permute-start | bytes 221192 | tf_op jit(solution)/shard_map/ppermute | solution.py:549
  21.4 32.0 %all-to-all-start = ((f32[64,8,128]{2,1,0:T(8,128)}), f32[64,8,128]{2,1,0:T(8,128)S(1)}, u32[]{:S(2)}, u32[]{:S(2)}) async-start(f32[64,8,128]{2,1,0:T(8,128)} %bitcast.57), calls=%async_computation | async-start | bytes 524288 | tf_op jit(solution)/shard_map/all_to_all | solution.py:598
  29.9 3.4 %collective-permute-start = (bf16[12,6,512]{2,1,0:T(8,128)(2,1)S(1)}, bf16[12,6,512]{2,1,0:T(8,128)(2,1)S(1)}, u32[]{:S(2)}, u32[]{:S(2)}) collective-permute-start(bf16[12,6,512]{2,1,0:T(8,128)(2,1)S(1)} %slice_select_fusion), channel_id=1, source_target_pairs={{0,1},{1,0},{2,3},{3,2},{4,5},{5,4},{6,7},{7,6},{8,9},{9,8},{10,11... | collective-permute-start | bytes 221192 | tf_op jit(solution)/shard_map/ppermute | solution.py:549
  34.2 17.1 %collective-permute-start.2 = (bf16[4,3,6,512]{3,2,1,0:T(8,128)(2,1)S(1)}, bf16[4,3,6,512]{3,2,1,0:T(8,128)(2,1)S(1)}, u32[]{:S(2)}, u32[]{:S(2)}) collective-permute-start(bf16[4,3,6,512]{3,2,1,0:T(8,128)(2,1)S(1)} %get-tuple-element.34), channel_id=1, source_target_pairs={{0,448},{64,128},{128,64},{192,256},{256,192},{320,384},{384,320},... | collective-permute-start | bytes 221192 | tf_op jit(solution)/shard_map/ppermute | solution.py:549
  43.0 10.4 %collective-permute-start.3 = (bf16[4,3,6,512]{3,2,1,0:T(8,128)(2,1)S(1)}, bf16[4,3,6,512]{3,2,1,0:T(8,128)(2,1)S(1)}, u32[]{:S(2)}, u32[]{:S(2)}) collective-permute-start(bf16[4,3,6,512]{3,2,1,0:T(8,128)(2,1)S(1)} %get-tuple-element.35), channel_id=1, source_target_pairs={{0,64},{64,0},{128,192},{192,128},{256,320},{320,256},{384,448},{4... | collective-permute-start | bytes 221192 | tf_op jit(solution)/shard_map/ppermute | solution.py:549
  44.9 8.5 %copy-start = (bf16[12,12,512]{2,1,0:T(8,128)(2,1)S(1)}, bf16[12,12,512]{2,1,0:T(8,128)(2,1)}, u32[]{:S(2)}) copy-start(bf16[12,12,512]{2,1,0:T(8,128)(2,1)} %own_ref.1) | copy-start | bytes 442372
  45.0 8.5 %copy-start.1 = (bf16[512,1536]{1,0:T(8,128)(2,1)S(1)}, bf16[512,1536]{1,0:T(8,128)(2,1)}, u32[]{:S(2)}) copy-start(bf16[512,1536]{1,0:T(8,128)(2,1)} %qkv_ref.1) | copy-start | bytes 4718596
  45.0 8.4 %copy-start.2 = (bf16[512,512]{1,0:T(8,128)(2,1)S(1)}, bf16[512,512]{1,0:T(8,128)(2,1)}, u32[]{:S(2)}) copy-start(bf16[512,512]{1,0:T(8,128)(2,1)} %wo_ref.1) | copy-start | bytes 1572868
  45.0 8.4 %copy-start.3 = (bf16[2,8,512]{2,1,0:T(8,128)(2,1)S(1)}, bf16[2,8,512]{2,1,0:T(8,128)(2,1)}, u32[]{:S(2)}) copy-start(bf16[2,8,512]{2,1,0:T(8,128)(2,1)} %param.14) | copy-start | bytes 49156
  45.0 8.4 %copy-start.4 = (bf16[2,8,512]{2,1,0:T(8,128)(2,1)S(1)}, bf16[2,8,512]{2,1,0:T(8,128)(2,1)}, u32[]{:S(2)}) copy-start(bf16[2,8,512]{2,1,0:T(8,128)(2,1)} %param.15) | copy-start | bytes 49156
  65.3 15.7 %all-to-all-start.1 = ((f32[32,4,128]{2,1,0:T(4,128)}), f32[32,4,128]{2,1,0:T(4,128)S(1)}, u32[]{:S(2)}, u32[]{:S(2)}) async-start(f32[32,4,128]{2,1,0:T(4,128)} %bitcast.17), calls=%async_computation.1 | async-start | bytes 131072 | tf_op jit(solution)/shard_map/all_to_all | solution.py:625
  72.8 28.1 %collective-permute-start.4 = (f32[32,128]{1,0:T(8,128)S(1)}, f32[32,128]{1,0:T(8,128)S(1)}, u32[]{:S(2)}, u32[]{:S(2)}) collective-permute-start(f32[32,128]{1,0:T(8,128)S(1)} %get-tuple-element.46), channel_id=1, source_target_pairs={{0,2},{1,3},{2,0},{3,1},{4,6},{5,7},{6,4},{7,5},{8,10},{9,11},{10,... | collective-permute-start | bytes 49160 | tf_op jit(solution)/shard_map/ppermute | solution.py:628
  81.7 18.8 %all-to-all-start.2 = ((f32[16,5,128]{2,1,0:T(8,128)}), f32[16,5,128]{2,1,0:T(8,128)S(1)}, u32[]{:S(2)}, u32[]{:S(2)}) async-start(f32[16,5,128]{2,1,0:T(8,128)} %broadcast_in_dim.24), calls=%async_computation.2 | async-start | bytes 131072 | tf_op jit(solution)/shard_map/all_to_all | solution.py:632
  101.7 15.8 %all-to-all-start.3 = ((f32[32,8,128]{2,1,0:T(8,128)}), f32[32,8,128]{2,1,0:T(8,128)S(1)}, u32[]{:S(2)}, u32[]{:S(2)}) async-start(f32[32,8,128]{2,1,0:T(8,128)} %pad_maximum_fusion), calls=%async_computation.3 | async-start | bytes 262144 | tf_op jit(solution)/shard_map/all_to_all | solution.py:660

commit v9 on v8

--- a/solution.py
+++ b/solution.py
@@ -197,44 +197,44 @@
     masked_first = jnp.where(lane_part == 0, NEG * first, 0.0)
     masked_last = jnp.where(lane_part == 1, NEG * last, 0.0)
 
-    ones = jnp.ones((WINDOW, WINDOW), BF16)
-
-    def fold(rows):
-        return jnp.sum(jnp.where(head_mask, rows.reshape(8, GROUP, 256), 0.0), axis=0)
+    def fold(rows, size):
+        return jnp.sum(jnp.where(head_mask, rows.reshape(8, size, 256), 0.0), axis=0)
 
     bias_load.wait()
-    for n in range(8):
-        half, row = n // 4, n % 4
-        window = half * 3 + (row + 1) // 2
+    for window in range(6):
+        half, window_row = window // 3, window % 3
+        groups = ((0,), (1, 2), (3,))[window_row]
+        size = GROUP * len(groups)
+        own_rows = slice((4 * half + groups[0]) * GROUP, (4 * half + groups[0]) * GROUP + size)
         keys = slice(window * WINDOW, (window + 1) * WINDOW)
         for part in range(2):
             cols = slice(256 * part, 256 * (part + 1))
             k_win, v_win = k_ref[keys, cols], v_ref[keys, cols]
-            q_own = q_ref[n * GROUP : (n + 1) * GROUP, cols]
-            lhs = jnp.where(head_mask, q_own[None], 0.0).reshape(8 * GROUP, 256).astype(BF16)
-            bias = bias_ref[(row % 2) * 2 + half, 8 * part : 8 * part + 8].reshape(8 * GROUP, WINDOW)
+            lhs = jnp.where(head_mask, q_ref[own_rows, cols][None], 0.0)
+            lhs = lhs.reshape(8 * size, 256).astype(BF16)
+            bias = [bias_ref[(g % 2) * 2 + half, 8 * part : 8 * part + 8] for g in groups]
+            bias = jnp.concatenate(bias, axis=1).reshape(8 * size, WINDOW)
             scores = mm(lhs, k_win, NT) * scale + bias
-            if row == 0:
+            if window_row == 0:
                 scores = scores + masked_first
-            if row == 3:
+            if window_row == 2:
                 scores = scores + masked_last
             raised = jnp.exp(scores - jnp.max(scores, axis=1, keepdims=True))
             probs = raised * (1.0 / jnp.sum(raised, axis=1, keepdims=True))
-            probs_bf = probs.astype(BF16)
-            probs_ref[n, 8 * GROUP * part : 8 * GROUP * (part + 1), :] = probs_bf
-            att_ref[n * GROUP : (n + 1) * GROUP, cols] = fold(mm(probs_bf, v_win))
+            probs3 = probs.reshape(8, size, WINDOW)
+            for i, g in enumerate(groups):
+                of_group = probs3[:, GROUP * i : GROUP * (i + 1)].reshape(8 * GROUP, WINDOW)
+                rows = slice(8 * GROUP * part, 8 * GROUP * (part + 1))
+                probs_ref[4 * half + g, rows, :] = of_group.astype(BF16)
+            att_ref[own_rows, cols] = fold(mm(probs.astype(BF16), v_win), size)
             w_masked = jnp.where(head_mask[:, 0, :], w_row[:, cols], 0.0)
             w_high = w_masked.astype(BF16).astype(F32)
             w_pair = jnp.concatenate([w_high, w_masked - w_high], axis=0).astype(BF16)
             v_pair = mm(w_pair, v_win, NT)
             v_w = (v_pair[:8] + v_pair[8:]).reshape(8, 1, WINDOW)
-            v_w = jnp.broadcast_to(v_w, (8, GROUP, WINDOW)).reshape(8 * GROUP, WINDOW)
-            share = probs * v_w
-            share_high = share.astype(BF16)
-            share_low = (share - share_high.astype(F32)).astype(BF16)
-            mean = jnp.sum(share, axis=1, keepdims=True)
-            slope = (probs * (v_w - mean) * scale).astype(BF16)
-            gq_ref[n * GROUP : (n + 1) * GROUP, cols] = fold(mm(slope, k_win))
+            mean = jnp.sum(probs3 * v_w, axis=2, keepdims=True)
+            slope = (probs3 * (v_w - mean) * scale).reshape(8 * size, WINDOW).astype(BF16)
+            gq_ref[own_rows, cols] = fold(mm(slope, k_win), size)
 
     x_own = jnp.concatenate([piece(1 + n // 4, 1 + n % 4) for n in range(8)], axis=0)
     out = (x_own + mm(att_ref[...].astype(BF16), wo_ref[...])).astype(BF16)
@@ -297,7 +297,7 @@
         place_ref[1, rows, :] = places[k] & 15
 
     digit = lax.broadcasted_iota(jnp.int32, (16, 128), 0)
-    per_step = 32
+    per_step = 128
 
     def add_rows(step, total):
         left, right = [], []
@@ -587,13 +587,11 @@
     strips = (left, own[0], own[1], right)
     top = jnp.stack([strip[:3] for strip in strips])
     bottom = jnp.stack([strip[9:] for strip in strips])
-    near_send, far_send, readout = lax.optimization_barrier(
-        (jnp.where(even_lat, bottom, top), jnp.where(even_lat, top, bottom), readout)
-    )
-    far_send, readout, bias = lax.optimization_barrier(
-        (far_send, readout.reshape(1, MODEL), relative_position_bias)
-    )
-    far_lat = paired(far_send, "lat", True)
+    near_send, top, bottom, bias, readout = lax.optimization_barrier(
+        (jnp.where(even_lat, bottom, top), top, bottom, relative_position_bias, readout)
+    )
+    readout = readout.reshape(1, MODEL)
+    far_lat = paired(jnp.where(even_lat, top, bottom), "lat", True)
     near_lat = paired(near_send, "lat", False)
     slots = lax.all_to_all(slots, "lon", 0, 0, tiled=True).reshape(lon_count * 8, 128)
 

time: 119 us -> 117 us (0.983)
  Pallas kernels: 17.2 us -> 15.5 us
    pallas_call x1, Pallas kernels: 11.9 us -> 10.1 us  [core(): pl.pallas_call(functools.partial(core_kernel, loss_scale=loss_scale, lat_...]
where the time goes in v9:
time: 117 us; the launch traced here: 116 us
  starting transfers between devices  69.8 us (60%)
  waiting for transfers between devices  24.6 us (21%)
  Pallas kernels  15.5 us (13%)
  other arithmetic  3.2 us (3%)
  local copies, waits for them, and re-layouts  1.85 us (2%)
    ppermute x4, starting transfers between devices, paired(): return lax.ppermute(value, axis, pairs)  30.1 us
    all_to_all x1, waiting for transfers between devices, shards(): lax.all_to_all(jnp.broadcast_to(chunk[None], (2 * lat_count, 5, 128)), ('...  11.5 us
    pallas_call x1, Pallas kernels, core(): pl.pallas_call(functools.partial(core_kernel, loss_scale=loss_scale, lat_...  10.1 us
    all_to_all x1, starting transfers between devices, shards(): lax.all_to_all(slots, 'lon', 0, 0, tiled=True).reshape(lon_count * 8, 128)  8.53 us
    ppermute x1, starting transfers between devices, shards(): other = lax.ppermute(other, 'lon', [(i, i ^ 2) for i in range(lon_count)])  8.12 us
    all_to_all x1, starting transfers between devices, shards(): lax.all_to_all(final, 'lon', 0, 0, axis_index_groups=planes, tiled=True)  7.75 us
    all_to_all x1, starting transfers between devices, shards(): lax.all_to_all(jnp.broadcast_to(chunk[None], (2 * lat_count, 5, 128)), ('...  7.68 us
    all_to_all x1, starting transfers between devices, shards(): lax.all_to_all(grads.reshape(members, 4, 128), 'lon', 0, 0, axis_index_gr...  7.68 us
  transfers between devices with their start and end apart: 9, of which 4 were waited for; matrix products, arithmetic and copies ran while one was open for 3% of the time, Pallas kernels for 4%

profile of v9, /device:TPU:1, one launch (start us, length us, event | category | flops | bytes accessed | tf_op | source)
XLA Modules:
  0.0 116.0 jit_solution(9944361101652943234)
XLA Ops:
  0.6 1.0 slice_select_fusion.1
  1.7 16.8 %collective-permute-start.1 = (bf16[12,6,512]{2,1,0:T(8,128)(2,1)S(1)}, bf16[12,6,512]{2,1,0:T(8,128)(2,1)S(1)}, u32[]{:S(2)}, u32[]{:S(2)}) collective-permute-start(bf16[12,6,512]{2,1,0:T(8,128)(2,1)S(1)} %slice_select_fusion.1), channel_id=1, source_target_pairs={{0,63},{1,2},{2,1},{3,4},{4,3},{5,6},{6,5},{7,8},{8,7},{9,10},{10,... | collective-permute-start | bytes 221192 | tf_op jit(solution)/shard_map/ppermute | solution.py:549
  18.5 1.0 slice_select_fusion
  19.6 1.9 %packed_slots.1 = f32[512,128]{1,0:T(8,128)} custom-call(s32[256,128]{1,0:T(8,128)} %bitcast.58, f32[256,128]{1,0:T(8,128)} %bitcast.59, f32[64,128]{1,0:T(8,128)} %bitcast.60, s32[1,64]{1,0:T(1,128)} %bitcast.62), custom_call_target="tpu_custom_call" | custom-call | flops 1000000 | bytes 500000 | tf_op jit(solution)/shard_map/packed_slots/pallas_call | solution.py:97
  21.4 8.5 %all-to-all-start = ((f32[64,8,128]{2,1,0:T(8,128)}), f32[64,8,128]{2,1,0:T(8,128)S(1)}, u32[]{:S(2)}, u32[]{:S(2)}) async-start(f32[64,8,128]{2,1,0:T(8,128)} %bitcast.57), calls=%async_computation | async-start | bytes 524288 | tf_op jit(solution)/shard_map/all_to_all | solution.py:596
  30.0 2.5 %collective-permute-start = (bf16[12,6,512]{2,1,0:T(8,128)(2,1)S(1)}, bf16[12,6,512]{2,1,0:T(8,128)(2,1)S(1)}, u32[]{:S(2)}, u32[]{:S(2)}) collective-permute-start(bf16[12,6,512]{2,1,0:T(8,128)(2,1)S(1)} %slice_select_fusion), channel_id=1, source_target_pairs={{0,1},{1,0},{2,3},{3,2},{4,5},{5,4},{6,7},{7,6},{8,9},{9,8},{10,11... | collective-permute-start | bytes 221192 | tf_op jit(solution)/shard_map/ppermute | solution.py:549
  32.4 0.9 slice_bitcast_fusion.7
  33.4 0.0 collective-permute-done.1.far_lon_ref
  33.4 0.0 collective-permute-done.near_lon_ref
  33.4 0.1 pad_maximum_fusion.1
  33.5 8.8 %collective-permute-start.2 = (bf16[4,3,6,512]{3,2,1,0:T(8,128)(2,1)S(1)}, bf16[4,3,6,512]{3,2,1,0:T(8,128)(2,1)S(1)}, u32[]{:S(2)}, u32[]{:S(2)}) collective-permute-start(bf16[4,3,6,512]{3,2,1,0:T(8,128)(2,1)S(1)} %broadcast_select_fusion), channel_id=1, source_target_pairs={{0,448},{64,128},{128,64},{192,256},{256,192},{320,384},{384,320},... | collective-permute-start | bytes 221192 | tf_op jit(solution)/shard_map/ppermute | solution.py:549
  42.4 1.9 %collective-permute-start.3 = (bf16[4,3,6,512]{3,2,1,0:T(8,128)(2,1)S(1)}, bf16[4,3,6,512]{3,2,1,0:T(8,128)(2,1)S(1)}, u32[]{:S(2)}, u32[]{:S(2)}) collective-permute-start(bf16[4,3,6,512]{3,2,1,0:T(8,128)(2,1)S(1)} %get-tuple-element.33), channel_id=1, source_target_pairs={{0,64},{64,0},{128,192},{192,128},{256,320},{320,256},{384,448},{4... | collective-permute-start | bytes 221192 | tf_op jit(solution)/shard_map/ppermute | solution.py:549
  44.3 0.0 copy-start.5
  44.3 0.0 copy-start
  44.3 0.0 copy-start.1
  44.3 0.0 copy-start.2
  44.3 0.0 copy-start.3
  44.3 0.0 copy-start.4
  44.4 2.8 %ordered_bias.1.bias_hbm = f32[64,16,24,96]{3,2,1,0:T(8,128)} custom-call(f32[1152,72]{1,0:T(8,128)} %bitcast.63), custom_call_target="tpu_custom_call" | custom-call | flops 20000000000 | bytes 2000000 | tf_op jit(solution)/shard_map/ordered_bias/pallas_call | solution.py:57
  47.2 0.0 copy-done.5
  47.2 3.4 %collective-permute-done.2.far_lat_ref = bf16[4,3,6,512]{3,2,1,0:T(8,128)(2,1)S(1)} collective-permute-done((bf16[4,3,6,512]{3,2,1,0:T(8,128)(2,1)S(1)}, bf16[4,3,6,512]{3,2,1,0:T(8,128)(2,1)S(1)}, u32[]{:S(2)}, u32[]{:S(2)}) %collective-permute-start.2) | collective-permute-done | bytes 73760 | tf_op jit(solution)/shard_map/ppermute | solution.py:549
  50.6 2.1 %collective-permute-done.3.near_lat_ref = bf16[4,3,6,512]{3,2,1,0:T(8,128)(2,1)S(1)} collective-permute-done((bf16[4,3,6,512]{3,2,1,0:T(8,128)(2,1)S(1)}, bf16[4,3,6,512]{3,2,1,0:T(8,128)(2,1)S(1)}, u32[]{:S(2)}, u32[]{:S(2)}) %collective-permute-start.3) | collective-permute-done | bytes 73760 | tf_op jit(solution)/shard_map/ppermute | solution.py:549
  52.8 0.0 all-to-all-done
  52.8 0.0 copy-done
  52.8 0.0 copy-done.1
  52.8 0.0 copy-done.2
  52.8 0.0 copy-done.3
  52.8 0.0 copy-done.4
  52.8 10.1 %window_and_observe.1 = (bf16[12,12,512]{2,1,0:T(8,128)(2,1)}, f32[1,256]{1,0:T(1,128)S(1)}, f32[1,128]{1,0:T(1,128)S(1)}, f32[128,128]{1,0:T(8,128)}, f32[32,128]{1,0:T(8,128)S(1)}, /*index=5*/f32[32,128]{1,0:T(8,128)S(1)}) custom-call(bf16[12,12,512]{2,1,0:T(8,128)(2,1)S(1)} %copy-done, bf16[12,6,512]{2,1,0:T(8,128)(2,1)S(1)} %collective-permute-done.near_lon_ref, ...), custom_call_target="tpu_custom_call" | custom-call | flops 3000000000 | bytes 8000000 | tf_op jit(solution)/shard_map/window_and_observe/pallas_call | solution.py:462
  62.9 7.7 %all-to-all-start.1 = ((f32[32,4,128]{2,1,0:T(4,128)}), f32[32,4,128]{2,1,0:T(4,128)S(1)}, u32[]{:S(2)}, u32[]{:S(2)}) async-start(f32[32,4,128]{2,1,0:T(4,128)} %bitcast.17), calls=%async_computation.1 | async-start | bytes 131072 | tf_op jit(solution)/shard_map/all_to_all | solution.py:623
  70.7 8.1 %collective-permute-start.4 = (f32[32,128]{1,0:T(8,128)S(1)}, f32[32,128]{1,0:T(8,128)S(1)}, u32[]{:S(2)}, u32[]{:S(2)}) collective-permute-start(f32[32,128]{1,0:T(8,128)S(1)} %get-tuple-element.44), channel_id=1, source_target_pairs={{0,2},{1,3},{2,0},{3,1},{4,6},{5,7},{6,4},{7,5},{8,10},{9,11},{10,... | collective-permute-start | bytes 49160 | tf_op jit(solution)/shard_map/ppermute | solution.py:626
  78.8 0.0 all-to-all-done.1
  78.9 0.6 broadcast_in_dim.24
  79.5 7.7 %all-to-all-start.2 = ((f32[16,5,128]{2,1,0:T(8,128)}), f32[16,5,128]{2,1,0:T(8,128)S(1)}, u32[]{:S(2)}, u32[]{:S(2)}) async-start(f32[16,5,128]{2,1,0:T(8,128)} %broadcast_in_dim.24), calls=%async_computation.2 | async-start | bytes 131072 | tf_op jit(solution)/shard_map/all_to_all | solution.py:630
  87.2 0.1 slice_bitcast_fusion.9
  87.3 11.5 %all-to-all-done.2 = f32[16,5,128]{2,1,0:T(8,128)S(1)} async-done(((f32[16,5,128]{2,1,0:T(8,128)}), f32[16,5,128]{2,1,0:T(8,128)S(1)}, u32[]{:S(2)}, u32[]{:S(2)}) %all-to-all-start.2) | async-done | bytes 40992 | tf_op jit(solution)/shard_map/all_to_all | solution.py:630
  98.8 0.1 slice_bitcast_fusion.11
  98.9 0.1 slice_bitcast_fusion.8
  99.0 0.1 maximum_bitcast_fusion.1
  99.0 0.1 maximum_bitcast_fusion
  99.2 0.0 collective-permute-done.4
  99.2 0.7 pad_maximum_fusion
  99.9 7.7 %all-to-all-start.3 = ((f32[32,8,128]{2,1,0:T(8,128)}), f32[32,8,128]{2,1,0:T(8,128)S(1)}, u32[]{:S(2)}, u32[]{:S(2)}) async-start(f32[32,8,128]{2,1,0:T(8,128)} %pad_maximum_fusion), calls=%async_computation.3 | async-start | bytes 262144 | tf_op jit(solution)/shard_map/all_to_all | solution.py:658
  107.7 0.1 maximum_bitcast_fusion.2.moved_ref
  107.7 7.5 %all-to-all-done.3 = f32[32,8,128]{2,1,0:T(8,128)S(1)} async-done(((f32[32,8,128]{2,1,0:T(8,128)}), f32[32,8,128]{2,1,0:T(8,128)S(1)}, u32[]{:S(2)}, u32[]{:S(2)}) %all-to-all-start.3) | async-done | bytes 131104 | tf_op jit(solution)/shard_map/all_to_all | solution.py:658
  115.3 0.7 finish.1
  (14 shorter events, 0.2 us)
Async XLA Ops:
  1.7 31.7 %collective-permute-start.1 = (bf16[12,6,512]{2,1,0:T(8,128)(2,1)S(1)}, bf16[12,6,512]{2,1,0:T(8,128)(2,1)S(1)}, u32[]{:S(2)}, u32[]{:S(2)}) collective-permute-start(bf16[12,6,512]{2,1,0:T(8,128)(2,1)S(1)} %slice_select_fusion.1), channel_id=1, source_target_pairs={{0,63},{1,2},{2,1},{3,4},{4,3},{5,6},{6,5},{7,8},{8,7},{9,10},{10,... | collective-permute-start | bytes 221192 | tf_op jit(solution)/shard_map/ppermute | solution.py:549
  21.4 31.3 %all-to-all-start = ((f32[64,8,128]{2,1,0:T(8,128)}), f32[64,8,128]{2,1,0:T(8,128)S(1)}, u32[]{:S(2)}, u32[]{:S(2)}) async-start(f32[64,8,128]{2,1,0:T(8,128)} %bitcast.57), calls=%async_computation | async-start | bytes 524288 | tf_op jit(solution)/shard_map/all_to_all | solution.py:596
  30.0 3.4 %collective-permute-start = (bf16[12,6,512]{2,1,0:T(8,128)(2,1)S(1)}, bf16[12,6,512]{2,1,0:T(8,128)(2,1)S(1)}, u32[]{:S(2)}, u32[]{:S(2)}) collective-permute-start(bf16[12,6,512]{2,1,0:T(8,128)(2,1)S(1)} %slice_select_fusion), channel_id=1, source_target_pairs={{0,1},{1,0},{2,3},{3,2},{4,5},{5,4},{6,7},{7,6},{8,9},{9,8},{10,11... | collective-permute-start | bytes 221192 | tf_op jit(solution)/shard_map/ppermute | solution.py:549
  33.5 17.1 %collective-permute-start.2 = (bf16[4,3,6,512]{3,2,1,0:T(8,128)(2,1)S(1)}, bf16[4,3,6,512]{3,2,1,0:T(8,128)(2,1)S(1)}, u32[]{:S(2)}, u32[]{:S(2)}) collective-permute-start(bf16[4,3,6,512]{3,2,1,0:T(8,128)(2,1)S(1)} %broadcast_select_fusion), channel_id=1, source_target_pairs={{0,448},{64,128},{128,64},{192,256},{256,192},{320,384},{384,320},... | collective-permute-start | bytes 221192 | tf_op jit(solution)/shard_map/ppermute | solution.py:549
  42.4 10.4 %collective-permute-start.3 = (bf16[4,3,6,512]{3,2,1,0:T(8,128)(2,1)S(1)}, bf16[4,3,6,512]{3,2,1,0:T(8,128)(2,1)S(1)}, u32[]{:S(2)}, u32[]{:S(2)}) collective-permute-start(bf16[4,3,6,512]{3,2,1,0:T(8,128)(2,1)S(1)} %get-tuple-element.33), channel_id=1, source_target_pairs={{0,64},{64,0},{128,192},{192,128},{256,320},{320,256},{384,448},{4... | collective-permute-start | bytes 221192 | tf_op jit(solution)/shard_map/ppermute | solution.py:549
  44.3 2.9 %copy-start.5 = (bf16[512]{0:T(512)(128)(2,1)S(1)}, bf16[512]{0:T(512)(128)(2,1)}, u32[]{:S(2)}) copy-start(bf16[512]{0:T(512)(128)(2,1)} %param.17) | copy-start | bytes 3076
  44.3 8.5 %copy-start = (bf16[12,12,512]{2,1,0:T(8,128)(2,1)S(1)}, bf16[12,12,512]{2,1,0:T(8,128)(2,1)}, u32[]{:S(2)}) copy-start(bf16[12,12,512]{2,1,0:T(8,128)(2,1)} %own_ref.1) | copy-start | bytes 442372
  44.3 8.4 %copy-start.1 = (bf16[512,1536]{1,0:T(8,128)(2,1)S(1)}, bf16[512,1536]{1,0:T(8,128)(2,1)}, u32[]{:S(2)}) copy-start(bf16[512,1536]{1,0:T(8,128)(2,1)} %qkv_ref.1) | copy-start | bytes 4718596
  44.3 8.4 %copy-start.2 = (bf16[512,512]{1,0:T(8,128)(2,1)S(1)}, bf16[512,512]{1,0:T(8,128)(2,1)}, u32[]{:S(2)}) copy-start(bf16[512,512]{1,0:T(8,128)(2,1)} %wo_ref.1) | copy-start | bytes 1572868
  44.3 8.4 %copy-start.3 = (bf16[2,8,512]{2,1,0:T(8,128)(2,1)S(1)}, bf16[2,8,512]{2,1,0:T(8,128)(2,1)}, u32[]{:S(2)}) copy-start(bf16[2,8,512]{2,1,0:T(8,128)(2,1)} %param.14) | copy-start | bytes 49156
  44.3 8.4 %copy-start.4 = (bf16[2,8,512]{2,1,0:T(8,128)(2,1)S(1)}, bf16[2,8,512]{2,1,0:T(8,128)(2,1)}, u32[]{:S(2)}) copy-start(bf16[2,8,512]{2,1,0:T(8,128)(2,1)} %param.15) | copy-start | bytes 49156
  62.9 15.9 %all-to-all-start.1 = ((f32[32,4,128]{2,1,0:T(4,128)}), f32[32,4,128]{2,1,0:T(4,128)S(1)}, u32[]{:S(2)}, u32[]{:S(2)}) async-start(f32[32,4,128]{2,1,0:T(4,128)} %bitcast.17), calls=%async_computation.1 | async-start | bytes 131072 | tf_op jit(solution)/shard_map/all_to_all | solution.py:623
  70.7 28.5 %collective-permute-start.4 = (f32[32,128]{1,0:T(8,128)S(1)}, f32[32,128]{1,0:T(8,128)S(1)}, u32[]{:S(2)}, u32[]{:S(2)}) collective-permute-start(f32[32,128]{1,0:T(8,128)S(1)} %get-tuple-element.44), channel_id=1, source_target_pairs={{0,2},{1,3},{2,0},{3,1},{4,6},{5,7},{6,4},{7,5},{8,10},{9,11},{10,... | collective-permute-start | bytes 49160 | tf_op jit(solution)/shard_map/ppermute | solution.py:626
  79.5 19.3 %all-to-all-start.2 = ((f32[16,5,128]{2,1,0:T(8,128)}), f32[16,5,128]{2,1,0:T(8,128)S(1)}, u32[]{:S(2)}, u32[]{:S(2)}) async-start(f32[16,5,128]{2,1,0:T(8,128)} %broadcast_in_dim.24), calls=%async_computation.2 | async-start | bytes 131072 | tf_op jit(solution)/shard_map/all_to_all | solution.py:630
  99.9 15.4 %all-to-all-start.3 = ((f32[32,8,128]{2,1,0:T(8,128)}), f32[32,8,128]{2,1,0:T(8,128)S(1)}, u32[]{:S(2)}, u32[]{:S(2)}) async-start(f32[32,8,128]{2,1,0:T(8,128)} %pad_maximum_fusion), calls=%async_computation.3 | async-start | bytes 262144 | tf_op jit(solution)/shard_map/all_to_all | solution.py:658

commit v10 on v9

--- a/solution.py
+++ b/solution.py
@@ -26,6 +26,14 @@
 
 def mm(a, b, dims=NN, precision=None):
     return lax.dot_general(a, b, dims, precision=precision, preferred_element_type=F32)
+
+
+def parts_of(x, count):
+    parts = []
+    for _ in range(count):
+        parts.append(x.astype(BF16))
+        x = x - parts[-1].astype(F32)
+    return parts
 
 
 def exact(a, b, dims=NN):
@@ -69,7 +77,11 @@
     )(bias.reshape(HEADS * 72, 72))
 
 
-def slots_kernel(index_ref, weight_ref, value_ref, count_ref, out_ref):
+def slots_kernel(index_ref, weight_ref, value_ref, count_ref, tokens_ref, out_ref, near_ref):
+    even = lax.axis_index("lon") % 2 == 0
+    for row in range(tokens_ref.shape[0]):
+        x = tokens_ref[row].astype(F32)
+        near_ref[row] = jnp.where(even, x[6:], x[:6]).astype(BF16)
     strips = value_ref.shape[0]
     square = (strips, strips)
     own_lane = lax.broadcasted_iota(jnp.int32, square, 0) == lax.broadcasted_iota(jnp.int32, square, 1)
@@ -93,13 +105,16 @@
     out_ref[pl.ds(7, strips, stride=8), :] = jnp.zeros((strips, 128), F32)
 
 
-def packed_slots(index, weight, value, count):
+def packed_slots(index, weight, value, count, tokens):
     return pl.pallas_call(
         slots_kernel,
-        out_shape=jax.ShapeDtypeStruct((value.shape[0] * 8, 128), F32),
+        out_shape=[
+            jax.ShapeDtypeStruct((value.shape[0] * 8, 128), F32),
+            jax.ShapeDtypeStruct((12, 6, MODEL), BF16),
+        ],
         cost_estimate=pl.CostEstimate(flops=10**6, bytes_accessed=5 * 10**5, transcendentals=0),
         name="packed_slots",
-    )(index, weight, value, count)
+    )(index, weight, value, count, tokens)
 
 
 def forward_part(
@@ -317,11 +332,16 @@
         digits = lax.broadcasted_iota(jnp.int32, shape, 1 - axis)
         return cell // 16 == digits, cell % 16 == digits
 
-    high, low = cells((OWN, 16), 0)
-    column = exact(high.astype(F32), total)
+    total = jnp.concatenate([part.astype(F32) for part in parts_of(total, 3)], axis=0).astype(BF16)
+    cell = lax.broadcasted_iota(jnp.int32, (OWN, 48), 0)
+    high = cell // 16 == lax.broadcasted_iota(jnp.int32, (OWN, 48), 1) % 16
+    column = mm(jnp.where(high, 1.0, 0.0).astype(BF16), total)
+    low = cells((OWN, 16), 0)[1]
     adjoint = jnp.sum(jnp.where(low, column, 0.0), axis=1, keepdims=True)
     high, low = cells((16, OWN), 1)
-    row = jnp.sum(jnp.where(high, exact(total, low.astype(F32)), 0.0), axis=0, keepdims=True)
+    row = mm(total, jnp.where(low, 1.0, 0.0).astype(BF16))
+    row = jnp.where(high, row[:16] + row[16:32] + row[32:], 0.0)
+    row = jnp.sum(row, axis=0, keepdims=True)
     adjoint_ref[...] = jnp.concatenate([row, jnp.zeros((1, 256 - OWN), F32)], axis=1)
     edge_ref[...] = row[:, :128]
     low_plane = (lax.axis_index("lon") // 2) % 2 == 0
@@ -347,14 +367,23 @@
     head = lax.broadcasted_iota(jnp.int32, (HEADS, MODEL), 0)
     of_head = head == lax.broadcasted_iota(jnp.int32, (HEADS, MODEL), 1) // HEAD_DIM
     w_masked = jnp.where(of_head, jnp.broadcast_to(w_ref[0:1, :], (HEADS, MODEL)), 0.0)
-    rank_head = exact(up.astype(F32), w_masked, NT)
+    w_high, w_low = [part.astype(F32) for part in parts_of(w_masked, 2)]
+    rank_head = mm(up, w_high.astype(BF16), NT) + mm(up, w_low.astype(BF16), NT)
+    rank_head = [part.astype(F32) for part in parts_of(rank_head, 2)]
+    rank_head = jnp.concatenate(rank_head, axis=0).astype(BF16)
     sums, down_value = jnp.zeros((HEADS, 16), F32), jnp.zeros((16, MODEL), F32)
     for window in range(6):
         keys = slice(window * WINDOW, (window + 1) * WINDOW)
         sums = sums + mm(weighted[window].astype(BF16), low_ref[keys, :])
-        of_rank = exact(rank_head, weighted[window])
-        down_value = down_value + mm(of_rank.astype(BF16), norm_ref[keys, :])
-    up_value = exact(sums, w_masked, TN)
+        of_rank = sum(mm(rank_head, part) for part in parts_of(weighted[window], 2))
+        of_rank = (of_rank[:HEADS] + of_rank[HEADS:]).astype(BF16)
+        down_value = down_value + mm(of_rank, norm_ref[keys, :])
+    high, low = [part.astype(F32) for part in parts_of(sums, 2)]
+    up_value = mm(
+        jnp.concatenate([high, high, low], axis=0).astype(BF16),
+        jnp.concatenate([w_high, w_low, w_high], axis=0).astype(BF16),
+        TN,
+    )
 
     parts = (up_query[:8], up_value[8:], down_query[:8], down_value[8:])
     for m, part in enumerate(parts):
@@ -567,19 +596,19 @@
     even_lat, even_lon = lat % 2 == 0, lon % 2 == 0
 
     own = (tokens[:, :6], tokens[:, 6:])
-    far_send, observation_index, own_later = lax.optimization_barrier(
-        (jnp.where(even_lon, own[0], own[1]), observation_index, tokens)
-    )
-    near_send = jnp.where(even_lon, own_later[:, 6:], own_later[:, :6])
+    far_send, observation_index = lax.optimization_barrier(
+        (jnp.where(even_lon, own[0], own[1]), observation_index)
+    )
     far_lon = paired(far_send, "lon", True)
 
-    slots = packed_slots(
+    slots, near_send = packed_slots(
         observation_index.reshape(lon_count * 4, 128),
         observation_weight.reshape(lon_count * 4, 128),
         observation_value.reshape(lon_count, 128),
         observation_count.reshape(1, lon_count),
-    ).reshape(lon_count, 8, 128)
-    near_send, slots = lax.optimization_barrier((near_send, slots))
+        tokens,
+    )
+    slots = slots.reshape(lon_count, 8, 128)
     near_lon = paired(near_send, "lon", False)
 
     left = jnp.where(even_lon, far_lon, near_lon)

time: 117 us -> 115 us (0.983)
  transfers between devices with their start and end apart: 9 -> 9, of which waited for: 4 -> 5; matrix products, arithmetic and copies ran while one was open for 3% -> 2% of each run, Pallas kernels for 4% -> 4%
where the time goes in v10:
time: 115 us
  starting transfers between devices  69.7 us (61%)
  waiting for transfers between devices  25 us (22%)
  Pallas kernels  15 us (13%)
  other arithmetic  2.17 us (2%)
  local copies, waits for them, and re-layouts  1.84 us (2%)
    ppermute x4, starting transfers between devices, paired(): return lax.ppermute(value, axis, pairs)  30.1 us
    all_to_all x1, waiting for transfers between devices, shards(): lax.all_to_all(jnp.broadcast_to(chunk[None], (2 * lat_count, 5, 128)), ('...  11.5 us
    pallas_call x1, Pallas kernels, core(): pl.pallas_call(functools.partial(core_kernel, loss_scale=loss_scale, lat_...  9.45 us
    all_to_all x1, starting transfers between devices, shards(): lax.all_to_all(slots, 'lon', 0, 0, tiled=True).reshape(lon_count * 8, 128)  8.52 us
    ppermute x1, starting transfers between devices, shards(): other = lax.ppermute(other, 'lon', [(i, i ^ 2) for i in range(lon_count)])  8.09 us
    all_to_all x1, starting transfers between devices, shards(): lax.all_to_all(final, 'lon', 0, 0, axis_index_groups=planes, tiled=True)  7.92 us
    all_to_all x1, starting transfers between devices, shards(): lax.all_to_all(jnp.broadcast_to(chunk[None], (2 * lat_count, 5, 128)), ('...  7.54 us
    all_to_all x1, waiting for transfers between devices, shards(): lax.all_to_all(final, 'lon', 0, 0, axis_index_groups=planes, tiled=True)  7.54 us
  transfers between devices with their start and end apart: 9, of which 5 were waited for; matrix products, arithmetic and copies ran while one was open for 2% of the time, Pallas kernels for 4%

profile of v10, /device:TPU:1, one launch (start us, length us, event | category | flops | bytes accessed | tf_op | source)
XLA Modules:
  0.0 114.6 jit_solution(10173200283782252943)
XLA Ops:
  0.6 1.0 slice_select_fusion
  1.7 16.8 %collective-permute-start.1 = (bf16[12,6,512]{2,1,0:T(8,128)(2,1)S(1)}, bf16[12,6,512]{2,1,0:T(8,128)(2,1)S(1)}, u32[]{:S(2)}, u32[]{:S(2)}) collective-permute-start(bf16[12,6,512]{2,1,0:T(8,128)(2,1)S(1)} %slice_select_fusion), channel_id=1, source_target_pairs={{0,63},{1,2},{2,1},{3,4},{4,3},{5,6},{6,5},{7,8},{8,7},{9,10},{10,... | collective-permute-start | bytes 221192 | tf_op jit(solution)/shard_map/ppermute | solution.py:578
  18.5 2.0 %packed_slots.1 = (f32[512,128]{1,0:T(8,128)}, bf16[12,6,512]{2,1,0:T(8,128)(2,1)}) custom-call(s32[256,128]{1,0:T(8,128)} %bitcast.58, f32[256,128]{1,0:T(8,128)} %bitcast.59, f32[64,128]{1,0:T(8,128)} %bitcast.60, s32[1,64]{1,0:T(1,128)} %bitcast.62, bf16[12,12,512]{2,1,0:T(8,128)(2,1)} %own_ref.1), custom_call_target="tpu_custom_call" | custom-call | flops 1000000 | bytes 500000 | tf_op jit(solution)/shard_map/packed_slots/pallas_call | solution.py:109
  20.5 8.5 %all-to-all-start = ((f32[64,8,128]{2,1,0:T(8,128)}), f32[64,8,128]{2,1,0:T(8,128)S(1)}, u32[]{:S(2)}, u32[]{:S(2)}) async-start(f32[64,8,128]{2,1,0:T(8,128)} %bitcast.57), calls=%async_computation | async-start | bytes 524288 | tf_op jit(solution)/shard_map/all_to_all | solution.py:625
  29.1 2.5 %collective-permute-start = (bf16[12,6,512]{2,1,0:T(8,128)(2,1)}, bf16[12,6,512]{2,1,0:T(8,128)(2,1)S(1)}, u32[]{:S(2)}, u32[]{:S(2)}) collective-permute-start(bf16[12,6,512]{2,1,0:T(8,128)(2,1)} %get-tuple-element.27), channel_id=1, source_target_pairs={{0,1},{1,0},{2,3},{3,2},{4,5},{5,4},{6,7},{7,6},{8,9},{9,8},{10,11... | collective-permute-start | bytes 221192 | tf_op jit(solution)/shard_map/ppermute | solution.py:578
  31.5 0.9 slice_bitcast_fusion.7
  32.5 0.0 collective-permute-done.1.far_lon_ref
  32.5 0.2 collective-permute-done.near_lon_ref
  32.7 0.1 pad_maximum_fusion.1
  32.8 8.8 %collective-permute-start.2 = (bf16[4,3,6,512]{3,2,1,0:T(8,128)(2,1)S(1)}, bf16[4,3,6,512]{3,2,1,0:T(8,128)(2,1)S(1)}, u32[]{:S(2)}, u32[]{:S(2)}) collective-permute-start(bf16[4,3,6,512]{3,2,1,0:T(8,128)(2,1)S(1)} %broadcast_select_fusion), channel_id=1, source_target_pairs={{0,448},{64,128},{128,64},{192,256},{256,192},{320,384},{384,320},... | collective-permute-start | bytes 221192 | tf_op jit(solution)/shard_map/ppermute | solution.py:578
  41.7 1.9 %collective-permute-start.3 = (bf16[4,3,6,512]{3,2,1,0:T(8,128)(2,1)S(1)}, bf16[4,3,6,512]{3,2,1,0:T(8,128)(2,1)S(1)}, u32[]{:S(2)}, u32[]{:S(2)}) collective-permute-start(bf16[4,3,6,512]{3,2,1,0:T(8,128)(2,1)S(1)} %get-tuple-element.31), channel_id=1, source_target_pairs={{0,64},{64,0},{128,192},{192,128},{256,320},{320,256},{384,448},{4... | collective-permute-start | bytes 221192 | tf_op jit(solution)/shard_map/ppermute | solution.py:578
  43.6 0.0 copy-start.5
  43.6 0.0 copy-start
  43.6 0.0 copy-start.1
  43.6 0.0 copy-start.2
  43.6 0.0 copy-start.3
  43.7 0.0 copy-start.4
  43.7 2.8 %ordered_bias.1.bias_hbm = f32[64,16,24,96]{3,2,1,0:T(8,128)} custom-call(f32[1152,72]{1,0:T(8,128)} %bitcast.63), custom_call_target="tpu_custom_call" | custom-call | flops 20000000000 | bytes 2000000 | tf_op jit(solution)/shard_map/ordered_bias/pallas_call | solution.py:65
  46.5 0.0 copy-done.5
  46.5 3.6 %collective-permute-done.2.far_lat_ref = bf16[4,3,6,512]{3,2,1,0:T(8,128)(2,1)S(1)} collective-permute-done((bf16[4,3,6,512]{3,2,1,0:T(8,128)(2,1)S(1)}, bf16[4,3,6,512]{3,2,1,0:T(8,128)(2,1)S(1)}, u32[]{:S(2)}, u32[]{:S(2)}) %collective-permute-start.2) | collective-permute-done | bytes 73760 | tf_op jit(solution)/shard_map/ppermute | solution.py:578
  50.1 2.1 %collective-permute-done.3.near_lat_ref = bf16[4,3,6,512]{3,2,1,0:T(8,128)(2,1)S(1)} collective-permute-done((bf16[4,3,6,512]{3,2,1,0:T(8,128)(2,1)S(1)}, bf16[4,3,6,512]{3,2,1,0:T(8,128)(2,1)S(1)}, u32[]{:S(2)}, u32[]{:S(2)}) %collective-permute-start.3) | collective-permute-done | bytes 73760 | tf_op jit(solution)/shard_map/ppermute | solution.py:578
  52.2 0.0 all-to-all-done
  52.2 0.0 copy-done
  52.2 0.0 copy-done.1
  52.3 0.0 copy-done.2
  52.3 0.0 copy-done.3
  52.3 0.0 copy-done.4
  52.3 9.4 %window_and_observe.1 = (bf16[12,12,512]{2,1,0:T(8,128)(2,1)}, f32[1,256]{1,0:T(1,128)S(1)}, f32[1,128]{1,0:T(1,128)S(1)}, f32[128,128]{1,0:T(8,128)}, f32[32,128]{1,0:T(8,128)S(1)}, /*index=5*/f32[32,128]{1,0:T(8,128)S(1)}) custom-call(bf16[12,12,512]{2,1,0:T(8,128)(2,1)S(1)} %copy-done, bf16[12,6,512]{2,1,0:T(8,128)(2,1)S(1)} %collective-permute-done.near_lon_ref, ...), custom_call_target="tpu_custom_call" | custom-call | flops 3000000000 | bytes 8000000 | tf_op jit(solution)/shard_map/window_and_observe/pallas_call | solution.py:491
  61.7 7.5 %all-to-all-start.1 = ((f32[32,4,128]{2,1,0:T(4,128)}), f32[32,4,128]{2,1,0:T(4,128)S(1)}, u32[]{:S(2)}, u32[]{:S(2)}) async-start(f32[32,4,128]{2,1,0:T(4,128)} %bitcast.17), calls=%async_computation.1 | async-start | bytes 131072 | tf_op jit(solution)/shard_map/all_to_all | solution.py:652
  69.3 8.1 %collective-permute-start.4 = (f32[32,128]{1,0:T(8,128)S(1)}, f32[32,128]{1,0:T(8,128)S(1)}, u32[]{:S(2)}, u32[]{:S(2)}) collective-permute-start(f32[32,128]{1,0:T(8,128)S(1)} %get-tuple-element.42), channel_id=1, source_target_pairs={{0,2},{1,3},{2,0},{3,1},{4,6},{5,7},{6,4},{7,5},{8,10},{9,11},{10,... | collective-permute-start | bytes 49160 | tf_op jit(solution)/shard_map/ppermute | solution.py:655
  77.4 0.0 all-to-all-done.1
  77.5 0.6 broadcast_in_dim.24
  78.1 7.5 %all-to-all-start.2 = ((f32[16,5,128]{2,1,0:T(8,128)}), f32[16,5,128]{2,1,0:T(8,128)S(1)}, u32[]{:S(2)}, u32[]{:S(2)}) async-start(f32[16,5,128]{2,1,0:T(8,128)} %broadcast_in_dim.24), calls=%async_computation.2 | async-start | bytes 131072 | tf_op jit(solution)/shard_map/all_to_all | solution.py:659
  85.7 0.1 slice_bitcast_fusion.9
  85.7 11.5 %all-to-all-done.2 = f32[16,5,128]{2,1,0:T(8,128)S(1)} async-done(((f32[16,5,128]{2,1,0:T(8,128)}), f32[16,5,128]{2,1,0:T(8,128)S(1)}, u32[]{:S(2)}, u32[]{:S(2)}) %all-to-all-start.2) | async-done | bytes 40992 | tf_op jit(solution)/shard_map/all_to_all | solution.py:659
  97.3 0.1 slice_bitcast_fusion.11
  97.4 0.1 slice_bitcast_fusion.8
  97.4 0.1 maximum_bitcast_fusion.1
  97.5 0.1 maximum_bitcast_fusion
  97.6 0.0 collective-permute-done.4
  97.7 0.7 pad_maximum_fusion
  98.4 7.9 %all-to-all-start.3 = ((f32[32,8,128]{2,1,0:T(8,128)}), f32[32,8,128]{2,1,0:T(8,128)S(1)}, u32[]{:S(2)}, u32[]{:S(2)}) async-start(f32[32,8,128]{2,1,0:T(8,128)} %pad_maximum_fusion), calls=%async_computation.3 | async-start | bytes 262144 | tf_op jit(solution)/shard_map/all_to_all | solution.py:687
  106.3 0.1 maximum_bitcast_fusion.2.moved_ref
  106.4 7.5 %all-to-all-done.3 = f32[32,8,128]{2,1,0:T(8,128)S(1)} async-done(((f32[32,8,128]{2,1,0:T(8,128)}), f32[32,8,128]{2,1,0:T(8,128)S(1)}, u32[]{:S(2)}, u32[]{:S(2)}) %all-to-all-start.3) | async-done | bytes 131104 | tf_op jit(solution)/shard_map/all_to_all | solution.py:687
  113.9 0.7 finish.1
  (14 shorter events, 0.2 us)
Async XLA Ops:
  1.7 30.8 %collective-permute-start.1 = (bf16[12,6,512]{2,1,0:T(8,128)(2,1)S(1)}, bf16[12,6,512]{2,1,0:T(8,128)(2,1)S(1)}, u32[]{:S(2)}, u32[]{:S(2)}) collective-permute-start(bf16[12,6,512]{2,1,0:T(8,128)(2,1)S(1)} %slice_select_fusion), channel_id=1, source_target_pairs={{0,63},{1,2},{2,1},{3,4},{4,3},{5,6},{6,5},{7,8},{8,7},{9,10},{10,... | collective-permute-start | bytes 221192 | tf_op jit(solution)/shard_map/ppermute | solution.py:578
  20.5 31.7 %all-to-all-start = ((f32[64,8,128]{2,1,0:T(8,128)}), f32[64,8,128]{2,1,0:T(8,128)S(1)}, u32[]{:S(2)}, u32[]{:S(2)}) async-start(f32[64,8,128]{2,1,0:T(8,128)} %bitcast.57), calls=%async_computation | async-start | bytes 524288 | tf_op jit(solution)/shard_map/all_to_all | solution.py:625
  29.1 3.6 %collective-permute-start = (bf16[12,6,512]{2,1,0:T(8,128)(2,1)}, bf16[12,6,512]{2,1,0:T(8,128)(2,1)S(1)}, u32[]{:S(2)}, u32[]{:S(2)}) collective-permute-start(bf16[12,6,512]{2,1,0:T(8,128)(2,1)} %get-tuple-element.27), channel_id=1, source_target_pairs={{0,1},{1,0},{2,3},{3,2},{4,5},{5,4},{6,7},{7,6},{8,9},{9,8},{10,11... | collective-permute-start | bytes 221192 | tf_op jit(solution)/shard_map/ppermute | solution.py:578
  32.8 17.3 %collective-permute-start.2 = (bf16[4,3,6,512]{3,2,1,0:T(8,128)(2,1)S(1)}, bf16[4,3,6,512]{3,2,1,0:T(8,128)(2,1)S(1)}, u32[]{:S(2)}, u32[]{:S(2)}) collective-permute-start(bf16[4,3,6,512]{3,2,1,0:T(8,128)(2,1)S(1)} %broadcast_select_fusion), channel_id=1, source_target_pairs={{0,448},{64,128},{128,64},{192,256},{256,192},{320,384},{384,320},... | collective-permute-start | bytes 221192 | tf_op jit(solution)/shard_map/ppermute | solution.py:578
  41.7 10.6 %collective-permute-start.3 = (bf16[4,3,6,512]{3,2,1,0:T(8,128)(2,1)S(1)}, bf16[4,3,6,512]{3,2,1,0:T(8,128)(2,1)S(1)}, u32[]{:S(2)}, u32[]{:S(2)}) collective-permute-start(bf16[4,3,6,512]{3,2,1,0:T(8,128)(2,1)S(1)} %get-tuple-element.31), channel_id=1, source_target_pairs={{0,64},{64,0},{128,192},{192,128},{256,320},{320,256},{384,448},{4... | collective-permute-start | bytes 221192 | tf_op jit(solution)/shard_map/ppermute | solution.py:578
  43.6 2.9 %copy-start.5 = (bf16[512]{0:T(512)(128)(2,1)S(1)}, bf16[512]{0:T(512)(128)(2,1)}, u32[]{:S(2)}) copy-start(bf16[512]{0:T(512)(128)(2,1)} %param.17) | copy-start | bytes 3076
  43.6 8.6 %copy-start = (bf16[12,12,512]{2,1,0:T(8,128)(2,1)S(1)}, bf16[12,12,512]{2,1,0:T(8,128)(2,1)}, u32[]{:S(2)}) copy-start(bf16[12,12,512]{2,1,0:T(8,128)(2,1)} %own_ref.1) | copy-start | bytes 442372
  43.6 8.6 %copy-start.1 = (bf16[512,1536]{1,0:T(8,128)(2,1)S(1)}, bf16[512,1536]{1,0:T(8,128)(2,1)}, u32[]{:S(2)}) copy-start(bf16[512,1536]{1,0:T(8,128)(2,1)} %qkv_ref.1) | copy-start | bytes 4718596
  43.6 8.6 %copy-start.2 = (bf16[512,512]{1,0:T(8,128)(2,1)S(1)}, bf16[512,512]{1,0:T(8,128)(2,1)}, u32[]{:S(2)}) copy-start(bf16[512,512]{1,0:T(8,128)(2,1)} %wo_ref.1) | copy-start | bytes 1572868
  43.6 8.6 %copy-start.3 = (bf16[2,8,512]{2,1,0:T(8,128)(2,1)S(1)}, bf16[2,8,512]{2,1,0:T(8,128)(2,1)}, u32[]{:S(2)}) copy-start(bf16[2,8,512]{2,1,0:T(8,128)(2,1)} %param.14) | copy-start | bytes 49156
  43.7 8.6 %copy-start.4 = (bf16[2,8,512]{2,1,0:T(8,128)(2,1)S(1)}, bf16[2,8,512]{2,1,0:T(8,128)(2,1)}, u32[]{:S(2)}) copy-start(bf16[2,8,512]{2,1,0:T(8,128)(2,1)} %param.15) | copy-start | bytes 49156
  61.7 15.7 %all-to-all-start.1 = ((f32[32,4,128]{2,1,0:T(4,128)}), f32[32,4,128]{2,1,0:T(4,128)S(1)}, u32[]{:S(2)}, u32[]{:S(2)}) async-start(f32[32,4,128]{2,1,0:T(4,128)} %bitcast.17), calls=%async_computation.1 | async-start | bytes 131072 | tf_op jit(solution)/shard_map/all_to_all | solution.py:652
  69.3 28.3 %collective-permute-start.4 = (f32[32,128]{1,0:T(8,128)S(1)}, f32[32,128]{1,0:T(8,128)S(1)}, u32[]{:S(2)}, u32[]{:S(2)}) collective-permute-start(f32[32,128]{1,0:T(8,128)S(1)} %get-tuple-element.42), channel_id=1, source_target_pairs={{0,2},{1,3},{2,0},{3,1},{4,6},{5,7},{6,4},{7,5},{8,10},{9,11},{10,... | collective-permute-start | bytes 49160 | tf_op jit(solution)/shard_map/ppermute | solution.py:655
  78.1 19.1 %all-to-all-start.2 = ((f32[16,5,128]{2,1,0:T(8,128)}), f32[16,5,128]{2,1,0:T(8,128)S(1)}, u32[]{:S(2)}, u32[]{:S(2)}) async-start(f32[16,5,128]{2,1,0:T(8,128)} %broadcast_in_dim.24), calls=%async_computation.2 | async-start | bytes 131072 | tf_op jit(solution)/shard_map/all_to_all | solution.py:659
  98.4 15.6 %all-to-all-start.3 = ((f32[32,8,128]{2,1,0:T(8,128)}), f32[32,8,128]{2,1,0:T(8,128)S(1)}, u32[]{:S(2)}, u32[]{:S(2)}) async-start(f32[32,8,128]{2,1,0:T(8,128)} %pad_maximum_fusion), calls=%async_computation.3 | async-start | bytes 262144 | tf_op jit(solution)/shard_map/all_to_all | solution.py:687

commit v11 on v10

--- a/solution.py
+++ b/solution.py
@@ -77,11 +77,14 @@
     )(bias.reshape(HEADS * 72, 72))
 
 
-def slots_kernel(index_ref, weight_ref, value_ref, count_ref, tokens_ref, out_ref, near_ref):
+def slots_kernel(index_ref, weight_ref, value_ref, count_ref, tokens_ref, out_ref, near_ref, edge_ref):
     even = lax.axis_index("lon") % 2 == 0
     for row in range(tokens_ref.shape[0]):
         x = tokens_ref[row].astype(F32)
         near_ref[row] = jnp.where(even, x[6:], x[:6]).astype(BF16)
+        if row < 3 or row >= 9:
+            for half in range(2):
+                edge_ref[row // 9, half, row % 3] = x[6 * half : 6 * half + 6].astype(BF16)
     strips = value_ref.shape[0]
     square = (strips, strips)
     own_lane = lax.broadcasted_iota(jnp.int32, square, 0) == lax.broadcasted_iota(jnp.int32, square, 1)
@@ -111,6 +114,7 @@
         out_shape=[
             jax.ShapeDtypeStruct((value.shape[0] * 8, 128), F32),
             jax.ShapeDtypeStruct((12, 6, MODEL), BF16),
+            jax.ShapeDtypeStruct((2, 2, 3, 6, MODEL), BF16),
         ],
         cost_estimate=pl.CostEstimate(flops=10**6, bytes_accessed=5 * 10**5, transcendentals=0),
         name="packed_slots",
@@ -601,7 +605,7 @@
     )
     far_lon = paired(far_send, "lon", True)
 
-    slots, near_send = packed_slots(
+    slots, near_send, edges = packed_slots(
         observation_index.reshape(lon_count * 4, 128),
         observation_weight.reshape(lon_count * 4, 128),
         observation_value.reshape(lon_count, 128),
@@ -613,9 +617,8 @@
 
     left = jnp.where(even_lon, far_lon, near_lon)
     right = jnp.where(even_lon, near_lon, far_lon)
-    strips = (left, own[0], own[1], right)
-    top = jnp.stack([strip[:3] for strip in strips])
-    bottom = jnp.stack([strip[9:] for strip in strips])
+    top = jnp.concatenate([left[None, :3], edges[0], right[None, :3]])
+    bottom = jnp.concatenate([left[None, 9:], edges[1], right[None, 9:]])
     near_send, top, bottom, bias, readout = lax.optimization_barrier(
         (jnp.where(even_lat, bottom, top), top, bottom, relative_position_bias, readout)
     )

time: 115 us -> 115 us (level)
  no operation moved by 1% of the time
where the time goes in v11:
time: 115 us
  starting transfers between devices  69.7 us (61%)
  waiting for transfers between devices  25.1 us (22%)
  Pallas kernels  15 us (13%)
  other arithmetic  2.16 us (2%)
  local copies, waits for them, and re-layouts  1.77 us (2%)
    ppermute x4, starting transfers between devices, paired(): return lax.ppermute(value, axis, pairs)  30.1 us
    all_to_all x1, waiting for transfers between devices, shards(): lax.all_to_all(jnp.broadcast_to(chunk[None], (2 * lat_count, 5, 128)), ('...  11.5 us
    pallas_call x1, Pallas kernels, core(): pl.pallas_call(functools.partial(core_kernel, loss_scale=loss_scale, lat_...  9.45 us
    all_to_all x1, starting transfers between devices, shards(): lax.all_to_all(slots, 'lon', 0, 0, tiled=True).reshape(lon_count * 8, 128)  8.52 us
    ppermute x1, starting transfers between devices, shards(): other = lax.ppermute(other, 'lon', [(i, i ^ 2) for i in range(lon_count)])  8.09 us
    all_to_all x1, starting transfers between devices, shards(): lax.all_to_all(final, 'lon', 0, 0, axis_index_groups=planes, tiled=True)  7.91 us
    all_to_all x1, starting transfers between devices, shards(): lax.all_to_all(jnp.broadcast_to(chunk[None], (2 * lat_count, 5, 128)), ('...  7.55 us
    all_to_all x1, waiting for transfers between devices, shards(): lax.all_to_all(final, 'lon', 0, 0, axis_index_groups=planes, tiled=True)  7.54 us
  transfers between devices with their start and end apart: 9, of which 5 were waited for; matrix products, arithmetic and copies ran while one was open for 2% of the time, Pallas kernels for 4%

profile of v11, /device:TPU:1, one launch (start us, length us, event | category | flops | bytes accessed | tf_op | source)
XLA Modules:
  0.0 114.6 jit_solution(1864535837932438170)
XLA Ops:
  0.6 1.0 slice_select_fusion
  1.7 16.8 %collective-permute-start.1 = (bf16[12,6,512]{2,1,0:T(8,128)(2,1)S(1)}, bf16[12,6,512]{2,1,0:T(8,128)(2,1)S(1)}, u32[]{:S(2)}, u32[]{:S(2)}) collective-permute-start(bf16[12,6,512]{2,1,0:T(8,128)(2,1)S(1)} %slice_select_fusion), channel_id=1, source_target_pairs={{0,63},{1,2},{2,1},{3,4},{4,3},{5,6},{6,5},{7,8},{8,7},{9,10},{10,... | collective-permute-start | bytes 221192 | tf_op jit(solution)/shard_map/ppermute | solution.py:582
  18.5 2.0 %packed_slots.1 = (f32[512,128]{1,0:T(8,128)}, bf16[12,6,512]{2,1,0:T(8,128)(2,1)}, bf16[2,2,3,6,512]{4,3,2,1,0:T(8,128)(2,1)}) custom-call(s32[256,128]{1,0:T(8,128)} %bitcast.54, f32[256,128]{1,0:T(8,128)} %bitcast.55, f32[64,128]{1,0:T(8,128)} %bitcast.56, s32[1,64]{1,0:T(1,128)} %bitcast.58, bf16[12,12,512]{2,1,0:T(8,128)(2,1)} %own_ref.1), custom_call_target="tpu_custom_call" | custom-call | flops 1000000 | bytes 500000 | tf_op jit(solution)/shard_map/packed_slots/pallas_call | solution.py:112
  20.5 8.5 %all-to-all-start = ((f32[64,8,128]{2,1,0:T(8,128)}), f32[64,8,128]{2,1,0:T(8,128)S(1)}, u32[]{:S(2)}, u32[]{:S(2)}) async-start(f32[64,8,128]{2,1,0:T(8,128)} %bitcast.53), calls=%async_computation | async-start | bytes 524288 | tf_op jit(solution)/shard_map/all_to_all | solution.py:628
  29.1 2.5 %collective-permute-start = (bf16[12,6,512]{2,1,0:T(8,128)(2,1)}, bf16[12,6,512]{2,1,0:T(8,128)(2,1)S(1)}, u32[]{:S(2)}, u32[]{:S(2)}) collective-permute-start(bf16[12,6,512]{2,1,0:T(8,128)(2,1)} %get-tuple-element.28), channel_id=1, source_target_pairs={{0,1},{1,0},{2,3},{3,2},{4,5},{5,4},{6,7},{7,6},{8,9},{9,8},{10,11... | collective-permute-start | bytes 221192 | tf_op jit(solution)/shard_map/ppermute | solution.py:582
  31.5 0.8 slice_bitcast_fusion.1
  32.4 0.0 collective-permute-done.1.far_lon_ref
  32.4 0.3 collective-permute-done.near_lon_ref
  32.7 0.1 pad_maximum_fusion.1
  32.8 8.8 %collective-permute-start.2 = (bf16[4,3,6,512]{3,2,1,0:T(8,128)(2,1)S(1)}, bf16[4,3,6,512]{3,2,1,0:T(8,128)(2,1)S(1)}, u32[]{:S(2)}, u32[]{:S(2)}) collective-permute-start(bf16[4,3,6,512]{3,2,1,0:T(8,128)(2,1)S(1)} %broadcast_select_fusion), channel_id=1, source_target_pairs={{0,448},{64,128},{128,64},{192,256},{256,192},{320,384},{384,320},... | collective-permute-start | bytes 221192 | tf_op jit(solution)/shard_map/ppermute | solution.py:582
  41.7 1.9 %collective-permute-start.3 = (bf16[4,3,6,512]{3,2,1,0:T(8,128)(2,1)S(1)}, bf16[4,3,6,512]{3,2,1,0:T(8,128)(2,1)S(1)}, u32[]{:S(2)}, u32[]{:S(2)}) collective-permute-start(bf16[4,3,6,512]{3,2,1,0:T(8,128)(2,1)S(1)} %get-tuple-element.33), channel_id=1, source_target_pairs={{0,64},{64,0},{128,192},{192,128},{256,320},{320,256},{384,448},{4... | collective-permute-start | bytes 221192 | tf_op jit(solution)/shard_map/ppermute | solution.py:582
  43.6 0.0 copy-start.5
  43.6 0.0 copy-start
  43.6 0.0 copy-start.1
  43.6 0.0 copy-start.2
  43.6 0.0 copy-start.3
  43.6 0.0 copy-start.4
  43.7 2.8 %ordered_bias.1.bias_hbm = f32[64,16,24,96]{3,2,1,0:T(8,128)} custom-call(f32[1152,72]{1,0:T(8,128)} %bitcast.59), custom_call_target="tpu_custom_call" | custom-call | flops 20000000000 | bytes 2000000 | tf_op jit(solution)/shard_map/ordered_bias/pallas_call | solution.py:65
  46.5 0.0 copy-done.5
  46.5 3.6 %collective-permute-done.2.far_lat_ref = bf16[4,3,6,512]{3,2,1,0:T(8,128)(2,1)S(1)} collective-permute-done((bf16[4,3,6,512]{3,2,1,0:T(8,128)(2,1)S(1)}, bf16[4,3,6,512]{3,2,1,0:T(8,128)(2,1)S(1)}, u32[]{:S(2)}, u32[]{:S(2)}) %collective-permute-start.2) | collective-permute-done | bytes 73760 | tf_op jit(solution)/shard_map/ppermute | solution.py:582
  50.1 2.1 %collective-permute-done.3.near_lat_ref = bf16[4,3,6,512]{3,2,1,0:T(8,128)(2,1)S(1)} collective-permute-done((bf16[4,3,6,512]{3,2,1,0:T(8,128)(2,1)S(1)}, bf16[4,3,6,512]{3,2,1,0:T(8,128)(2,1)S(1)}, u32[]{:S(2)}, u32[]{:S(2)}) %collective-permute-start.3) | collective-permute-done | bytes 73760 | tf_op jit(solution)/shard_map/ppermute | solution.py:582
  52.2 0.0 all-to-all-done
  52.2 0.0 copy-done
  52.2 0.0 copy-done.1
  52.2 0.0 copy-done.2
  52.2 0.0 copy-done.3
  52.3 0.0 copy-done.4
  52.3 9.4 %window_and_observe.1 = (bf16[12,12,512]{2,1,0:T(8,128)(2,1)}, f32[1,256]{1,0:T(1,128)S(1)}, f32[1,128]{1,0:T(1,128)S(1)}, f32[128,128]{1,0:T(8,128)}, f32[32,128]{1,0:T(8,128)S(1)}, /*index=5*/f32[32,128]{1,0:T(8,128)S(1)}) custom-call(bf16[12,12,512]{2,1,0:T(8,128)(2,1)S(1)} %copy-done, bf16[12,6,512]{2,1,0:T(8,128)(2,1)S(1)} %collective-permute-done.near_lon_ref, ...), custom_call_target="tpu_custom_call" | custom-call | flops 3000000000 | bytes 8000000 | tf_op jit(solution)/shard_map/window_and_observe/pallas_call | solution.py:495
  61.7 7.5 %all-to-all-start.1 = ((f32[32,4,128]{2,1,0:T(4,128)}), f32[32,4,128]{2,1,0:T(4,128)S(1)}, u32[]{:S(2)}, u32[]{:S(2)}) async-start(f32[32,4,128]{2,1,0:T(4,128)} %bitcast.15), calls=%async_computation.1 | async-start | bytes 131072 | tf_op jit(solution)/shard_map/all_to_all | solution.py:655
  69.3 8.1 %collective-permute-start.4 = (f32[32,128]{1,0:T(8,128)S(1)}, f32[32,128]{1,0:T(8,128)S(1)}, u32[]{:S(2)}, u32[]{:S(2)}) collective-permute-start(f32[32,128]{1,0:T(8,128)S(1)} %get-tuple-element.44), channel_id=1, source_target_pairs={{0,2},{1,3},{2,0},{3,1},{4,6},{5,7},{6,4},{7,5},{8,10},{9,11},{10,... | collective-permute-start | bytes 49160 | tf_op jit(solution)/shard_map/ppermute | solution.py:658
  77.4 0.0 all-to-all-done.1
  77.5 0.6 broadcast_in_dim.40
  78.1 7.5 %all-to-all-start.2 = ((f32[16,5,128]{2,1,0:T(8,128)}), f32[16,5,128]{2,1,0:T(8,128)S(1)}, u32[]{:S(2)}, u32[]{:S(2)}) async-start(f32[16,5,128]{2,1,0:T(8,128)} %broadcast_in_dim.40), calls=%async_computation.2 | async-start | bytes 131072 | tf_op jit(solution)/shard_map/all_to_all | solution.py:662
  85.7 0.1 slice_bitcast_fusion.7
  85.7 11.5 %all-to-all-done.2 = f32[16,5,128]{2,1,0:T(8,128)S(1)} async-done(((f32[16,5,128]{2,1,0:T(8,128)}), f32[16,5,128]{2,1,0:T(8,128)S(1)}, u32[]{:S(2)}, u32[]{:S(2)}) %all-to-all-start.2) | async-done | bytes 40992 | tf_op jit(solution)/shard_map/all_to_all | solution.py:662
  97.3 0.1 slice_bitcast_fusion.9
  97.4 0.1 slice_bitcast_fusion.6
  97.4 0.1 maximum_bitcast_fusion.1
  97.5 0.1 maximum_bitcast_fusion
  97.6 0.0 collective-permute-done.4
  97.7 0.7 pad_maximum_fusion
  98.4 7.9 %all-to-all-start.3 = ((f32[32,8,128]{2,1,0:T(8,128)}), f32[32,8,128]{2,1,0:T(8,128)S(1)}, u32[]{:S(2)}, u32[]{:S(2)}) async-start(f32[32,8,128]{2,1,0:T(8,128)} %pad_maximum_fusion), calls=%async_computation.3 | async-start | bytes 262144 | tf_op jit(solution)/shard_map/all_to_all | solution.py:690
  106.3 0.1 maximum_bitcast_fusion.2.moved_ref
  106.4 7.5 %all-to-all-done.3 = f32[32,8,128]{2,1,0:T(8,128)S(1)} async-done(((f32[32,8,128]{2,1,0:T(8,128)}), f32[32,8,128]{2,1,0:T(8,128)S(1)}, u32[]{:S(2)}, u32[]{:S(2)}) %all-to-all-start.3) | async-done | bytes 131104 | tf_op jit(solution)/shard_map/all_to_all | solution.py:690
  113.9 0.7 finish.1
  (14 shorter events, 0.2 us)
Async XLA Ops:
  1.7 30.7 %collective-permute-start.1 = (bf16[12,6,512]{2,1,0:T(8,128)(2,1)S(1)}, bf16[12,6,512]{2,1,0:T(8,128)(2,1)S(1)}, u32[]{:S(2)}, u32[]{:S(2)}) collective-permute-start(bf16[12,6,512]{2,1,0:T(8,128)(2,1)S(1)} %slice_select_fusion), channel_id=1, source_target_pairs={{0,63},{1,2},{2,1},{3,4},{4,3},{5,6},{6,5},{7,8},{8,7},{9,10},{10,... | collective-permute-start | bytes 221192 | tf_op jit(solution)/shard_map/ppermute | solution.py:582
  20.5 31.7 %all-to-all-start = ((f32[64,8,128]{2,1,0:T(8,128)}), f32[64,8,128]{2,1,0:T(8,128)S(1)}, u32[]{:S(2)}, u32[]{:S(2)}) async-start(f32[64,8,128]{2,1,0:T(8,128)} %bitcast.53), calls=%async_computation | async-start | bytes 524288 | tf_op jit(solution)/shard_map/all_to_all | solution.py:628
  29.1 3.6 %collective-permute-start = (bf16[12,6,512]{2,1,0:T(8,128)(2,1)}, bf16[12,6,512]{2,1,0:T(8,128)(2,1)S(1)}, u32[]{:S(2)}, u32[]{:S(2)}) collective-permute-start(bf16[12,6,512]{2,1,0:T(8,128)(2,1)} %get-tuple-element.28), channel_id=1, source_target_pairs={{0,1},{1,0},{2,3},{3,2},{4,5},{5,4},{6,7},{7,6},{8,9},{9,8},{10,11... | collective-permute-start | bytes 221192 | tf_op jit(solution)/shard_map/ppermute | solution.py:582
  32.8 17.3 %collective-permute-start.2 = (bf16[4,3,6,512]{3,2,1,0:T(8,128)(2,1)S(1)}, bf16[4,3,6,512]{3,2,1,0:T(8,128)(2,1)S(1)}, u32[]{:S(2)}, u32[]{:S(2)}) collective-permute-start(bf16[4,3,6,512]{3,2,1,0:T(8,128)(2,1)S(1)} %broadcast_select_fusion), channel_id=1, source_target_pairs={{0,448},{64,128},{128,64},{192,256},{256,192},{320,384},{384,320},... | collective-permute-start | bytes 221192 | tf_op jit(solution)/shard_map/ppermute | solution.py:582
  41.7 10.6 %collective-permute-start.3 = (bf16[4,3,6,512]{3,2,1,0:T(8,128)(2,1)S(1)}, bf16[4,3,6,512]{3,2,1,0:T(8,128)(2,1)S(1)}, u32[]{:S(2)}, u32[]{:S(2)}) collective-permute-start(bf16[4,3,6,512]{3,2,1,0:T(8,128)(2,1)S(1)} %get-tuple-element.33), channel_id=1, source_target_pairs={{0,64},{64,0},{128,192},{192,128},{256,320},{320,256},{384,448},{4... | collective-permute-start | bytes 221192 | tf_op jit(solution)/shard_map/ppermute | solution.py:582
  43.6 2.9 %copy-start.5 = (bf16[512]{0:T(512)(128)(2,1)S(1)}, bf16[512]{0:T(512)(128)(2,1)}, u32[]{:S(2)}) copy-start(bf16[512]{0:T(512)(128)(2,1)} %param.17) | copy-start | bytes 3076
  43.6 8.6 %copy-start = (bf16[12,12,512]{2,1,0:T(8,128)(2,1)S(1)}, bf16[12,12,512]{2,1,0:T(8,128)(2,1)}, u32[]{:S(2)}) copy-start(bf16[12,12,512]{2,1,0:T(8,128)(2,1)} %own_ref.1) | copy-start | bytes 442372
  43.6 8.6 %copy-start.1 = (bf16[512,1536]{1,0:T(8,128)(2,1)S(1)}, bf16[512,1536]{1,0:T(8,128)(2,1)}, u32[]{:S(2)}) copy-start(bf16[512,1536]{1,0:T(8,128)(2,1)} %qkv_ref.1) | copy-start | bytes 4718596
  43.6 8.6 %copy-start.2 = (bf16[512,512]{1,0:T(8,128)(2,1)S(1)}, bf16[512,512]{1,0:T(8,128)(2,1)}, u32[]{:S(2)}) copy-start(bf16[512,512]{1,0:T(8,128)(2,1)} %wo_ref.1) | copy-start | bytes 1572868
  43.6 8.6 %copy-start.3 = (bf16[2,8,512]{2,1,0:T(8,128)(2,1)S(1)}, bf16[2,8,512]{2,1,0:T(8,128)(2,1)}, u32[]{:S(2)}) copy-start(bf16[2,8,512]{2,1,0:T(8,128)(2,1)} %param.14) | copy-start | bytes 49156
  43.6 8.6 %copy-start.4 = (bf16[2,8,512]{2,1,0:T(8,128)(2,1)S(1)}, bf16[2,8,512]{2,1,0:T(8,128)(2,1)}, u32[]{:S(2)}) copy-start(bf16[2,8,512]{2,1,0:T(8,128)(2,1)} %param.15) | copy-start | bytes 49156
  61.7 15.7 %all-to-all-start.1 = ((f32[32,4,128]{2,1,0:T(4,128)}), f32[32,4,128]{2,1,0:T(4,128)S(1)}, u32[]{:S(2)}, u32[]{:S(2)}) async-start(f32[32,4,128]{2,1,0:T(4,128)} %bitcast.15), calls=%async_computation.1 | async-start | bytes 131072 | tf_op jit(solution)/shard_map/all_to_all | solution.py:655
  69.3 28.3 %collective-permute-start.4 = (f32[32,128]{1,0:T(8,128)S(1)}, f32[32,128]{1,0:T(8,128)S(1)}, u32[]{:S(2)}, u32[]{:S(2)}) collective-permute-start(f32[32,128]{1,0:T(8,128)S(1)} %get-tuple-element.44), channel_id=1, source_target_pairs={{0,2},{1,3},{2,0},{3,1},{4,6},{5,7},{6,4},{7,5},{8,10},{9,11},{10,... | collective-permute-start | bytes 49160 | tf_op jit(solution)/shard_map/ppermute | solution.py:658
  78.1 19.1 %all-to-all-start.2 = ((f32[16,5,128]{2,1,0:T(8,128)}), f32[16,5,128]{2,1,0:T(8,128)S(1)}, u32[]{:S(2)}, u32[]{:S(2)}) async-start(f32[16,5,128]{2,1,0:T(8,128)} %broadcast_in_dim.40), calls=%async_computation.2 | async-start | bytes 131072 | tf_op jit(solution)/shard_map/all_to_all | solution.py:662
  98.4 15.5 %all-to-all-start.3 = ((f32[32,8,128]{2,1,0:T(8,128)}), f32[32,8,128]{2,1,0:T(8,128)S(1)}, u32[]{:S(2)}, u32[]{:S(2)}) async-start(f32[32,8,128]{2,1,0:T(8,128)} %pad_maximum_fusion), calls=%async_computation.3 | async-start | bytes 262144 | tf_op jit(solution)/shard_map/all_to_all | solution.py:690
